TPU v7x, 32 devices: a whole 2x2x4 slice. The times are simulated.
32 devices in a mesh: seq: 2 (over y), tp: 4 (over z), dp: 4 (over x, core).
Axes of the slice: x: 2, y: 2, z: 4, core: 2. Of those that a mesh axis runs over, the one named last changes fastest.
Arguments:
- query_rows: bfloat16 [4, 256, 2048], P('dp', 'seq', 'tp'), may hold values from -8 to 8
- key_rows: bfloat16 [4, 256, 256], P('dp', 'seq', 'tp'), may hold values from -6 to 6
- value_rows: bfloat16 [4, 256, 256], P('dp', 'seq', 'tp'), may hold values from -6 to 6
- gate_rows: bfloat16 [4, 256, 2048], P('dp', 'seq', 'tp'), may hold values from -6 to 6
- write_vec: bfloat16 [4, 256, 128], P('dp', 'seq'), may hold values from -0.5 to 0.5
- read_vec: bfloat16 [4, 256, 128], P('dp', 'seq'), may hold values from -0.5 to 0.5
- dt_raw: float32 [4, 32, 256], P('dp', 'tp', 'seq'), may hold values from -4 to 4
- a_log: float32 [32], P('tp')
- skip_gain: float32 [32], P('tp'), may hold values from 0.5 to 1.5
- dt_bias: float32 [32], P('tp'), may hold values from -1 to 1
- out_grad: bfloat16 [4, 256, 2048], P('dp', 'seq', 'tp'), may hold values from -6 to 6
Outputs:
- grad_query: float32 [4, 256, 2048], P('dp', 'seq', 'tp')
- grad_key: float32 [4, 256, 256], P('dp', 'seq', 'tp')
- grad_value: float32 [4, 256, 256], P('dp', 'seq', 'tp')
- grad_gate: float32 [4, 256, 2048], P('dp', 'seq', 'tp')
- grad_write: float32 [4, 256, 128], P('dp', 'seq')
- grad_read: float32 [4, 256, 128], P('dp', 'seq')
- grad_dt: float32 [4, 32, 256], P('dp', 'tp', 'seq')
- grad_alog: float32 [32], P('tp')
- grad_skip: float32 [32], P('tp')
- grad_bias: float32 [32], P('tp')
All inputs are finite; a program needn't handle non-finite values.
Results may differ from a plain program's by a relative error of at most 0.024.
Values may be sent and summed in bfloat16 or wider, within the bound.
No kernel may reach another device: no remote copies, remote signals or barrier semaphores. Data moves between devices by JAX's collectives and lax.ppermute only.
A program may use at most 64 MiB of HBM per device.

v0:
```python
import math

import jax
import jax.numpy as jnp
from jax import lax
from jax.sharding import PartitionSpec as P

NEG_FILL = -1e30
HIGH = lax.Precision.HIGHEST


def from_partner(array, axis, distance):
    return lax.ppermute(array, axis, [(i, i ^ 1 << distance) for i in range(lax.axis_size(axis))])


def carried_in(array, axis, join, neutral):
    place = lax.axis_index(axis)
    gathered = jax.tree.map(
        lambda a, kind: lax.all_gather(a.astype(kind), axis), array, (jnp.bfloat16, jnp.bfloat16)
    )
    state = jax.tree.map(lambda a, e: jnp.zeros_like(a) + jnp.asarray(e, a.dtype), array, neutral)

    def one(turn, state):
        return join(
            state,
            jax.tree.map(
                lambda a, own: lax.dynamic_index_in_dim(a, turn, 0, False).astype(own.dtype),
                gathered,
                array,
            ),
        )

    return lax.fori_loop(0, place, one, state)


def prefix(array, axis, combine, identity):
    devices, here = (lax.axis_size(axis), lax.axis_index(axis))
    everything = jax.tree.map(lambda part: lax.all_gather(part, axis), array)
    start = jax.tree.map(
        lambda part, zero: jnp.broadcast_to(jnp.asarray(zero, part.dtype), part.shape),
        array,
        identity,
    )

    def turn(k, before):
        at = devices - 1 - k
        reached = at > here
        new = combine(before, jax.tree.map(lambda part: part[at], everything))
        return jax.tree.map(lambda a, b: jnp.where(reached, a, b), new, before)

    return lax.fori_loop(0, devices, turn, start)


def block_scan(inner, gate_in, write_in, read_in, dt_raw, a_log, skip_gain, dt_bias):
    num_rows, num_heads, head_width = inner.shape
    num_states = write_in.shape[1]
    block_len = math.gcd(num_rows, 256)
    block_count = num_rows // block_len
    step_dt = jax.nn.softplus(dt_raw + dt_bias[:, None])
    rate_all = step_dt * jnp.exp(a_log)[:, None]
    rate_blocks = rate_all.reshape(num_heads, block_count, block_len).transpose(1, 0, 2)
    dt_blocks = step_dt.reshape(num_heads, block_count, block_len).transpose(1, 0, 2)
    inner_blocks = inner.reshape(block_count, block_len, num_heads, head_width)
    write_blocks = write_in.reshape(block_count, block_len, num_states)
    read_blocks = read_in.reshape(block_count, block_len, num_states)
    causal = jnp.arange(block_len)[:, None] >= jnp.arange(block_len)[None, :]

    def advance(carried, pieces):
        rate_now, dt_now, inner_now, write_now, read_now = pieces
        cum_rate = jnp.cumsum(rate_now, axis=1)
        intersection = jnp.dot(read_now, write_now.T, precision=HIGH)
        log_gap = cum_rate[:, :, None] - cum_rate[:, None, :]
        weight = (
            jnp.where(causal, jnp.exp(-jnp.maximum(log_gap, 0.0)), 0.0)
            * intersection[None]
            * dt_now[:, None, :]
        )
        output = jnp.einsum("hts,shp->thp", weight, inner_now, precision=HIGH)
        output = (
            output
            + jnp.einsum("tn,hpn->thp", read_now, carried, precision=HIGH)
            * jnp.exp(-cum_rate).T[:, :, None]
        )
        to_end = jnp.exp(-(cum_rate[:, -1:] - cum_rate)) * dt_now
        next_state = jnp.exp(-cum_rate[:, -1])[:, None, None] * carried + jnp.einsum(
            "hs,shp,sn->hpn", to_end, inner_now, write_now, precision=HIGH
        )
        return (next_state, output)

    zero_state = jnp.zeros((num_heads, head_width, num_states), jnp.float32)
    end_state, outputs = lax.scan(
        advance, zero_state, (rate_blocks, dt_blocks, inner_blocks, write_blocks, read_blocks)
    )
    mixed_out = outputs.reshape(num_rows, num_heads, head_width) + skip_gain[None, :, None] * inner
    gated_out = mixed_out.reshape(num_rows, num_heads * head_width) * jax.nn.silu(gate_in)
    return (gated_out, end_state, jnp.exp(-jnp.sum(rate_all, axis=1)))


def entry_term(gate_in, read_in, dt_raw, a_log, dt_bias, entry_state):
    step_dt = jax.nn.softplus(dt_raw + dt_bias[:, None])
    cum_rate = jnp.cumsum(step_dt * jnp.exp(a_log)[:, None], axis=1)
    carried = (
        jnp.einsum("tn,hpn->thp", read_in, entry_state, precision=HIGH)
        * jnp.exp(-cum_rate).T[:, :, None]
    )
    return carried.reshape(read_in.shape[0], -1) * jax.nn.silu(gate_in)


def carry_combine(earlier, later):
    return (earlier[0] * later[0], later[0][:, None, None] * earlier[1] + later[1])


def join_halves(own_part, other_part, parity):
    lower_first = jnp.concatenate([own_part, other_part], axis=1)
    upper_first = jnp.concatenate([other_part, own_part], axis=1)
    return jnp.where(parity == 0, lower_first, upper_first)


def block_scores(query_blk, key_piece, key_start, row_pos, scale):
    scores = (
        jnp.einsum("rhd,kd->hrk", query_blk, key_piece, preferred_element_type=jnp.float32) * scale
    )
    allowed = (key_start + jnp.arange(key_piece.shape[0]))[None, :] <= row_pos[:, None]
    return jnp.where(allowed[None], scores, NEG_FILL)


def attend_forward(query_blk, full_keys, full_values, first_row):
    num_rows, num_heads, head_dim = query_blk.shape
    key_block = math.gcd(full_keys.shape[0], 512)
    scale = head_dim ** (-0.5)
    row_pos = first_row + jnp.arange(num_rows)
    needed = (first_row + num_rows + key_block - 1) // key_block

    def visit(index, carry):
        run_max, run_sum, run_acc = carry
        key_start = index * key_block
        key_piece = lax.dynamic_slice_in_dim(full_keys, key_start, key_block, 0)
        value_piece = lax.dynamic_slice_in_dim(full_values, key_start, key_block, 0)
        scores = block_scores(query_blk, key_piece, key_start, row_pos, scale)
        new_max = jnp.maximum(run_max, jnp.max(scores, axis=2))
        shrink = jnp.exp(run_max - new_max)
        probs = jnp.exp(scores - new_max[:, :, None])
        run_sum = run_sum * shrink + jnp.sum(probs, axis=2)
        update = jnp.einsum(
            "hrk,kd->hrd",
            probs.astype(jnp.bfloat16),
            value_piece,
            preferred_element_type=jnp.float32,
        )
        run_acc = run_acc * shrink[:, :, None] + update
        return (new_max, run_sum, run_acc)

    start_max = jnp.full((num_heads, num_rows), NEG_FILL, jnp.float32)
    start_sum = jnp.zeros((num_heads, num_rows), jnp.float32)
    start_acc = jnp.zeros((num_heads, num_rows, head_dim), jnp.float32)
    run_max, run_sum, run_acc = lax.fori_loop(0, needed, visit, (start_max, start_sum, start_acc))
    return (run_acc / run_sum[:, :, None], run_max + jnp.log(run_sum))


def attend_backward(query_blk, full_keys, full_values, first_row, attn, log_sum, grad_attn):
    num_rows, num_heads, head_dim = query_blk.shape
    seq_len = full_keys.shape[0]
    key_block = math.gcd(seq_len, 512)
    scale = head_dim ** (-0.5)
    row_pos = first_row + jnp.arange(num_rows)
    needed = (first_row + num_rows + key_block - 1) // key_block
    delta = jnp.sum(grad_attn * attn, axis=2)
    grad_low = grad_attn.astype(jnp.bfloat16)

    def visit(index, carry):
        grad_q, key_terms, value_terms = carry
        key_start = index * key_block
        key_piece = lax.dynamic_slice_in_dim(full_keys, key_start, key_block, 0)
        value_piece = lax.dynamic_slice_in_dim(full_values, key_start, key_block, 0)
        scores = block_scores(query_blk, key_piece, key_start, row_pos, scale)
        probs = jnp.exp(scores - log_sum[:, :, None])
        probs_low = probs.astype(jnp.bfloat16)
        value_part = jnp.einsum(
            "hrk,hrd->kd", probs_low, grad_low, preferred_element_type=jnp.float32
        )
        grad_probs = jnp.einsum(
            "hrd,kd->hrk", grad_low, value_piece, preferred_element_type=jnp.float32
        )
        grad_scores = (probs * (grad_probs - delta[:, :, None])).astype(jnp.bfloat16)
        grad_q = grad_q + jnp.einsum(
            "hrk,kd->rhd", grad_scores, key_piece, preferred_element_type=jnp.float32
        )
        key_part = (
            jnp.einsum("hrk,rhd->kd", grad_scores, query_blk, preferred_element_type=jnp.float32)
            * scale
        )
        key_terms = lax.dynamic_update_slice_in_dim(key_terms, key_part, key_start, 0)
        value_terms = lax.dynamic_update_slice_in_dim(value_terms, value_part, key_start, 0)
        return (grad_q, key_terms, value_terms)

    start_q = jnp.zeros((num_rows, num_heads, head_dim), jnp.float32)
    start_terms = jnp.zeros((seq_len, head_dim), jnp.float32)
    grad_q, key_terms, value_terms = lax.fori_loop(
        0, needed, visit, (start_q, start_terms, start_terms)
    )
    return (grad_q * scale, key_terms, value_terms)


def body(
    query_rows,
    key_rows,
    value_rows,
    gate_rows,
    write_vec,
    read_vec,
    dt_raw,
    a_log,
    skip_gain,
    dt_bias,
    out_grad,
):
    num_rows = query_rows.shape[1]
    half_dim = key_rows.shape[2]
    head_dim = 2 * half_dim
    query_blk = query_rows[0].reshape(num_rows, -1, head_dim)
    parity = lax.axis_index("tp") % 2
    first_row = lax.axis_index("seq") * num_rows
    other_keys, other_values = from_partner((key_rows[0], value_rows[0]), "tp", 0)
    local_keys = join_halves(key_rows[0], other_keys, parity)
    local_values = join_halves(value_rows[0], other_values, parity)
    full_keys, full_values = (
        lax.all_gather(local_keys, "seq", axis=0, tiled=True),
        lax.all_gather(local_values, "seq", axis=0, tiled=True),
    )
    attn, log_sum = attend_forward(query_blk, full_keys, full_values, first_row)
    mamba_heads = a_log.shape[0]
    inner_heads = attn.transpose(1, 0, 2).reshape(num_rows, mamba_heads, -1)
    gate_f = gate_rows[0].astype(jnp.float32)
    write_f = write_vec[0].astype(jnp.float32)
    read_f = read_vec[0].astype(jnp.float32)
    raw_dt = dt_raw[0]
    main_outs, main_pullback = jax.vjp(
        block_scan, inner_heads, gate_f, write_f, read_f, raw_dt, a_log, skip_gain, dt_bias
    )
    local_state = main_outs[1]
    local_decay = main_outs[2]
    identity = (jnp.ones_like(local_decay), jnp.zeros_like(local_state))
    entry_state = carried_in((local_decay, local_state), "seq", carry_combine, identity)[1]
    cotangent = out_grad[0].astype(jnp.float32)
    entry_out, entry_pullback = jax.vjp(
        entry_term, gate_f, read_f, raw_dt, a_log, dt_bias, entry_state
    )
    entry_gate, entry_read, entry_dt, entry_alog, entry_bias, entry_grad = entry_pullback(cotangent)
    exit_grad = prefix((local_decay, entry_grad), "seq", carry_combine, identity)[1]
    decay_grad = jnp.sum(exit_grad * entry_state, axis=(1, 2))
    main_grads = main_pullback((cotangent, exit_grad, decay_grad))
    main_inner, main_gate, main_write, main_read, main_dt, main_alog, main_skip, main_bias = (
        main_grads
    )
    grad_write, grad_read = (
        lax.psum(main_write.astype(jnp.bfloat16), "tp").astype(jnp.float32),
        lax.psum((main_read + entry_read).astype(jnp.bfloat16), "tp").astype(jnp.float32),
    )
    grad_alog, grad_skip, grad_bias = lax.psum(
        (main_alog + entry_alog, main_skip, main_bias + entry_bias), ("seq", "dp")
    )
    grad_attn = main_inner.reshape(num_rows, -1, head_dim).transpose(1, 0, 2)
    grad_q, key_terms, value_terms = attend_backward(
        query_blk, full_keys, full_values, first_row, attn, log_sum, grad_attn
    )
    own_start = parity * half_dim
    give_start = (1 - parity) * half_dim
    key_sum, value_sum = (
        lax.psum_scatter(
            key_terms.astype(jnp.bfloat16), "seq", scatter_dimension=0, tiled=True
        ).astype(jnp.float32),
        lax.psum_scatter(
            value_terms.astype(jnp.bfloat16), "seq", scatter_dimension=0, tiled=True
        ).astype(jnp.float32),
    )
    give_key = lax.dynamic_slice_in_dim(key_sum, give_start, half_dim, 1)
    give_value = lax.dynamic_slice_in_dim(value_sum, give_start, half_dim, 1)
    received = (
        from_partner(give_key.astype(jnp.bfloat16), "tp", 0).astype(give_key.dtype),
        from_partner(give_value.astype(jnp.bfloat16), "tp", 0).astype(give_value.dtype),
    )
    grad_key = lax.dynamic_slice_in_dim(key_sum, own_start, half_dim, 1) + received[0]
    grad_value = lax.dynamic_slice_in_dim(value_sum, own_start, half_dim, 1) + received[1]
    grad_query = grad_q.reshape(num_rows, -1)[None]
    grad_gate = (main_gate + entry_gate)[None]
    grad_dt = (main_dt + entry_dt)[None]
    return (
        grad_query,
        grad_key[None],
        grad_value[None],
        grad_gate,
        grad_write[None],
        grad_read[None],
        grad_dt,
        grad_alog,
        grad_skip,
        grad_bias,
    )


def solution(mesh):
    in_specs = (
        P("dp", "seq", "tp"),
        P("dp", "seq", "tp"),
        P("dp", "seq", "tp"),
        P("dp", "seq", "tp"),
        P("dp", "seq", None),
        P("dp", "seq", None),
        P("dp", "tp", "seq"),
        P("tp"),
        P("tp"),
        P("tp"),
        P("dp", "seq", "tp"),
    )
    out_specs = (
        P("dp", "seq", "tp"),
        P("dp", "seq", "tp"),
        P("dp", "seq", "tp"),
        P("dp", "seq", "tp"),
        P("dp", "seq", None),
        P("dp", "seq", None),
        P("dp", "tp", "seq"),
        P("tp"),
        P("tp"),
        P("tp"),
    )
    return jax.shard_map(body, mesh=mesh, in_specs=in_specs, out_specs=out_specs, check_vma=False)
```

profile of v0, /device:TPU:0, one launch (start us, length us, event | category | flops | bytes accessed | tf_op | source)
XLA Modules:
  0.0 134.5 jit_solution(11046249703808162612)
XLA Ops:
  8.1 0.8 copy.90
  8.9 3.1 %collective-permute-start = (bf16[128,64]{1,0:T(8,128)(2,1)S(1)}, bf16[128,64]{1,0:T(8,128)(2,1)S(1)}, u32[]{:S(2)}, u32[]{:S(2)}) collective-permute-start(bf16[128,64]{1,0:T(8,128)(2,1)S(1)} %bitcast.284), channel_id=1, source_target_pairs={{0,4},{4,0},{8,12},{12,8},{1,5},{5,1},{9,13},{13,9},{2,6},{6,2},{1... | collective-permute-start | bytes 49160 | tf_op jit(solution)/shard_map/ppermute | solution.py:13
  13.3 0.8 fusion.118
  15.9 0.8 fusion.89
  19.6 4.9 %all-reduce.3 = bf16[16]{0:T(256)(128)(2,1)S(1)} all-reduce(bf16[16]{0:T(256)(128)(2,1)S(1)} %dynamic-update-slice.1), channel_id=5, replica_groups=mesh['seq'=2,'tp'=4,'dp'=4] {'seq'}, use_global_device_ids=true, to_apply=%add.3 | all-reduce | flops 16 | bytes 64
  28.4 4.9 %all-reduce.2 = f32[16]{0:T(128)S(1)} all-reduce(f32[16]{0:T(128)S(1)} %get-tuple-element.740), channel_id=2, replica_groups=mesh['seq'=2,'tp'=4,'dp'=4] {'seq'}, use_global_device_ids=true, to_apply=%add.2 | all-reduce | flops 16 | bytes 128
  34.8 4.8 %all_gather.26 = bf16[256,128]{1,0:T(8,128)(2,1)S(1)} all-gather(bf16[128,128]{1,0:T(8,128)(2,1)S(1)} %maximum_select_fusion), channel_id=1, replica_groups=mesh['seq'=2,'tp'=4,'dp'=4] {'seq'}, dimensions={0}, use_global_device_ids=true | all-gather | bytes 98304 | tf_op jit(solution)/shard_map/all_gather | solution.py:227
  39.7 4.6 %all_gather.27 = bf16[256,128]{1,0:T(8,128)(2,1)S(1)} all-gather(bf16[128,128]{1,0:T(8,128)(2,1)S(1)} %maximum_select_fusion.1), channel_id=1, replica_groups=mesh['seq'=2,'tp'=4,'dp'=4] {'seq'}, dimensions={0}, use_global_device_ids=true | all-gather | bytes 98304 | tf_op jit(solution)/shard_map/all_gather | solution.py:228
  44.3 0.9 while.17
  46.3 5.6 %all-gather.2 = bf16[16,64,128]{2,1,0:T(8,128)(2,1)S(1)} all-gather(bf16[8,64,128]{2,1,0:T(8,128)(2,1)S(1)} %fusion.27), channel_id=4, replica_groups=mesh['seq'=2,'tp'=4,'dp'=4] {'seq'}, dimensions={0}, use_global_device_ids=true | all-gather | bytes 393216 | tf_op jit(solution)/shard_map/all_gather | solution.py:19
  52.0 0.9 multiply_reduce_fusion.1
  52.9 1.2 fusion.25
  54.1 2.0 %fusion.115 = (f32[8,128]{1,0:T(8,128)}, f32[8,128]{1,0:T(8,128)}, f32[8,128]{1,0:T(8,128)}, f32[128,128]{1,0:T(8,128)S(1)}) fusion(f32[8,128]{1,0:T(8,128)S(1)} %reduce_window_sum.33, f32[128,128]{1,0:T(8,128)S(1)} %copy-done.12, f32[8,128]{1,0:T(8,128)S(1)} %copy-done.31, pred[128,128]{1,0:T(8,128)(4,1)S(1)} %copy-done.23, ...), kind=kOutput, calls=%fused_computation.197 | convolution fusion | flops 103396352 | bytes 692224 | tf_op jit(solution)/shard_map/transpose(jvp())/while/body/eval_jaxpr/hts,shp->thp/dot_general | solution.py:78
  56.2 1.2 convolution_bitcast_fusion.7
  57.4 1.2 convolution_bitcast_fusion.8
  59.1 7.0 %all-gather.1 = f32[16,64,128]{2,1,0:T(8,128)S(1)} all-gather(f32[8,64,128]{2,1,0:T(8,128)S(1)} %fusion.94), channel_id=3, replica_groups=mesh['seq'=2,'tp'=4,'dp'=4] {'seq'}, dimensions={0}, use_global_device_ids=true | all-gather | bytes 786432 | tf_op jit(solution)/shard_map/all_gather | solution.py:38
  74.2 2.6 %while.18 = (s32[]{:T(128)}, f32[128,4,128]{2,0,1:T(8,128)S(1)}, bf16[256,128]{1,0:T(8,128)(2,1)}, bf16[256,128]{1,0:T(8,128)(2,1)}, s32[]{:T(128)}, /*index=5*/...) while((s32[]{:T(128)}, f32[128,4,128]{2,0,1:T(8,128)S(1)}, ...), condition=%wide.region_10.12_spmd.clone, body=%wide.region_9.11_spmd.clone.sunk | while | flops 168853888 | bytes 3808409 | solution.py:198
  75.1 0.8 fusion.174
  75.9 0.8 convolution_bitcast_fusion.11
  77.6 1.2 reduce_window_sum.34
  78.8 1.2 reduce_window_sum.35
  80.1 0.9 fusion.32
  80.9 0.8 fusion.31
  86.2 12.3 %all-reduce.4 = (f32[8]{0:T(128)}, f32[8]{0:T(128)}, f32[8]{0:T(128)}) all-reduce(f32[8]{0:T(128)S(1)} %add_multiply_fusion.1, f32[8]{0:T(128)S(1)} %reduce_sum.239, f32[8]{0:T(128)S(1)} %add.243), channel_id=1, replica_groups=mesh['seq'=2,'tp'=4,'dp'=4] {'seq','dp'}, use_global_device_ids=true, to_apply=%region_30.32 | all-reduce | flops 24 | bytes 192 | tf_op jit(solution)/shard_map/psum | solution.py:259
  98.7 0.8 broadcast_in_dim_reshape.3
  99.5 0.8 copy.108
  100.3 17.0 %all-reduce.8.cloned.1.call-done = (bf16[1,128,128]{2,1,0:T(8,128)(2,1)}, bf16[1,128,128]{2,1,0:T(8,128)(2,1)}) async-done(((bf16[1,128,128]{2,1,0:T(8,128)(2,1)}, bf16[1,128,128]{2,1,0:T(8,128)(2,1)}), (bf16[1,128,128]{2,1,0:T(8,128)(2,1)}, bf16[1,128,128]{2,1,0:T(8,128)(2,1)})) %all-reduce.8.cloned.1.call-update) | async-done | bytes 65552 | tf_op jit(solution)/shard_map/psum | solution.py:256
  117.3 1.4 %broadcast_in_dim.183 = f32[1,128,128]{2,1,0:T(8,128)} convert(bf16[1,128,128]{2,1,0:T(8,128)(2,1)} %get-tuple-element.717) | non-fusion elementwise | flops 16384 | bytes 98304 | tf_op jit(solution)/shard_map/broadcast_in_dim | solution.py:292
  119.3 0.9 copy.121
  120.2 1.5 %collective-permute-start.3 = (bf16[128,64]{0,1:T(8,128)(2,1)S(1)}, bf16[128,64]{0,1:T(8,128)(2,1)S(1)}, u32[]{:S(2)}, u32[]{:S(2)}) collective-permute-start(bf16[128,64]{0,1:T(8,128)(2,1)S(1)} %dynamic-slice_convert_fusion), channel_id=1, source_target_pairs={{0,4},{4,0},{8,12},{12,8},{1,5},{5,1},{9,13},{13,9},{2,6},{6,2},{1... | collective-permute-start | bytes 49160 | tf_op jit(solution)/shard_map/ppermute | solution.py:13
  121.7 0.9 copy.119
  124.6 1.8 %collective-permute-done.2 = bf16[128,64]{0,1:T(8,128)(2,1)S(1)} collective-permute-done((bf16[128,64]{0,1:T(8,128)(2,1)S(1)}, bf16[128,64]{0,1:T(8,128)(2,1)S(1)}, u32[]{:S(2)}, u32[]{:S(2)}) %collective-permute-start.2) | collective-permute-done | bytes 16416 | tf_op jit(solution)/shard_map/ppermute | solution.py:13
  (197 shorter events, 30.8 us)
Async XLA Ops:
  8.0 7.2 %copy-start = (bf16[1,128,128]{2,1,0:T(8,128)(2,1)S(1)}, bf16[1,128,128]{2,1,0:T(8,128)(2,1)}, u32[]{:S(2)}) copy-start(bf16[1,128,128]{2,1,0:T(8,128)(2,1)} %param.25) | copy-start | bytes 98308
  8.0 4.0 %copy-start.22 = (bf16[1,128,64]{1,2,0:T(8,128)(2,1)S(1)}, bf16[1,128,64]{1,2,0:T(8,128)(2,1)}, u32[]{:S(2)}) copy-start(bf16[1,128,64]{1,2,0:T(8,128)(2,1)} %param.22) | copy-start | bytes 49156
  8.0 109.2 %all-reduce.8.cloned.1.call-start = ((), (), s32[]{:S(2)}) async-start(), calls=%async_computation.4 | async-start | bytes 131072 | tf_op jit(solution)/shard_map/psum | solution.py:256
  8.9 25.8 %collective-permute-start = (bf16[128,64]{1,0:T(8,128)(2,1)S(1)}, bf16[128,64]{1,0:T(8,128)(2,1)S(1)}, u32[]{:S(2)}, u32[]{:S(2)}) collective-permute-start(bf16[128,64]{1,0:T(8,128)(2,1)S(1)} %bitcast.284), channel_id=1, source_target_pairs={{0,4},{4,0},{8,12},{12,8},{1,5},{5,1},{9,13},{13,9},{2,6},{6,2},{1... | collective-permute-start | bytes 49160 | tf_op jit(solution)/shard_map/ppermute | solution.py:13
  12.1 27.4 %collective-permute-start.1 = (bf16[128,64]{1,0:T(8,128)(2,1)S(1)}, bf16[128,64]{1,0:T(8,128)(2,1)S(1)}, u32[]{:S(2)}, u32[]{:S(2)}) collective-permute-start(bf16[128,64]{1,0:T(8,128)(2,1)S(1)} %bitcast.282), channel_id=1, source_target_pairs={{0,4},{4,0},{8,12},{12,8},{1,5},{5,1},{9,13},{13,9},{2,6},{6,2},{1... | collective-permute-start | bytes 49160 | tf_op jit(solution)/shard_map/ppermute | solution.py:13
  13.3 0.8 copy-start.29
  14.1 4.5 %copy-start.36 = (f32[8]{0:T(128)}, f32[8]{0:T(128)S(1)}, u32[]{:S(2)}) copy-start(f32[8]{0:T(128)S(1)} %get-tuple-element.726) | copy-start | bytes 100
  15.1 30.9 %copy-start.14 = (f32[128,8]{0,1:T(8,128)}, f32[128,8]{0,1:T(8,128)S(1)}, u32[]{:S(2)}) copy-start(f32[128,8]{0,1:T(8,128)S(1)} %get-tuple-element.739) | copy-start | bytes 12292
  15.1 37.8 %copy-start.10 = (f32[128,8]{0,1:T(8,128)}, f32[128,8]{0,1:T(8,128)S(1)}, u32[]{:S(2)}) copy-start(f32[128,8]{0,1:T(8,128)S(1)} %get-tuple-element.738) | copy-start | bytes 12292
  15.2 0.8 copy-start.1
  15.9 8.6 %copy-start.7 = (bf16[1,128,512]{2,1,0:T(8,128)(2,1)S(1)}, bf16[1,128,512]{2,1,0:T(8,128)(2,1)}, u32[]{:S(2)}) copy-start(bf16[1,128,512]{2,1,0:T(8,128)(2,1)} %param.20) | copy-start | bytes 393220
  24.6 0.9 copy-start.8
  25.7 0.9 copy-start.9
  52.0 0.9 copy-start.12
  52.0 0.9 copy-start.23
  52.0 0.9 copy-start.31
  54.1 2.0 %copy-start.11 = (f32[128,8]{0,1:T(8,128)S(1)}, f32[128,8]{0,1:T(8,128)}, u32[]{:S(2)}) copy-start(f32[128,8]{0,1:T(8,128)} %copy-done.10) | copy-start | bytes 12292
  57.4 1.2 copy-start.28
  68.4 0.8 copy-start.13
  68.4 0.8 copy-start.24
  68.4 0.8 copy-start.32
  80.1 0.9 copy-start.2
  80.1 0.9 copy-start.5
  80.1 2.6 %copy-start.27 = (f32[4,128]{1,0:T(4,128)S(1)}, f32[4,128]{1,0:T(4,128)}, u32[]{:S(2)}) copy-start(f32[4,128]{1,0:T(4,128)} %get-tuple-element.723) | copy-start | bytes 6148
  81.7 1.0 copy-start.4
  81.7 0.7 copy-start.35
  81.8 37.5 %reduce-scatter.9.cloned.1.call-start = ((), (), s32[]{:S(2)}) async-start(), calls=%async_computation.3 | async-start | bytes 98304
  82.9 0.8 copy-start.3
  84.7 37.0 %reduce-scatter.7.cloned.1.call-start = ((), (), s32[]{:S(2)}) async-start(), calls=%async_computation.2 | async-start | bytes 98304
  117.3 1.4 %copy-start.16 = (bf16[1,128,128]{2,1,0:T(8,128)(2,1)S(1)}, bf16[1,128,128]{2,1,0:T(8,128)(2,1)}, u32[]{:S(2)}) copy-start(bf16[1,128,128]{2,1,0:T(8,128)(2,1)} %get-tuple-element.718) | copy-start | bytes 98308
  120.2 3.8 %collective-permute-start.3 = (bf16[128,64]{0,1:T(8,128)(2,1)S(1)}, bf16[128,64]{0,1:T(8,128)(2,1)S(1)}, u32[]{:S(2)}, u32[]{:S(2)}) collective-permute-start(bf16[128,64]{0,1:T(8,128)(2,1)S(1)} %dynamic-slice_convert_fusion), channel_id=1, source_target_pairs={{0,4},{4,0},{8,12},{12,8},{1,5},{5,1},{9,13},{13,9},{2,6},{6,2},{1... | collective-permute-start | bytes 49160 | tf_op jit(solution)/shard_map/ppermute | solution.py:13
  122.6 3.8 %collective-permute-start.2 = (bf16[128,64]{0,1:T(8,128)(2,1)S(1)}, bf16[128,64]{0,1:T(8,128)(2,1)S(1)}, u32[]{:S(2)}, u32[]{:S(2)}) collective-permute-start(bf16[128,64]{0,1:T(8,128)(2,1)S(1)} %dynamic-slice_convert_fusion.1), channel_id=1, source_target_pairs={{0,4},{4,0},{8,12},{12,8},{1,5},{5,1},{9,13},{13,9},{2,6},{6,2},{1... | collective-permute-start | bytes 49160 | tf_op jit(solution)/shard_map/ppermute | solution.py:13
  (18 other events, 12.0 us)
Sparse Core Ops, SparseCore 0:
  81.9 35.3 all-reduce.7
Sparse Core Ops, SparseCore 1:
  84.8 11.1 reduce-scatter.8
  98.0 9.9 reduce-scatter.6
where the time goes:
time: 135 us; the launch traced here: 134 us
  blocking collectives  44.2 us (33%)
  local copies, waits for them, and re-layouts  22.6 us (17%)
  waiting for transfers between devices  19.5 us (14%)
  between operations  16.7 us (12%)
  matrix products  14.5 us (11%)
  other arithmetic  11.3 us (8%)
  starting transfers between devices  5.47 us (4%)
    psum x1, waiting for transfers between devices, body(): lax.psum(main_write.astype(jnp.bfloat16), 'tp').astype(jnp.float32)  17 us
    unnamed x101, local copies, waits for them, and re-layouts  16.8 us
    psum x1, blocking collectives, body(): lax.psum((main_alog + entry_alog, main_skip, main_bias + entry_bias), ('s...  12.3 us
    unnamed x2, blocking collectives  9.83 us
    all_gather x1, blocking collectives, prefix(): everything = jax.tree.map(lambda part: lax.all_gather(part, axis), array)  7.05 us
    all_gather x1, blocking collectives, carried_in(): lax.all_gather(a.astype(kind), axis)  5.64 us
    ppermute x4, starting transfers between devices, from_partner(): lax.ppermute(array, axis, [(i, i ^ 1 << distance) for i in range(lax.axis...  5.34 us
    all_gather x1, blocking collectives, body(): lax.all_gather(local_keys, 'seq', axis=0, tiled=True)  4.77 us
  transfers between devices with their start and end apart: 7, of which 3 were waited for; matrix products, arithmetic and copies ran while one was open for 12% of the time, Pallas kernels for 0%

commit v1 on v0

v1 whole, which is shorter than its diff:
```python
import jax
import jax.numpy as jnp
from jax import lax
from jax.experimental import pallas as pl
from jax.experimental.pallas import tpu as pltpu
from jax.sharding import PartitionSpec as P

NEG_FILL = -1e30
LOG2E = 1.4426950408889634
F32 = jnp.float32
BF16 = jnp.bfloat16
NN = (((1,), (0,)), ((), ()))
NT = (((1,), (1,)), ((), ()))
TN = (((0,), (0,)), ((), ()))


def dot(a, b, dims=NN):
    return lax.dot_general(a.astype(BF16), b.astype(BF16), dims, preferred_element_type=F32)


def parts_of(array, count):
    parts = []
    for _ in range(count):
        parts.append(array.astype(BF16))
        array = array - parts[-1].astype(F32)
    return parts


def dot_flags(arrays, flags, count=3):
    split_up = [parts_of(a, count) for a in arrays]
    left = [parts[i] for i in range(count) for parts in split_up]
    right = jnp.concatenate([jnp.where(f, 1.0, 0.0) for f in flags] * count, axis=0)
    return dot(jnp.concatenate(left, axis=1), right)


def iota(shape, axis):
    return lax.broadcasted_iota(jnp.int32, shape, axis)


def column(ref, width):
    heads = ref.shape[0]
    at = iota((heads, width), 0)
    out = jnp.full((heads, width), ref[0], F32)
    for m in range(1, heads):
        out = jnp.where(at == m, ref[m], out)
    return out


def rates(raw, bias, alog):
    rows = raw.shape[1]
    shifted = raw + bias
    step = jnp.maximum(shifted, 0.0) + jnp.log1p(jnp.exp(-jnp.abs(shifted)))
    rate = step * jnp.exp(alog)
    return step, rate, dot_flags([rate], [iota((rows, rows), 0) <= iota((rows, rows), 1)])


def spread(cols, m, width):
    return jnp.broadcast_to(cols[:, m : m + 1], (cols.shape[0], width))


def widen(factors, channels):
    heads = factors.shape[0]
    shape = (3 * heads, heads * channels)
    pick = (iota(shape, 1) // channels == iota(shape, 0) % heads).astype(BF16)
    return dot(jnp.concatenate(parts_of(factors, 3), axis=0), pick, TN)


def stack(wide, width):
    return jnp.concatenate([wide[:, i : i + width] for i in range(0, wide.shape[1], width)], axis=0)


def unstack(tall, rows):
    return jnp.concatenate([tall[i : i + rows] for i in range(0, tall.shape[0], rows)], axis=1)


def attend(jobs, scale):
    shapes = [(q.shape[0] // m.shape[0],) + m.shape for q, _, _, m in jobs]
    scores = [
        jnp.where(m[None], (dot(q, k) * (scale * LOG2E)).reshape(dims), NEG_FILL)
        for (q, k, _, m), dims in zip(jobs, shapes)
    ]
    tops = [jnp.max(s, axis=2, keepdims=True) for s in scores]
    weights = [
        jnp.exp2(s - top).reshape(dims[0] * dims[1], dims[2])
        for s, top, dims in zip(scores, tops, shapes)
    ]
    both = [
        dot(w, jnp.concatenate([v, jnp.ones_like(v)], axis=0), NT)
        for w, (_, _, v, _) in zip(weights, jobs)
    ]
    width = jobs[0][2].shape[0]
    shares = [1.0 / b[:, width:] for b in both]
    return [(b[:, :width] * share, w, share) for b, w, share in zip(both, weights, shares)]


def _fold(join, parts):
    out = parts[0]
    for part in parts[1:]:
        out = join(out, part)
    return out


def slot_mask(here, query_slot, slots, rows):
    masks = []
    for slot in slots:
        if slot == query_slot:
            masks.append(iota((rows, rows), 0) >= iota((rows, rows), 1))
        else:
            seen = jnp.bitwise_xor(here, slot) < jnp.bitwise_xor(here, query_slot)
            masks.append(jnp.broadcast_to(seen, (rows, rows)))
    return jnp.concatenate(masks, axis=1)


def share_kernel(*refs):
    sources, (pack, message), held, arrived = refs[:10], refs[10:12], refs[12:22], refs[22]
    copies = [
        pltpu.make_async_copy(source, here, arrived.at[i])
        for i, (source, here) in enumerate(zip(sources, held))
    ]
    for copy in copies:
        copy.start()
    raw, alog, bias, gate, cotangent, read, query, key, value, write = held
    for copy in copies[:3]:
        copy.wait()
    here = lax.axis_index("seq")
    heads, rows = raw.shape[1:]
    wide, states = gate.shape[2], read.shape[2]
    half = key.shape[1]
    step, _, cum = rates(raw[0], column(bias, rows), column(alog, rows))
    decay = widen(jnp.exp(-cum), wide // heads)
    to_end = jnp.exp(cum - cum[:, rows - 1 :]) * step
    whole = jnp.broadcast_to(jnp.exp(-cum[:, rows - 1 :]), (heads, rows))
    tail = jnp.concatenate([to_end, whole], axis=0).astype(BF16)
    for copy in copies[3:]:
        copy.wait()
    pack[:half] = key[0]
    pack[half:] = value[0]
    gate_f = gate[0].astype(F32)
    grad_mixed = cotangent[0].astype(F32) * gate_f * jax.nn.sigmoid(gate_f)
    entry = dot(read[0], grad_mixed * decay, TN).astype(BF16)
    for bit in range(message.shape[0]):
        is_early = jnp.bitwise_and(lax.shift_right_logical(here, bit), 1) == 0
        for at in range(0, wide, states):
            message[bit, at : at + rows] = jnp.where(
                is_early, query[0, :, at : at + states], entry[:, at : at + states]
            )
        message[bit, wide : wide + half] = key[0]
        message[bit, wide + half : wide + 2 * half] = value[0]
        message[bit, wide + rows : wide + 2 * rows] = write[0]
        message[bit, wide + 2 * rows :] = tail


def prepare_kernel(gate, cotangent, write, read, raw, alog, skip, bias, *outs):
    mixed_out, slope_out, step_out, in_out, out_out, own_out, fall_out, back_out = outs[:8]
    ahead_out, split_out, rates_out, skip_out = outs[8:]
    heads, rows = raw.shape[1:]
    wide = gate.shape[2]
    channels = wide // heads
    pair = 2 * channels
    alog_c, bias_c = column(alog, rows), column(bias, rows)
    step, rate, cum = rates(raw[0], bias_c, alog_c)
    for i, table in enumerate((step, rate, cum, jnp.exp(alog_c), jax.nn.sigmoid(raw[0] + bias_c))):
        rates_out[i * heads : (i + 1) * heads] = table
    head_of = iota(skip_out.shape, 1) // channels
    skip_w = jnp.full(skip_out.shape, skip[0], F32)
    for m in range(1, heads):
        skip_w = jnp.where(head_of == m, skip[m], skip_w)
    skip_out[...] = skip_w
    gate_f = gate[0].astype(F32)
    sig = jax.nn.sigmoid(gate_f)
    cot = cotangent[0].astype(F32)
    grad_mixed = cot * gate_f * sig
    mixed_out[...] = grad_mixed
    slope_out[...] = cot * sig * (1.0 + gate_f * (1.0 - sig))
    cum_cols = cum.T
    step_out[...] = widen(step, channels)
    in_out[...] = widen(jnp.exp(-cum), channels)
    out_out[...] = widen(jnp.exp(cum - cum[:, rows - 1 :]), channels)
    read_b, write_b = read[0], write[0]
    upper = iota((rows, rows), 0) <= iota((rows, rows), 1)
    lower = iota((rows, rows), 0) >= iota((rows, rows), 1)
    cross = jnp.where(lower, dot(read_b, write_b, NT), 0.0)
    cross_t = jnp.where(upper, dot(write_b, read_b, NT), 0.0)
    low = iota((rows, pair), 1) < channels
    for m in range(0, heads, 2):
        block = slice(m * channels, (m + 2) * channels)
        grad_p = grad_mixed[:, block]
        grad_d = jnp.concatenate(
            [jnp.where(low, grad_p, 0.0), jnp.where(low, 0.0, grad_p)], axis=0
        ).astype(BF16)
        split_out[m * rows : (m + 2) * rows] = grad_d
        backs = []
        for k in range(m, m + 2):
            gap = spread(cum_cols, k, rows) - cum[k : k + 1, :]
            fall = jnp.exp(-jnp.abs(gap))
            back = fall * cross_t
            at = slice(k * rows, (k + 1) * rows)
            fall_out[at] = fall
            back_out[at] = back
            ahead_out[:, at] = (fall * cross).astype(BF16)
            backs.append(back.astype(BF16))
        own_out[:, block] = dot(jnp.concatenate(backs, axis=1), grad_d)


def state_kernel(slots, scale, query, write, read, partner, *refs):
    mixed_in, step_in, in_in, out_in, own_in, fall_in, split_in, skip_in = refs[:8]
    refs = refs[8:]
    far, sources, refs = refs[: slots - 1], refs[slots - 1 : 2 * slots - 1], refs[2 * slots - 1 :]
    kept, sent, scores_out, keys_out, scaled_out, base_out, products_out = refs[:7]
    (pack, *messages), arrived = refs[7 : 7 + slots], refs[7 + slots]
    copies = [
        pltpu.make_async_copy(source, held, arrived.at[i])
        for i, (source, held) in enumerate(zip(sources, (pack, *messages)))
    ]
    for copy in copies:
        copy.start()
    here = lax.axis_index("seq")
    parity = lax.axis_index("tp") % 2
    rows, wide = query.shape[1:]
    heads = fall_in.shape[0] // rows
    channels = wide // heads
    states, head_dim = write.shape[2], pack.shape[0]
    half, pair, count = head_dim // 2, 2 * channels, wide // head_dim
    for copy in copies:
        copy.wait()

    key_parts, value_parts = [], []
    for slot in range(slots):
        near = messages[slot - 1][wide : wide + head_dim] if slot else pack[...]
        paired = far[slot - 1][...] if slot else partner[...]
        first = jnp.where(parity == 0, near, paired)
        second = jnp.where(parity == 0, paired, near)
        key_parts.append(jnp.concatenate([first[:half], second[:half]], axis=0))
        value_parts.append(jnp.concatenate([first[half:], second[half:]], axis=0))
    keys, values = jnp.concatenate(key_parts, axis=1), jnp.concatenate(value_parts, axis=1)
    keys_out[...] = keys

    grad_mixed, step_w, decay_in, decay_out = mixed_in[...], step_in[...], in_in[...], out_in[...]
    skip_w = skip_in[:1]
    read_b, write_b = read[0], write[0]
    tails = [m[wide + 2 * rows :].astype(F32) for m in messages]
    exit_t = jnp.zeros((states, wide), F32)
    early, to_ends = [], []
    for slot in range(1, slots):
        block = jnp.bitwise_xor(here, slot)
        early.append(block < here)
        between = jnp.ones((heads, rows), F32)
        for third in range(1, slots):
            if third != slot:
                at = jnp.bitwise_xor(here, third)
                inside = jnp.logical_and(
                    at > jnp.minimum(block, here), at < jnp.maximum(block, here)
                )
                between = between * jnp.where(inside, tails[third - 1][heads:], 1.0)
        later = unstack(messages[slot - 1][:wide], rows).astype(F32)
        if slots > 2:
            later = later * widen(between, channels)
        exit_t = exit_t + jnp.where(early[-1], 0.0, later)
        to_ends.append(widen(tails[slot - 1][:heads] * between, channels))
    exit_b = exit_t.astype(BF16)
    from_exit = decay_out * dot(write_b, exit_b)
    grad_scaled = own_in[...] + from_exit
    grad_inner = step_w * grad_scaled + skip_w * grad_mixed
    grads = stack(grad_inner, head_dim)
    grads_b = grads.astype(BF16)

    queries = stack(query[0], head_dim)
    jobs = [(queries, keys, values, slot_mask(here, 0, range(slots), rows))]
    for slot in range(1, slots):
        whole = slots > 2
        mask = slot_mask(here, slot, range(slots) if whole else [slot], rows)
        some = (keys, values) if whole else (key_parts[slot], value_parts[slot])
        jobs.append((messages[slot - 1][:wide], *some, mask))
    (attn, weights, share), *before = attend(jobs, scale)
    grad_probs = dot(grads_b, values)
    inner = unstack(attn, rows)
    scaled = inner * step_w
    scaled_b = scaled.astype(BF16)
    scaled_out[...] = scaled_b
    entry_t = jnp.zeros((states, wide), F32)
    for message, is_early, to_end, (attn_o, _, _) in zip(messages, early, to_ends, before):
        carried = unstack(attn_o, rows) * to_end
        end_state = dot(message[wide + rows : wide + 2 * rows], carried, TN)
        entry_t = entry_t + jnp.where(is_early, end_state, 0.0)
    entry_b = entry_t.astype(BF16)
    from_entry = decay_in * dot(read_b, entry_b)
    base_out[...] = from_entry + skip_w * inner

    product = grads * attn
    ones = jnp.ones((2 * head_dim, head_dim), BF16)
    delta = dot(jnp.concatenate(parts_of(product, 2), axis=1), ones)
    probs = weights * jnp.concatenate([share] * slots, axis=1)
    grad_scores = (probs * (grad_probs - jnp.concatenate([delta] * slots, axis=1))).astype(BF16)
    scores_out[...] = grad_scores
    key_t = (dot(queries, grad_scores, TN) * scale).astype(BF16)
    value_t = dot(grads_b, probs, TN).astype(BF16)
    for slot in range(slots):
        block = slice(slot * rows, (slot + 1) * rows)
        first = jnp.concatenate([key_t[:half, block], value_t[:half, block]], axis=0)
        second = jnp.concatenate([key_t[half:, block], value_t[half:, block]], axis=0)
        kept[slot] = jnp.where(parity == 0, first, second)
        sent[slot * head_dim : (slot + 1) * head_dim] = jnp.where(parity == 0, second, first)

    upper = iota((rows, rows), 0) <= iota((rows, rows), 1)
    grad_cross_t = jnp.zeros((rows, rows), F32)
    for m in range(0, heads, 2):
        outer = dot(
            scaled_b[:, m * channels : (m + 2) * channels], split_in[m * rows : (m + 2) * rows], NT
        )
        grad_cross_t = grad_cross_t + outer[:, :rows] * fall_in[m * rows : (m + 1) * rows]
        grad_cross_t = grad_cross_t + outer[:, rows:] * fall_in[(m + 1) * rows : (m + 2) * rows]
    grad_cross_t = jnp.where(upper, grad_cross_t, 0.0)
    grad_write = dot(grad_cross_t, read_b) + dot(scaled * decay_out, exit_b, NT)
    grad_read = dot(grad_cross_t, write_b, TN) + dot(grad_mixed * decay_in, entry_b, NT)
    sent[slots * head_dim : slots * head_dim + rows] = grad_write.astype(BF16)
    sent[slots * head_dim + rows :] = grad_read.astype(BF16)
    products = (
        inner * grad_scaled,
        inner * from_exit,
        grad_mixed * from_entry,
        grad_mixed * inner,
        exit_t * entry_t,
    )
    for i, product in enumerate(products):
        products_out[i * rows : (i + 1) * rows] = product.astype(BF16)


def rates_kernel(products, scaled, halves, back, tables, grad_raw, params):
    heads, rows = grad_raw.shape[1:]
    wide = products.shape[1]
    channels = wide // heads
    step, rate, cum, grow, slope = [tables[i * heads : (i + 1) * heads] for i in range(5)]
    strict = iota((rows, rows), 0) < iota((rows, rows), 1)
    lower = iota((rows, rows), 0) >= iota((rows, rows), 1)
    terms = []
    for m in range(0, heads, 2):
        outer = dot(
            scaled[:, m * channels : (m + 2) * channels], halves[m * rows : (m + 2) * rows], NT
        )
        terms.append((outer[:, :rows] * back[m * rows : (m + 1) * rows]).astype(BF16))
        terms.append((outer[:, rows:] * back[(m + 1) * rows : (m + 2) * rows]).astype(BF16))
    later = dot(jnp.concatenate(terms, axis=0), jnp.where(lower, 1.0, 0.0))
    rate_rows = [
        jnp.sum(jnp.where(strict, later[m * rows : (m + 1) * rows], 0.0), axis=0, keepdims=True)
        for m in range(heads)
    ]
    pick = (iota((heads, wide), 1) // channels == iota((heads, wide), 0)).astype(BF16)
    sums = dot(pick, products[...], NT)
    grad_step = sums[:, :rows]
    exit_sum = sums[:, rows : 2 * rows] * step
    entry_sum = sums[:, 2 * rows : 3 * rows]
    skip_sum = sums[:, 3 * rows : 4 * rows]
    carry_sum = jnp.sum(sums[:, 4 * rows :], axis=1, keepdims=True) * jnp.exp(-cum[:, rows - 1 :])
    grad_rate = -(
        jnp.concatenate(rate_rows, axis=0)
        + dot_flags([entry_sum, exit_sum], [lower, strict])
        + carry_sum
    )
    grad_shift = (grad_step + grad_rate * grow) * slope
    grad_raw[0] = grad_shift
    terms = jnp.concatenate([grad_rate * rate, skip_sum, grad_shift], axis=0)
    summed = jnp.concatenate(parts_of(terms, 3), axis=1)
    params[:, : 3 * heads] = dot(jnp.ones((8, 3 * rows), F32), summed, NT)
    params[:, 3 * heads :] = jnp.zeros((8, params.shape[1] - 3 * heads), F32)


def output_kernel(scale, ahead, scaled, base, slope, scores, keys, grad_gate, grad_query):
    rows, wide = base.shape
    channels = wide * rows // ahead.shape[1]
    pair = 2 * channels
    low = iota((rows, pair), 1) < channels
    for at in range(0, wide, pair):
        block = slice(at, at + pair)
        scaled_p = scaled[:, block].astype(F32)
        scaled_d = jnp.concatenate(
            [jnp.where(low, scaled_p, 0.0), jnp.where(low, 0.0, scaled_p)], axis=0
        )
        m = at // channels
        mixed = dot(ahead[:, m * rows : (m + 2) * rows], scaled_d) + base[:, block]
        grad_gate[0, :, block] = mixed * slope[:, block]
    grad_query[0] = unstack(dot(scores[...], keys[...], NT) * scale, rows)


def finish_kernel(count, *refs):
    arrived, (mine, other, tail, shared, got) = refs[:count], refs[count : count + 5]
    grad_key, grad_value, grad_write, grad_read, grad_alog, grad_skip, grad_bias = refs[count + 5 :]
    half, rows = grad_key.shape[1:]
    total = mine[0].astype(F32) + other[: 2 * half].astype(F32)
    for term in arrived:
        total = total + term[: 2 * half].astype(F32)
    grad_key[0] = total[:half]
    grad_value[0] = total[half:]
    both = shared[...].astype(F32) + got[...].astype(F32)
    grad_write[0] = both[:rows]
    grad_read[0] = both[rows:]
    heads = grad_alog.shape[0]
    params = joined(tail[...]) + joined(arrived[-1][2 * half :])
    grad_alog[...] = params[0, :heads]
    grad_skip[...] = params[0, heads : 2 * heads]
    grad_bias[...] = params[0, 2 * heads : 3 * heads]


def split(sums):
    high = lax.reduce_precision(sums, 8, 7)
    return jnp.concatenate([high.astype(BF16), (sums - high).astype(BF16)], axis=0)


def joined(tail):
    tail = tail.astype(F32)
    count = tail.shape[0] // 2
    return tail[:count] + tail[count:]


def flip(axis, distance):
    return [(i, i ^ distance) for i in range(lax.axis_size(axis))]


def shape(dims, dtype):
    return jax.ShapeDtypeStruct(tuple(dims), dtype)


VMEM = pl.BlockSpec(memory_space=pltpu.VMEM)
SMEM = pl.BlockSpec(memory_space=pltpu.SMEM)
HBM = pl.BlockSpec(memory_space=pltpu.HBM)
PARAMS = pltpu.CompilerParams(vmem_limit_bytes=48 * 1024 * 1024)


def call(kernel, outs, args, specs=None, scratch=(), flops=0):
    return pl.pallas_call(
        kernel,
        out_shape=outs,
        in_specs=[(specs or {}).get(i, VMEM) for i in range(len(args))],
        out_specs=jax.tree.map(lambda _: VMEM, outs),
        scratch_shapes=scratch,
        compiler_params=PARAMS,
        cost_estimate=pl.CostEstimate(flops=flops, bytes_accessed=0, transcendentals=0),
    )(*args)


def swap(array, seq_bits, tp_bits, to_later=None):
    n_seq, n_tp = lax.axis_size("seq"), lax.axis_size("tp")
    pairs = [
        (s * n_tp + t, (s ^ seq_bits) * n_tp + (t ^ tp_bits))
        for s in range(n_seq)
        for t in range(n_tp)
        if to_later is None or ((s ^ seq_bits) > s) == to_later
    ]
    return lax.ppermute(array, ("seq", "tp"), pairs)


def body(
    query_rows,
    key_rows,
    value_rows,
    gate_rows,
    write_vec,
    read_vec,
    dt_raw,
    a_log,
    skip_gain,
    dt_bias,
    out_grad,
):
    slots = lax.axis_size("seq")
    rows, wide = query_rows.shape[1:]
    head_dim = 2 * key_rows.shape[2]
    states = write_vec.shape[2]
    heads = a_log.shape[0]
    scale = head_dim ** (-0.5)

    bits = slots.bit_length() - 1
    key_t, value_t = key_rows.swapaxes(1, 2), value_rows.swapaxes(1, 2)
    sources = (
        dt_raw,
        a_log,
        dt_bias,
        gate_rows,
        out_grad,
        read_vec,
        query_rows,
        key_t,
        value_t,
        write_vec,
    )
    pack, message = pl.pallas_call(
        share_kernel,
        out_shape=(
            shape((head_dim, rows), BF16),
            shape((bits, wide + 2 * rows + 2 * heads, head_dim), BF16),
        ),
        in_specs=[HBM] * len(sources),
        out_specs=(VMEM, VMEM),
        scratch_shapes=[
            pltpu.SMEM(a.shape, a.dtype) if a.ndim == 1 else pltpu.VMEM(a.shape, a.dtype)
            for a in sources
        ]
        + [pltpu.SemaphoreType.DMA((len(sources),))],
        compiler_params=PARAMS,
    )(*[pltpu.with_memory_space_constraint(a, pltpu.HBM) for a in sources])
    messages = [swap(message[slot.bit_length() - 1], slot, 0) for slot in range(1, slots)]
    partner = swap(pack, 0, 1)
    far = [swap(pack, slot, 1, True) for slot in range(1, slots)]

    wide_f, wide_b = shape((rows, wide), F32), shape((rows, wide), BF16)
    tall_f = shape((heads * rows, rows), F32)
    prepared = call(
        prepare_kernel,
        (wide_f,) * 6
        + (tall_f, tall_f)
        + (shape((rows, heads * rows), BF16), shape((heads * rows, 2 * wide // heads), BF16))
        + (shape((5 * heads, rows), F32), shape((8, wide), F32)),
        (gate_rows, out_grad, write_vec, read_vec, dt_raw, a_log, skip_gain, dt_bias),
        {5: SMEM, 6: SMEM, 7: SMEM},
    )
    grad_mixed, slope, step_w, decay_in, decay_out, own, fall, back = prepared[:8]
    ahead, halves, tables, skip_w = prepared[8:]
    mine, other, scores, keys, scaled, base, products = call(
        lambda *refs: state_kernel(slots, scale, *refs),
        (
            shape((slots, head_dim, rows), BF16),
            shape((slots * head_dim + 2 * rows, states), BF16),
            shape((wide // head_dim * rows, slots * rows), BF16),
            shape((head_dim, slots * rows), BF16),
            wide_b,
            wide_f,
            shape((5 * rows, wide), BF16),
        ),
        (
            query_rows,
            write_vec,
            read_vec,
            partner,
            grad_mixed,
            step_w,
            decay_in,
            decay_out,
            own,
            fall,
            halves,
            skip_w,
            *far,
            pack,
            *messages,
        ),
        {11 + slots + i: HBM for i in range(slots)},
        [pltpu.VMEM(m.shape, m.dtype) for m in (pack, *messages)]
        + [pltpu.SemaphoreType.DMA((slots,))],
    )
    got = swap(other, 0, 1)
    grad_dt, params = call(
        rates_kernel,
        (shape((1, heads, rows), F32), shape((8, states), F32)),
        (products, scaled, halves, back, tables),
    )
    reach = 1
    while reach < lax.axis_size("dp"):
        near = [params] + [lax.ppermute(params, "dp", flip("dp", k * reach)) for k in (1, 2, 3)]
        got, *near = lax.optimization_barrier((got, *near))
        params = (near[0] + near[1]) + (near[2] + near[3])
        reach *= 4
    sent = [
        (mine[slot].astype(F32) + got[slot * head_dim : (slot + 1) * head_dim].astype(F32)).astype(BF16)
        for slot in range(1, slots)
    ]
    arrived = [swap(sent[slot - 1], slot, 0, False) for slot in range(1, slots) if slot & (slot - 1)]
    slot = 1
    while slot < slots:
        tail = split(params)
        arrived.append(swap(jnp.concatenate([sent[slot - 1], tail], axis=0), slot, 0))
        slot *= 2
        if slot < slots:
            params = joined(tail) + joined(arrived[-1][head_dim:])
    shared, got_shared = other[slots * head_dim :], got[slots * head_dim :]
    reach = 2
    while reach < lax.axis_size("tp"):
        shared = (shared.astype(F32) + got_shared.astype(F32)).astype(BF16)
        got_shared = swap(shared, 0, reach)
        reach *= 2
    scores, shared = lax.optimization_barrier((scores, shared))
    grad_gate, grad_query = call(
        lambda *refs: output_kernel(scale, *refs),
        (shape((1, rows, wide), F32), shape((1, rows, wide), F32)),
        (ahead, scaled, base, slope, scores, keys),
    )
    vector = shape((heads,), F32)
    half = shape((1, head_dim // 2, rows), F32)
    full = shape((1, rows, states), F32)
    grad_key, grad_value, grad_write, grad_read, grad_alog, grad_skip, grad_bias = call(
        lambda *refs: finish_kernel(len(arrived), *refs),
        (half, half, full, full, vector, vector, vector),
        (*arrived, mine, got, tail, shared, got_shared),
    )
    grad_key, grad_value = grad_key.swapaxes(1, 2), grad_value.swapaxes(1, 2)
    return (
        grad_query,
        grad_key,
        grad_value,
        grad_gate,
        grad_write,
        grad_read,
        grad_dt,
        grad_alog,
        grad_skip,
        grad_bias,
    )


def solution(mesh):
    in_specs = (
        P("dp", "seq", "tp"),
        P("dp", "seq", "tp"),
        P("dp", "seq", "tp"),
        P("dp", "seq", "tp"),
        P("dp", "seq", None),
        P("dp", "seq", None),
        P("dp", "tp", "seq"),
        P("tp"),
        P("tp"),
        P("tp"),
        P("dp", "seq", "tp"),
    )
    out_specs = (
        P("dp", "seq", "tp"),
        P("dp", "seq", "tp"),
        P("dp", "seq", "tp"),
        P("dp", "seq", "tp"),
        P("dp", "seq", None),
        P("dp", "seq", None),
        P("dp", "tp", "seq"),
        P("tp"),
        P("tp"),
        P("tp"),
    )
    return jax.shard_map(body, mesh=mesh, in_specs=in_specs, out_specs=out_specs, check_vma=False)
```

time: 135 us -> 28.7 us (0.21)
  blocking collectives: 44.2 us -> 0 us
  local copies, waits for them, and re-layouts: 22.6 us -> 0.05 us
  between operations: 16.7 us -> 0.85 us
  matrix products: 14.5 us -> 0 us
  waiting for transfers between devices: 19.5 us -> 7.06 us
  other arithmetic: 11.3 us -> 0.06 us
  Pallas kernels: 0 us -> 7.76 us
  starting transfers between devices: 5.47 us -> 12.7 us
    all_gather x4 -> x0, blocking collectives: 22.1 us -> none  [the longest x1 7.05 us: prefix(): everything = jax.tree.map(lambda part: lax.all_gather(part, axis), array)]
    psum x1 -> x0, waiting for transfers between devices: 17 us -> none  [body(): lax.psum(main_write.astype(jnp.bfloat16), 'tp').astype(jnp.float32)]
    unnamed x101 -> x18, local copies, waits for them, and re-layouts: 16.8 us -> 0.05 us
    dot_general x21 -> x0, matrix products: 14.5 us -> none  [the longest x3 4 us: advance(): output = jnp.einsum('hts,shp->thp', weight, inner_now, precision=HIGH)]
    psum x1 -> x0, blocking collectives: 12.3 us -> none  [body(): lax.psum((main_alog + entry_alog, main_skip, main_bias + entry_bias), ('s...]
    unnamed x2 -> x0, blocking collectives: 9.83 us -> none
    pallas_call x0 -> x6, Pallas kernels: none -> 7.76 us  [the longest x5 6.24 us: call(): pl.pallas_call(kernel, out_shape=outs, in_specs=[(specs or {}).get(i, VME...]
    ppermute x4 -> x9, starting transfers between devices: 5.34 us -> 12.7 us  [the longest x6 10.9 us: swap(): return lax.ppermute(array, ('seq', 'tp'), pairs)]
  transfers between devices with their start and end apart: 7 -> 9, of which waited for: 3 -> 4; matrix products, arithmetic and copies ran while one was open for 12% -> 0% of each run, Pallas kernels for 0% -> 13%
where the time goes in v1:
time: 28.7 us; the launch traced here: 28.5 us
  starting transfers between devices  12.7 us (44%)
  Pallas kernels  7.76 us (27%)
  waiting for transfers between devices  7.06 us (25%)
  between operations  0.85 us (3%)
    ppermute x6, starting transfers between devices, swap(): return lax.ppermute(array, ('seq', 'tp'), pairs)  10.9 us
    pallas_call x5, Pallas kernels, call(): pl.pallas_call(kernel, out_shape=outs, in_specs=[(specs or {}).get(i, VME...  6.24 us
    ppermute x6, waiting for transfers between devices, swap(): return lax.ppermute(array, ('seq', 'tp'), pairs)  5.28 us
    ppermute x3, starting transfers between devices, body(): lax.ppermute(params, 'dp', flip('dp', k * reach))  1.86 us
    ppermute x3, waiting for transfers between devices, body(): lax.ppermute(params, 'dp', flip('dp', k * reach))  1.78 us
    pallas_call x1, Pallas kernels, body(): pl.pallas_call(share_kernel, out_shape=(shape((head_dim, rows), BF16), sh...  1.52 us
  transfers between devices with their start and end apart: 9, of which 4 were waited for; matrix products, arithmetic and copies ran while one was open for 0% of the time, Pallas kernels for 13%

profile of v1, /device:TPU:0, one launch (start us, length us, event | category | flops | bytes accessed | tf_op | source)
XLA Modules:
  0.0 28.5 jit_solution(9754200837224805673)
XLA Ops:
  0.6 0.0 copy-start.1
  0.7 0.0 copy-start.2
  0.7 0.0 copy-start.3
  0.7 1.5 %shard_map.187 = (bf16[128,128]{1,0:T(8,128)(2,1)S(1)}, bf16[1,784,128]{2,1,0:T(8,128)(2,1)S(1)}) custom-call(f32[1,8,128]{2,1,0:T(8,128)} %refs_0_.2, f32[8]{0:T(128)} %refs_1_.2, f32[8]{0:T(128)} %refs_2_.2, bf16[1,128,512]{2,1,0:T(8,128)(2,1)} %refs_3_.1, bf16[1,128,512]{2,1,0:T(8,128)(2,1)} %refs_4_.1, bf16[1,128,128]{2,1,0:T(8,128)(2,1)} %refs_2_.3, ...), custom_call_target="tpu_custom_call" | custom-call | tf_op jit(solution)/shard_map/pallas_call | solution.py:485
  2.2 0.0 copy-start.5
  2.2 0.0 copy-start.6
  2.2 0.0 copy-start.7
  2.2 0.0 copy-start.8
  2.3 3.0 %collective-permute-start.2 = (bf16[784,128]{1,0:T(8,128)(2,1)S(1)}, bf16[784,128]{1,0:T(8,128)(2,1)S(1)}, u32[]{:S(2)}, u32[]{:S(2)}) collective-permute-start(bf16[784,128]{1,0:T(8,128)(2,1)S(1)} %bitcast.8), channel_id=1, source_target_pairs={{0,16},{4,20},{8,24},{12,28},{16,0},{20,4},{24,8},{28,12},{1,17},{... | collective-permute-start | bytes 602120 | tf_op jit(solution)/shard_map/ppermute | solution.py:448
  5.3 3.5 %collective-permute-start.1 = (bf16[128,128]{1,0:T(8,128)(2,1)S(1)}, bf16[128,128]{1,0:T(8,128)(2,1)S(1)}, u32[]{:S(2)}, u32[]{:S(2)}) collective-permute-start(bf16[128,128]{1,0:T(8,128)(2,1)S(1)} %get-tuple-element.50.refs_13_), channel_id=1, source_target_pairs={{0,20},{4,16},{8,28},{12,24},{1,21},{5,17},{9,29},{13,25},{2,22},{... | collective-permute-start | bytes 98312 | tf_op jit(solution)/shard_map/ppermute | solution.py:448
  8.8 0.1 collective-permute-start
  9.0 1.4 %shard_map.186 = (f32[128,512]{1,0:T(8,128)S(1)}, f32[128,512]{1,0:T(8,128)S(1)}, f32[128,512]{1,0:T(8,128)S(1)}, f32[128,512]{1,0:T(8,128)S(1)}, f32[128,512]{1...) custom-call(bf16[1,128,512]{2,1,0:T(8,128)(2,1)S(1)} %copy-done.1, ...), custom_call_target="tpu_custom_call" | custom-call | tf_op jit(solution)/shard_map/pallas_call | solution.py:429
  10.4 0.0 collective-permute-done.1.refs_12_
  10.4 2.4 %collective-permute-done.refs_3_ = bf16[128,128]{1,0:T(8,128)(2,1)S(1)} collective-permute-done((bf16[128,128]{1,0:T(8,128)(2,1)S(1)}, bf16[128,128]{1,0:T(8,128)(2,1)S(1)}, u32[]{:S(2)}, u32[]{:S(2)}) %collective-permute-start) | collective-permute-done | bytes 32800 | tf_op jit(solution)/shard_map/ppermute | solution.py:448
  12.8 0.0 collective-permute-done.2.refs_14_
  12.8 0.0 copy-done
  12.8 1.9 %shard_map.188 = (bf16[2,128,128]{2,1,0:T(8,128)(2,1)S(1)}, bf16[512,128]{1,0:T(8,128)(2,1)S(1)}, bf16[512,256]{1,0:T(8,128)(2,1)S(1)}, bf16[128,256]{1,0:T(8,12...) custom-call(bf16[1,128,512]{2,1,0:T(8,128)(2,1)S(1)} %copy-done, ...), custom_call_target="tpu_custom_call" | custom-call | tf_op jit(solution)/shard_map/pallas_call | solution.py:429
  14.7 0.3 %collective-permute-start.3 = (bf16[512,128]{1,0:T(8,128)(2,1)S(1)}, bf16[512,128]{1,0:T(8,128)(2,1)S(1)}, u32[]{:S(2)}, u32[]{:S(2)}) collective-permute-start(bf16[512,128]{1,0:T(8,128)(2,1)S(1)} %get-tuple-element.64), channel_id=1, source_target_pairs={{0,4},{4,0},{8,12},{12,8},{16,20},{20,16},{24,28},{28,24},{1,5},{5... | collective-permute-start | bytes 393224 | tf_op jit(solution)/shard_map/ppermute | solution.py:448
  15.1 1.2 %shard_map.189 = (f32[1,8,128]{2,1,0:T(8,128)}, f32[8,128]{1,0:T(8,128)S(1)}) custom-call(bf16[640,512]{1,0:T(8,128)(2,1)S(1)} %get-tuple-element.65.products, bf16[128,512]{1,0:T(8,128)(2,1)S(1)} %get-tuple-element.60.scaled.refs_1_, bf16[1024,128]{1,0:T(8,128)(2,1)S(1)} %get-tuple-element.57.refs_10_.halves, f32[1024,128]{1,0:T(8,128)S(1)} %get-tuple-element.66.back, ...), custom_call_target="tpu_custom_call" | custom-call | tf_op jit(solution)/shard_map/pallas_call | solution.py:429
  16.3 0.0 collective-permute-start.6
  16.3 1.7 %collective-permute-start.5 = (f32[8,128]{1,0:T(8,128)S(1)}, f32[8,128]{1,0:T(8,128)S(1)}, u32[]{:S(2)}, u32[]{:S(2)}) collective-permute-start(f32[8,128]{1,0:T(8,128)S(1)} %get-tuple-element.74), channel_id=1, source_target_pairs={{0,2},{1,3},{2,0},{3,1},{4,6},{5,7},{6,4},{7,5},{8,10},{9,11},{10,... | collective-permute-start | bytes 12296 | tf_op jit(solution)/shard_map/ppermute | solution.py:557
  18.0 0.2 collective-permute-start.4
  18.2 1.2 %collective-permute-done.6 = f32[8,128]{1,0:T(8,128)S(1)} collective-permute-done((f32[8,128]{1,0:T(8,128)S(1)}, f32[8,128]{1,0:T(8,128)S(1)}, u32[]{:S(2)}, u32[]{:S(2)}) %collective-permute-start.6) | collective-permute-done | bytes 4128 | tf_op jit(solution)/shard_map/ppermute | solution.py:557
  19.3 0.6 %collective-permute-done.5 = f32[8,128]{1,0:T(8,128)S(1)} collective-permute-done((f32[8,128]{1,0:T(8,128)S(1)}, f32[8,128]{1,0:T(8,128)S(1)}, u32[]{:S(2)}, u32[]{:S(2)}) %collective-permute-start.5) | collective-permute-done | bytes 4128 | tf_op jit(solution)/shard_map/ppermute | solution.py:557
  20.0 0.0 collective-permute-done.4
  20.0 0.0 collective-permute-done.3.refs_2_
  20.1 1.3 %collective-permute-start.7 = (bf16[144,128]{1,0:T(8,128)(2,1)S(1)}, bf16[144,128]{1,0:T(8,128)(2,1)S(1)}, u32[]{:S(2)}, u32[]{:S(2)}) collective-permute-start(bf16[144,128]{1,0:T(8,128)(2,1)S(1)} %pad_maximum_fusion), channel_id=1, source_target_pairs={{0,16},{4,20},{8,24},{12,28},{16,0},{20,4},{24,8},{28,12},{1,17},{... | collective-permute-start | bytes 110600 | tf_op jit(solution)/shard_map/ppermute | solution.py:448
  21.3 2.6 %collective-permute-start.8 = (bf16[256,128]{1,0:T(8,128)(2,1)S(1)}, bf16[256,128]{1,0:T(8,128)(2,1)S(1)}, u32[]{:S(2)}, u32[]{:S(2)}) collective-permute-start(bf16[256,128]{1,0:T(8,128)(2,1)S(1)} %add_convert_fusion.refs_4_), channel_id=1, source_target_pairs={{0,8},{4,12},{8,0},{12,4},{16,24},{20,28},{24,16},{28,20},{1,9},{5... | collective-permute-start | bytes 196616 | tf_op jit(solution)/shard_map/ppermute | solution.py:448
  23.9 1.0 %shard_map.190 = (f32[1,128,512]{2,1,0:T(8,128)}, f32[1,128,512]{2,1,0:T(8,128)}) custom-call(bf16[128,1024]{1,0:T(8,128)(2,1)S(1)} %get-tuple-element.49.refs_0_, bf16[128,512]{1,0:T(8,128)(2,1)S(1)} %get-tuple-element.60.scaled.refs_1_, f32[128,512]{1,0:T(8,128)S(1)} %get-tuple-element.61.refs_2_, f32[128,512]{1,0:T(8,128)S(1)} %get-tuple-element.62.refs_3_, ...), custom_call_target="tpu_custom_call" | custom-call | tf_op jit(solution)/shard_map/pallas_call | solution.py:429
  25.0 0.0 collective-permute-done.7.refs_0_
  25.0 2.8 %collective-permute-done.8.refs_5_ = bf16[256,128]{1,0:T(8,128)(2,1)S(1)} collective-permute-done((bf16[256,128]{1,0:T(8,128)(2,1)S(1)}, bf16[256,128]{1,0:T(8,128)(2,1)S(1)}, u32[]{:S(2)}, u32[]{:S(2)}) %collective-permute-start.8) | collective-permute-done | bytes 65568 | tf_op jit(solution)/shard_map/ppermute | solution.py:448
  27.8 0.7 %shard_map.191 = (f32[1,64,128]{2,1,0:T(8,128)}, f32[1,64,128]{2,1,0:T(8,128)}, f32[1,128,128]{2,1,0:T(8,128)}, f32[1,128,128]{2,1,0:T(8,128)}, f32[8]{0:T(128)}, /*index=5*/f32[8]{0:T(128)}, f32[8]{0:T(128)}) custom-call(bf16[144,128]{1,0:T(8,128)(2,1)S(1)} %collective-permute-done.7.refs_0_, bf16[2,128,128]{2,1,0:T(8,128)(2,1)S(1)} %get-tuple-element.73.refs_1_, ...), custom_call_target="tpu_custom_call" | custom-call | tf_op jit(solution)/shard_map/pallas_call | solution.py:429
  (16 shorter events, 0.1 us)
Async XLA Ops:
  0.6 8.3 %copy-start.1 = (bf16[1,128,512]{2,1,0:T(8,128)(2,1)S(1)}, bf16[1,128,512]{2,1,0:T(8,128)(2,1)}, u32[]{:S(2)}) copy-start(bf16[1,128,512]{2,1,0:T(8,128)(2,1)} %refs_3_.1) | copy-start | bytes 393220
  0.7 8.3 %copy-start.2 = (bf16[1,128,512]{2,1,0:T(8,128)(2,1)S(1)}, bf16[1,128,512]{2,1,0:T(8,128)(2,1)}, u32[]{:S(2)}) copy-start(bf16[1,128,512]{2,1,0:T(8,128)(2,1)} %refs_4_.1) | copy-start | bytes 393220
  0.7 8.3 %copy-start.3 = (bf16[1,128,128]{2,1,0:T(8,128)(2,1)S(1)}, bf16[1,128,128]{2,1,0:T(8,128)(2,1)}, u32[]{:S(2)}) copy-start(bf16[1,128,128]{2,1,0:T(8,128)(2,1)} %refs_1_.3) | copy-start | bytes 98308
  0.7 8.3 %copy-start.4 = (bf16[1,128,128]{2,1,0:T(8,128)(2,1)S(1)}, bf16[1,128,128]{2,1,0:T(8,128)(2,1)}, u32[]{:S(2)}) copy-start(bf16[1,128,128]{2,1,0:T(8,128)(2,1)} %refs_2_.3) | copy-start | bytes 98308
  2.2 6.8 %copy-start.5 = (f32[1,8,128]{2,1,0:T(8,128)S(1)}, f32[1,8,128]{2,1,0:T(8,128)}, u32[]{:S(2)}) copy-start(f32[1,8,128]{2,1,0:T(8,128)} %refs_0_.2) | copy-start | bytes 12292
  2.2 6.8 %copy-start.6 = (f32[8]{0:T(128)S(1)}, f32[8]{0:T(128)}, u32[]{:S(2)}) copy-start(f32[8]{0:T(128)} %refs_1_.2) | copy-start | bytes 100
  2.2 6.7 %copy-start.7 = (f32[8]{0:T(128)S(1)}, f32[8]{0:T(128)}, u32[]{:S(2)}) copy-start(f32[8]{0:T(128)} %refs_2_.2) | copy-start | bytes 100
  2.2 6.7 %copy-start.8 = (f32[8]{0:T(128)S(1)}, f32[8]{0:T(128)}, u32[]{:S(2)}) copy-start(f32[8]{0:T(128)} %skip.1) | copy-start | bytes 100
  2.3 10.6 %collective-permute-start.2 = (bf16[784,128]{1,0:T(8,128)(2,1)S(1)}, bf16[784,128]{1,0:T(8,128)(2,1)S(1)}, u32[]{:S(2)}, u32[]{:S(2)}) collective-permute-start(bf16[784,128]{1,0:T(8,128)(2,1)S(1)} %bitcast.8), channel_id=1, source_target_pairs={{0,16},{4,20},{8,24},{12,28},{16,0},{20,4},{24,8},{28,12},{1,17},{... | collective-permute-start | bytes 602120 | tf_op jit(solution)/shard_map/ppermute | solution.py:448
  5.3 7.5 %copy-start = (bf16[1,128,512]{2,1,0:T(8,128)(2,1)S(1)}, bf16[1,128,512]{2,1,0:T(8,128)(2,1)}, u32[]{:S(2)}) copy-start(bf16[1,128,512]{2,1,0:T(8,128)(2,1)} %refs_0_.3) | copy-start | bytes 393220
  5.3 5.1 %collective-permute-start.1 = (bf16[128,128]{1,0:T(8,128)(2,1)S(1)}, bf16[128,128]{1,0:T(8,128)(2,1)S(1)}, u32[]{:S(2)}, u32[]{:S(2)}) collective-permute-start(bf16[128,128]{1,0:T(8,128)(2,1)S(1)} %get-tuple-element.50.refs_13_), channel_id=1, source_target_pairs={{0,20},{4,16},{8,28},{12,24},{1,21},{5,17},{9,29},{13,25},{2,22},{... | collective-permute-start | bytes 98312 | tf_op jit(solution)/shard_map/ppermute | solution.py:448
  8.8 4.0 %collective-permute-start = (bf16[128,128]{1,0:T(8,128)(2,1)S(1)}, bf16[128,128]{1,0:T(8,128)(2,1)S(1)}, u32[]{:S(2)}, u32[]{:S(2)}) collective-permute-start(bf16[128,128]{1,0:T(8,128)(2,1)S(1)} %get-tuple-element.50.refs_13_), channel_id=1, source_target_pairs={{0,4},{4,0},{8,12},{12,8},{16,20},{20,16},{24,28},{28,24},{1,5},{5... | collective-permute-start | bytes 98312 | tf_op jit(solution)/shard_map/ppermute | solution.py:448
  14.7 5.2 %collective-permute-start.3 = (bf16[512,128]{1,0:T(8,128)(2,1)S(1)}, bf16[512,128]{1,0:T(8,128)(2,1)S(1)}, u32[]{:S(2)}, u32[]{:S(2)}) collective-permute-start(bf16[512,128]{1,0:T(8,128)(2,1)S(1)} %get-tuple-element.64), channel_id=1, source_target_pairs={{0,4},{4,0},{8,12},{12,8},{16,20},{20,16},{24,28},{28,24},{1,5},{5... | collective-permute-start | bytes 393224 | tf_op jit(solution)/shard_map/ppermute | solution.py:448
  16.3 3.0 %collective-permute-start.6 = (f32[8,128]{1,0:T(8,128)S(1)}, f32[8,128]{1,0:T(8,128)S(1)}, u32[]{:S(2)}, u32[]{:S(2)}) collective-permute-start(f32[8,128]{1,0:T(8,128)S(1)} %get-tuple-element.74), channel_id=1, source_target_pairs={{0,3},{1,2},{2,1},{3,0},{4,7},{5,6},{6,5},{7,4},{8,11},{9,10},{10,... | collective-permute-start | bytes 12296 | tf_op jit(solution)/shard_map/ppermute | solution.py:557
  16.3 3.6 %collective-permute-start.5 = (f32[8,128]{1,0:T(8,128)S(1)}, f32[8,128]{1,0:T(8,128)S(1)}, u32[]{:S(2)}, u32[]{:S(2)}) collective-permute-start(f32[8,128]{1,0:T(8,128)S(1)} %get-tuple-element.74), channel_id=1, source_target_pairs={{0,2},{1,3},{2,0},{3,1},{4,6},{5,7},{6,4},{7,5},{8,10},{9,11},{10,... | collective-permute-start | bytes 12296 | tf_op jit(solution)/shard_map/ppermute | solution.py:557
  18.0 1.9 %collective-permute-start.4 = (f32[8,128]{1,0:T(8,128)S(1)}, f32[8,128]{1,0:T(8,128)S(1)}, u32[]{:S(2)}, u32[]{:S(2)}) collective-permute-start(f32[8,128]{1,0:T(8,128)S(1)} %get-tuple-element.74), channel_id=1, source_target_pairs={{0,1},{1,0},{2,3},{3,2},{4,5},{5,4},{6,7},{7,6},{8,9},{9,8},{10,11... | collective-permute-start | bytes 12296 | tf_op jit(solution)/shard_map/ppermute | solution.py:557
  20.1 4.9 %collective-permute-start.7 = (bf16[144,128]{1,0:T(8,128)(2,1)S(1)}, bf16[144,128]{1,0:T(8,128)(2,1)S(1)}, u32[]{:S(2)}, u32[]{:S(2)}) collective-permute-start(bf16[144,128]{1,0:T(8,128)(2,1)S(1)} %pad_maximum_fusion), channel_id=1, source_target_pairs={{0,16},{4,20},{8,24},{12,28},{16,0},{20,4},{24,8},{28,12},{1,17},{... | collective-permute-start | bytes 110600 | tf_op jit(solution)/shard_map/ppermute | solution.py:448
  21.3 6.5 %collective-permute-start.8 = (bf16[256,128]{1,0:T(8,128)(2,1)S(1)}, bf16[256,128]{1,0:T(8,128)(2,1)S(1)}, u32[]{:S(2)}, u32[]{:S(2)}) collective-permute-start(bf16[256,128]{1,0:T(8,128)(2,1)S(1)} %add_convert_fusion.refs_4_), channel_id=1, source_target_pairs={{0,8},{4,12},{8,0},{12,4},{16,24},{20,28},{24,16},{28,20},{1,9},{5... | collective-permute-start | bytes 196616 | tf_op jit(solution)/shard_map/ppermute | solution.py:448

commit v2 on v1

--- a/solution.py
+++ b/solution.py
@@ -381,18 +381,22 @@
     grad_query[0] = unstack(dot(scores[...], keys[...], NT) * scale, rows)
 
 
+def vectors_kernel(mine, other, grad_write, grad_read):
+    rows = grad_write.shape[1]
+    both = mine[...].astype(F32) + other[...].astype(F32)
+    grad_write[0] = both[:rows]
+    grad_read[0] = both[rows:]
+
+
 def finish_kernel(count, *refs):
-    arrived, (mine, other, tail, shared, got) = refs[:count], refs[count : count + 5]
-    grad_key, grad_value, grad_write, grad_read, grad_alog, grad_skip, grad_bias = refs[count + 5 :]
+    arrived, (mine, other, tail) = refs[:count], refs[count : count + 3]
+    grad_key, grad_value, grad_alog, grad_skip, grad_bias = refs[count + 3 :]
     half, rows = grad_key.shape[1:]
     total = mine[0].astype(F32) + other[: 2 * half].astype(F32)
     for term in arrived:
         total = total + term[: 2 * half].astype(F32)
     grad_key[0] = total[:half]
     grad_value[0] = total[half:]
-    both = shared[...].astype(F32) + got[...].astype(F32)
-    grad_write[0] = both[:rows]
-    grad_read[0] = both[rows:]
     heads = grad_alog.shape[0]
     params = joined(tail[...]) + joined(arrived[-1][2 * half :])
     grad_alog[...] = params[0, :heads]
@@ -552,10 +556,16 @@
         (shape((1, heads, rows), F32), shape((8, states), F32)),
         (products, scaled, halves, back, tables),
     )
+    shared, got_shared = other[slots * head_dim :], got[slots * head_dim :]
+    reach = 2
+    while reach < lax.axis_size("tp"):
+        shared = (shared.astype(F32) + got_shared.astype(F32)).astype(BF16)
+        got_shared = swap(shared, 0, reach)
+        reach *= 2
     reach = 1
     while reach < lax.axis_size("dp"):
         near = [params] + [lax.ppermute(params, "dp", flip("dp", k * reach)) for k in (1, 2, 3)]
-        got, *near = lax.optimization_barrier((got, *near))
+        shared, *near = lax.optimization_barrier((shared, *near))
         params = (near[0] + near[1]) + (near[2] + near[3])
         reach *= 4
     sent = [
@@ -570,12 +580,6 @@
         slot *= 2
         if slot < slots:
             params = joined(tail) + joined(arrived[-1][head_dim:])
-    shared, got_shared = other[slots * head_dim :], got[slots * head_dim :]
-    reach = 2
-    while reach < lax.axis_size("tp"):
-        shared = (shared.astype(F32) + got_shared.astype(F32)).astype(BF16)
-        got_shared = swap(shared, 0, reach)
-        reach *= 2
     scores, shared = lax.optimization_barrier((scores, shared))
     grad_gate, grad_query = call(
         lambda *refs: output_kernel(scale, *refs),
@@ -585,10 +589,12 @@
     vector = shape((heads,), F32)
     half = shape((1, head_dim // 2, rows), F32)
     full = shape((1, rows, states), F32)
-    grad_key, grad_value, grad_write, grad_read, grad_alog, grad_skip, grad_bias = call(
+    grad_write, grad_read = call(vectors_kernel, (full, full), (shared, got_shared))
+    grad_write, *arrived = lax.optimization_barrier((grad_write, *arrived))
+    grad_key, grad_value, grad_alog, grad_skip, grad_bias = call(
         lambda *refs: finish_kernel(len(arrived), *refs),
-        (half, half, full, full, vector, vector, vector),
-        (*arrived, mine, got, tail, shared, got_shared),
+        (half, half, vector, vector, vector),
+        (*arrived, mine, got, tail),
     )
     grad_key, grad_value = grad_key.swapaxes(1, 2), grad_value.swapaxes(1, 2)
     return (

time: 28.7 us -> 27.4 us (0.955)
  starting transfers between devices: 12.7 us -> 11.7 us
  waiting for transfers between devices: 7.06 us -> 6.16 us
  Pallas kernels: 7.76 us -> 8.37 us
    ppermute x3, waiting for transfers between devices: 1.78 us -> 0.01 us  [body(): lax.ppermute(params, 'dp', flip('dp', k * reach))]
    ppermute x6, starting transfers between devices: 10.9 us -> 9.85 us  [swap(): return lax.ppermute(array, ('seq', 'tp'), pairs)]
    ppermute x6, waiting for transfers between devices: 5.28 us -> 6.15 us  [swap(): return lax.ppermute(array, ('seq', 'tp'), pairs)]
    pallas_call x5 -> x6, Pallas kernels: 6.24 us -> 6.85 us  [call(): pl.pallas_call(kernel, out_shape=outs, in_specs=[(specs or {}).get(i, VME...]
  transfers between devices with their start and end apart: 9 -> 9, of which waited for: 4 -> 4; matrix products, arithmetic and copies ran while one was open for 0% -> 0% of each run, Pallas kernels for 13% -> 16%
where the time goes in v2:
time: 27.4 us; the launch traced here: 27.2 us
  starting transfers between devices  11.7 us (43%)
  Pallas kernels  8.37 us (31%)
  waiting for transfers between devices  6.16 us (22%)
  between operations  0.86 us (3%)
    ppermute x6, starting transfers between devices, swap(): return lax.ppermute(array, ('seq', 'tp'), pairs)  9.85 us
    pallas_call x6, Pallas kernels, call(): pl.pallas_call(kernel, out_shape=outs, in_specs=[(specs or {}).get(i, VME...  6.85 us
    ppermute x6, waiting for transfers between devices, swap(): return lax.ppermute(array, ('seq', 'tp'), pairs)  6.15 us
    ppermute x3, starting transfers between devices, body(): lax.ppermute(params, 'dp', flip('dp', k * reach))  1.86 us
    pallas_call x1, Pallas kernels, body(): pl.pallas_call(share_kernel, out_shape=(shape((head_dim, rows), BF16), sh...  1.52 us
  transfers between devices with their start and end apart: 9, of which 4 were waited for; matrix products, arithmetic and copies ran while one was open for 0% of the time, Pallas kernels for 16%

profile of v2, /device:TPU:0, one launch (start us, length us, event | category | flops | bytes accessed | tf_op | source)
XLA Modules:
  0.0 27.2 jit_solution(15074705592008549926)
XLA Ops:
  0.6 0.0 copy-start.1
  0.7 0.0 copy-start.2
  0.7 0.0 copy-start.3
  0.7 1.5 %shard_map.187 = (bf16[128,128]{1,0:T(8,128)(2,1)S(1)}, bf16[1,784,128]{2,1,0:T(8,128)(2,1)S(1)}) custom-call(f32[1,8,128]{2,1,0:T(8,128)} %refs_0_.2, f32[8]{0:T(128)} %refs_1_.2, f32[8]{0:T(128)} %refs_2_.2, bf16[1,128,512]{2,1,0:T(8,128)(2,1)} %refs_3_.1, bf16[1,128,512]{2,1,0:T(8,128)(2,1)} %refs_4_.1, bf16[1,128,128]{2,1,0:T(8,128)(2,1)} %refs_2_.3, ...), custom_call_target="tpu_custom_call" | custom-call | tf_op jit(solution)/shard_map/pallas_call | solution.py:489
  2.2 0.0 copy-start.5
  2.2 0.0 copy-start.6
  2.2 0.0 copy-start.7
  2.2 0.0 copy-start.8
  2.3 3.0 %collective-permute-start.2 = (bf16[784,128]{1,0:T(8,128)(2,1)S(1)}, bf16[784,128]{1,0:T(8,128)(2,1)S(1)}, u32[]{:S(2)}, u32[]{:S(2)}) collective-permute-start(bf16[784,128]{1,0:T(8,128)(2,1)S(1)} %bitcast.8), channel_id=1, source_target_pairs={{0,16},{4,20},{8,24},{12,28},{16,0},{20,4},{24,8},{28,12},{1,17},{... | collective-permute-start | bytes 602120 | tf_op jit(solution)/shard_map/ppermute | solution.py:452
  5.3 3.5 %collective-permute-start.1 = (bf16[128,128]{1,0:T(8,128)(2,1)S(1)}, bf16[128,128]{1,0:T(8,128)(2,1)S(1)}, u32[]{:S(2)}, u32[]{:S(2)}) collective-permute-start(bf16[128,128]{1,0:T(8,128)(2,1)S(1)} %get-tuple-element.52.refs_13_), channel_id=1, source_target_pairs={{0,20},{4,16},{8,28},{12,24},{1,21},{5,17},{9,29},{13,25},{2,22},{... | collective-permute-start | bytes 98312 | tf_op jit(solution)/shard_map/ppermute | solution.py:452
  8.8 0.1 collective-permute-start
  9.0 1.4 %shard_map.186 = (f32[128,512]{1,0:T(8,128)S(1)}, f32[128,512]{1,0:T(8,128)S(1)}, f32[128,512]{1,0:T(8,128)S(1)}, f32[128,512]{1,0:T(8,128)S(1)}, f32[128,512]{1...) custom-call(bf16[1,128,512]{2,1,0:T(8,128)(2,1)S(1)} %copy-done.1, ...), custom_call_target="tpu_custom_call" | custom-call | tf_op jit(solution)/shard_map/pallas_call | solution.py:433
  10.4 0.0 collective-permute-done.1.refs_12_
  10.4 2.4 %collective-permute-done.refs_3_ = bf16[128,128]{1,0:T(8,128)(2,1)S(1)} collective-permute-done((bf16[128,128]{1,0:T(8,128)(2,1)S(1)}, bf16[128,128]{1,0:T(8,128)(2,1)S(1)}, u32[]{:S(2)}, u32[]{:S(2)}) %collective-permute-start) | collective-permute-done | bytes 32800 | tf_op jit(solution)/shard_map/ppermute | solution.py:452
  12.8 0.0 collective-permute-done.2.refs_14_
  12.8 1.9 %shard_map.188 = (bf16[2,128,128]{2,1,0:T(8,128)(2,1)S(1)}, bf16[512,128]{1,0:T(8,128)(2,1)S(1)}, bf16[512,256]{1,0:T(8,128)(2,1)S(1)}, bf16[128,256]{1,0:T(8,12...) custom-call(bf16[1,128,512]{2,1,0:T(8,128)(2,1)S(1)} %copy-done, ...), custom_call_target="tpu_custom_call" | custom-call | tf_op jit(solution)/shard_map/pallas_call | solution.py:433
  14.7 0.3 %collective-permute-start.3 = (bf16[512,128]{1,0:T(8,128)(2,1)S(1)}, bf16[512,128]{1,0:T(8,128)(2,1)S(1)}, u32[]{:S(2)}, u32[]{:S(2)}) collective-permute-start(bf16[512,128]{1,0:T(8,128)(2,1)S(1)} %get-tuple-element.66), channel_id=1, source_target_pairs={{0,4},{4,0},{8,12},{12,8},{16,20},{20,16},{24,28},{28,24},{1,5},{5... | collective-permute-start | bytes 393224 | tf_op jit(solution)/shard_map/ppermute | solution.py:452
  15.1 1.2 %shard_map.189 = (f32[1,8,128]{2,1,0:T(8,128)}, f32[8,128]{1,0:T(8,128)S(1)}) custom-call(bf16[640,512]{1,0:T(8,128)(2,1)S(1)} %get-tuple-element.67.products, bf16[128,512]{1,0:T(8,128)(2,1)S(1)} %get-tuple-element.62.scaled.refs_1_, bf16[1024,128]{1,0:T(8,128)(2,1)S(1)} %get-tuple-element.59.refs_10_.halves, f32[1024,128]{1,0:T(8,128)S(1)} %get-tuple-element.68.back, ...), custom_call_target="tpu_custom_call" | custom-call | tf_op jit(solution)/shard_map/pallas_call | solution.py:433
  16.3 0.0 collective-permute-start.6
  16.3 1.7 %collective-permute-start.5 = (f32[8,128]{1,0:T(8,128)S(1)}, f32[8,128]{1,0:T(8,128)S(1)}, u32[]{:S(2)}, u32[]{:S(2)}) collective-permute-start(f32[8,128]{1,0:T(8,128)S(1)} %get-tuple-element.78), channel_id=1, source_target_pairs={{0,2},{1,3},{2,0},{3,1},{4,6},{5,7},{6,4},{7,5},{8,10},{9,11},{10,... | collective-permute-start | bytes 12296 | tf_op jit(solution)/shard_map/ppermute | solution.py:567
  18.0 0.2 collective-permute-start.4
  18.2 1.6 %collective-permute-done.3.refs_2_ = bf16[512,128]{1,0:T(8,128)(2,1)S(1)} collective-permute-done((bf16[512,128]{1,0:T(8,128)(2,1)S(1)}, bf16[512,128]{1,0:T(8,128)(2,1)S(1)}, u32[]{:S(2)}, u32[]{:S(2)}) %collective-permute-start.3) | collective-permute-done | bytes 131104 | tf_op jit(solution)/shard_map/ppermute | solution.py:452
  19.8 2.7 %collective-permute-start.7 = (bf16[256,128]{1,0:T(8,128)(2,1)S(1)}, bf16[256,128]{1,0:T(8,128)(2,1)S(1)}, u32[]{:S(2)}, u32[]{:S(2)}) collective-permute-start(bf16[256,128]{1,0:T(8,128)(2,1)S(1)} %add_convert_fusion.mine), channel_id=1, source_target_pairs={{0,8},{4,12},{8,0},{12,4},{16,24},{20,28},{24,16},{28,20},{1,9},{5... | collective-permute-start | bytes 196616 | tf_op jit(solution)/shard_map/ppermute | solution.py:452
  22.5 0.0 collective-permute-done.6
  22.5 0.0 collective-permute-done.5
  22.5 0.0 collective-permute-done.4
  22.5 0.2 collective-permute-start.8
  22.7 1.0 %shard_map.190 = (f32[1,128,512]{2,1,0:T(8,128)}, f32[1,128,512]{2,1,0:T(8,128)}) custom-call(bf16[128,1024]{1,0:T(8,128)(2,1)S(1)} %get-tuple-element.51.refs_0_, bf16[128,512]{1,0:T(8,128)(2,1)S(1)} %get-tuple-element.62.scaled.refs_1_, f32[128,512]{1,0:T(8,128)S(1)} %get-tuple-element.63.refs_2_, f32[128,512]{1,0:T(8,128)S(1)} %get-tuple-element.64.refs_3_, ...), custom_call_target="tpu_custom_call" | custom-call | tf_op jit(solution)/shard_map/pallas_call | solution.py:433
  23.8 1.7 %collective-permute-done.7.other = bf16[256,128]{1,0:T(8,128)(2,1)S(1)} collective-permute-done((bf16[256,128]{1,0:T(8,128)(2,1)S(1)}, bf16[256,128]{1,0:T(8,128)(2,1)S(1)}, u32[]{:S(2)}, u32[]{:S(2)}) %collective-permute-start.7) | collective-permute-done | bytes 65568 | tf_op jit(solution)/shard_map/ppermute | solution.py:452
  25.4 0.7 %shard_map.191 = (f32[1,128,128]{2,1,0:T(8,128)}, f32[1,128,128]{2,1,0:T(8,128)}) custom-call(bf16[256,128]{1,0:T(8,128)(2,1)S(1)} %add_convert_fusion.mine, bf16[256,128]{1,0:T(8,128)(2,1)S(1)} %collective-permute-done.7.other), custom_call_target="tpu_custom_call" | custom-call | tf_op jit(solution)/shard_map/pallas_call | solution.py:433
  26.1 0.5 %collective-permute-done.8.refs_0_ = bf16[144,128]{1,0:T(8,128)(2,1)S(1)} collective-permute-done((bf16[144,128]{1,0:T(8,128)(2,1)S(1)}, bf16[144,128]{1,0:T(8,128)(2,1)S(1)}, u32[]{:S(2)}, u32[]{:S(2)}) %collective-permute-start.8) | collective-permute-done | bytes 36896 | tf_op jit(solution)/shard_map/ppermute | solution.py:452
  26.6 0.6 %shard_map.192 = (f32[1,64,128]{2,1,0:T(8,128)}, f32[1,64,128]{2,1,0:T(8,128)}, f32[8]{0:T(128)}, f32[8]{0:T(128)}, f32[8]{0:T(128)}) custom-call(bf16[144,128]{1,0:T(8,128)(2,1)S(1)} %collective-permute-done.8.refs_0_, bf16[2,128,128]{2,1,0:T(8,128)(2,1)S(1)} %get-tuple-element.77.refs_1_, bf16[512,128]{1,0:T(8,128)(2,1)S(1)} %collective-permute-done.3.refs_2_, ...), custom_call_target="tpu_custom_call" | custom-call | tf_op jit(solution)/shard_map/pallas_call | solution.py:433
  (17 shorter events, 0.1 us)
Async XLA Ops:
  0.6 8.3 %copy-start.1 = (bf16[1,128,512]{2,1,0:T(8,128)(2,1)S(1)}, bf16[1,128,512]{2,1,0:T(8,128)(2,1)}, u32[]{:S(2)}) copy-start(bf16[1,128,512]{2,1,0:T(8,128)(2,1)} %refs_3_.1) | copy-start | bytes 393220
  0.7 8.3 %copy-start.2 = (bf16[1,128,512]{2,1,0:T(8,128)(2,1)S(1)}, bf16[1,128,512]{2,1,0:T(8,128)(2,1)}, u32[]{:S(2)}) copy-start(bf16[1,128,512]{2,1,0:T(8,128)(2,1)} %refs_4_.1) | copy-start | bytes 393220
  0.7 8.3 %copy-start.3 = (bf16[1,128,128]{2,1,0:T(8,128)(2,1)S(1)}, bf16[1,128,128]{2,1,0:T(8,128)(2,1)}, u32[]{:S(2)}) copy-start(bf16[1,128,128]{2,1,0:T(8,128)(2,1)} %refs_1_.3) | copy-start | bytes 98308
  0.7 8.3 %copy-start.4 = (bf16[1,128,128]{2,1,0:T(8,128)(2,1)S(1)}, bf16[1,128,128]{2,1,0:T(8,128)(2,1)}, u32[]{:S(2)}) copy-start(bf16[1,128,128]{2,1,0:T(8,128)(2,1)} %refs_2_.3) | copy-start | bytes 98308
  2.2 6.8 %copy-start.5 = (f32[1,8,128]{2,1,0:T(8,128)S(1)}, f32[1,8,128]{2,1,0:T(8,128)}, u32[]{:S(2)}) copy-start(f32[1,8,128]{2,1,0:T(8,128)} %refs_0_.2) | copy-start | bytes 12292
  2.2 6.8 %copy-start.6 = (f32[8]{0:T(128)S(1)}, f32[8]{0:T(128)}, u32[]{:S(2)}) copy-start(f32[8]{0:T(128)} %refs_1_.2) | copy-start | bytes 100
  2.2 6.7 %copy-start.7 = (f32[8]{0:T(128)S(1)}, f32[8]{0:T(128)}, u32[]{:S(2)}) copy-start(f32[8]{0:T(128)} %refs_2_.2) | copy-start | bytes 100
  2.2 6.7 %copy-start.8 = (f32[8]{0:T(128)S(1)}, f32[8]{0:T(128)}, u32[]{:S(2)}) copy-start(f32[8]{0:T(128)} %skip.1) | copy-start | bytes 100
  2.3 10.6 %collective-permute-start.2 = (bf16[784,128]{1,0:T(8,128)(2,1)S(1)}, bf16[784,128]{1,0:T(8,128)(2,1)S(1)}, u32[]{:S(2)}, u32[]{:S(2)}) collective-permute-start(bf16[784,128]{1,0:T(8,128)(2,1)S(1)} %bitcast.8), channel_id=1, source_target_pairs={{0,16},{4,20},{8,24},{12,28},{16,0},{20,4},{24,8},{28,12},{1,17},{... | collective-permute-start | bytes 602120 | tf_op jit(solution)/shard_map/ppermute | solution.py:452
  5.3 7.5 %copy-start = (bf16[1,128,512]{2,1,0:T(8,128)(2,1)S(1)}, bf16[1,128,512]{2,1,0:T(8,128)(2,1)}, u32[]{:S(2)}) copy-start(bf16[1,128,512]{2,1,0:T(8,128)(2,1)} %refs_0_.3) | copy-start | bytes 393220
  5.3 5.1 %collective-permute-start.1 = (bf16[128,128]{1,0:T(8,128)(2,1)S(1)}, bf16[128,128]{1,0:T(8,128)(2,1)S(1)}, u32[]{:S(2)}, u32[]{:S(2)}) collective-permute-start(bf16[128,128]{1,0:T(8,128)(2,1)S(1)} %get-tuple-element.52.refs_13_), channel_id=1, source_target_pairs={{0,20},{4,16},{8,28},{12,24},{1,21},{5,17},{9,29},{13,25},{2,22},{... | collective-permute-start | bytes 98312 | tf_op jit(solution)/shard_map/ppermute | solution.py:452
  8.8 4.0 %collective-permute-start = (bf16[128,128]{1,0:T(8,128)(2,1)S(1)}, bf16[128,128]{1,0:T(8,128)(2,1)S(1)}, u32[]{:S(2)}, u32[]{:S(2)}) collective-permute-start(bf16[128,128]{1,0:T(8,128)(2,1)S(1)} %get-tuple-element.52.refs_13_), channel_id=1, source_target_pairs={{0,4},{4,0},{8,12},{12,8},{16,20},{20,16},{24,28},{28,24},{1,5},{5... | collective-permute-start | bytes 98312 | tf_op jit(solution)/shard_map/ppermute | solution.py:452
  14.7 5.0 %collective-permute-start.3 = (bf16[512,128]{1,0:T(8,128)(2,1)S(1)}, bf16[512,128]{1,0:T(8,128)(2,1)S(1)}, u32[]{:S(2)}, u32[]{:S(2)}) collective-permute-start(bf16[512,128]{1,0:T(8,128)(2,1)S(1)} %get-tuple-element.66), channel_id=1, source_target_pairs={{0,4},{4,0},{8,12},{12,8},{16,20},{20,16},{24,28},{28,24},{1,5},{5... | collective-permute-start | bytes 393224 | tf_op jit(solution)/shard_map/ppermute | solution.py:452
  16.3 6.1 %collective-permute-start.6 = (f32[8,128]{1,0:T(8,128)S(1)}, f32[8,128]{1,0:T(8,128)S(1)}, u32[]{:S(2)}, u32[]{:S(2)}) collective-permute-start(f32[8,128]{1,0:T(8,128)S(1)} %get-tuple-element.78), channel_id=1, source_target_pairs={{0,3},{1,2},{2,1},{3,0},{4,7},{5,6},{6,5},{7,4},{8,11},{9,10},{10,... | collective-permute-start | bytes 12296 | tf_op jit(solution)/shard_map/ppermute | solution.py:567
  16.3 6.1 %collective-permute-start.5 = (f32[8,128]{1,0:T(8,128)S(1)}, f32[8,128]{1,0:T(8,128)S(1)}, u32[]{:S(2)}, u32[]{:S(2)}) collective-permute-start(f32[8,128]{1,0:T(8,128)S(1)} %get-tuple-element.78), channel_id=1, source_target_pairs={{0,2},{1,3},{2,0},{3,1},{4,6},{5,7},{6,4},{7,5},{8,10},{9,11},{10,... | collective-permute-start | bytes 12296 | tf_op jit(solution)/shard_map/ppermute | solution.py:567
  18.0 4.4 %collective-permute-start.4 = (f32[8,128]{1,0:T(8,128)S(1)}, f32[8,128]{1,0:T(8,128)S(1)}, u32[]{:S(2)}, u32[]{:S(2)}) collective-permute-start(f32[8,128]{1,0:T(8,128)S(1)} %get-tuple-element.78), channel_id=1, source_target_pairs={{0,1},{1,0},{2,3},{3,2},{4,5},{5,4},{6,7},{7,6},{8,9},{9,8},{10,11... | collective-permute-start | bytes 12296 | tf_op jit(solution)/shard_map/ppermute | solution.py:567
  19.8 5.6 %collective-permute-start.7 = (bf16[256,128]{1,0:T(8,128)(2,1)S(1)}, bf16[256,128]{1,0:T(8,128)(2,1)S(1)}, u32[]{:S(2)}, u32[]{:S(2)}) collective-permute-start(bf16[256,128]{1,0:T(8,128)(2,1)S(1)} %add_convert_fusion.mine), channel_id=1, source_target_pairs={{0,8},{4,12},{8,0},{12,4},{16,24},{20,28},{24,16},{28,20},{1,9},{5... | collective-permute-start | bytes 196616 | tf_op jit(solution)/shard_map/ppermute | solution.py:452
  22.5 4.0 %collective-permute-start.8 = (bf16[144,128]{1,0:T(8,128)(2,1)S(1)}, bf16[144,128]{1,0:T(8,128)(2,1)S(1)}, u32[]{:S(2)}, u32[]{:S(2)}) collective-permute-start(bf16[144,128]{1,0:T(8,128)(2,1)S(1)} %pad_maximum_fusion), channel_id=1, source_target_pairs={{0,16},{4,20},{8,24},{12,28},{16,0},{20,4},{24,8},{28,12},{1,17},{... | collective-permute-start | bytes 110600 | tf_op jit(solution)/shard_map/ppermute | solution.py:452

commit v3 on v2

--- a/solution.py
+++ b/solution.py
@@ -91,13 +91,6 @@
     width = jobs[0][2].shape[0]
     shares = [1.0 / b[:, width:] for b in both]
     return [(b[:, :width] * share, w, share) for b, w, share in zip(both, weights, shares)]
-
-
-def _fold(join, parts):
-    out = parts[0]
-    for part in parts[1:]:
-        out = join(out, part)
-    return out
 
 
 def slot_mask(here, query_slot, slots, rows):
@@ -441,13 +434,12 @@
     )(*args)
 
 
-def swap(array, seq_bits, tp_bits, to_later=None):
+def swap(array, seq_bits, tp_bits):
     n_seq, n_tp = lax.axis_size("seq"), lax.axis_size("tp")
     pairs = [
         (s * n_tp + t, (s ^ seq_bits) * n_tp + (t ^ tp_bits))
         for s in range(n_seq)
         for t in range(n_tp)
-        if to_later is None or ((s ^ seq_bits) > s) == to_later
     ]
     return lax.ppermute(array, ("seq", "tp"), pairs)
 
@@ -503,7 +495,7 @@
     )(*[pltpu.with_memory_space_constraint(a, pltpu.HBM) for a in sources])
     messages = [swap(message[slot.bit_length() - 1], slot, 0) for slot in range(1, slots)]
     partner = swap(pack, 0, 1)
-    far = [swap(pack, slot, 1, True) for slot in range(1, slots)]
+    far = [swap(pack, slot, 1) for slot in range(1, slots)]
 
     wide_f, wide_b = shape((rows, wide), F32), shape((rows, wide), BF16)
     tall_f = shape((heads * rows, rows), F32)
@@ -572,7 +564,7 @@
         (mine[slot].astype(F32) + got[slot * head_dim : (slot + 1) * head_dim].astype(F32)).astype(BF16)
         for slot in range(1, slots)
     ]
-    arrived = [swap(sent[slot - 1], slot, 0, False) for slot in range(1, slots) if slot & (slot - 1)]
+    arrived = [swap(sent[slot - 1], slot, 0) for slot in range(1, slots) if slot & (slot - 1)]
     slot = 1
     while slot < slots:
         tail = split(params)

time: 27.4 us -> 25.7 us (0.938)
  waiting for transfers between devices: 6.16 us -> 3.49 us
  starting transfers between devices: 11.7 us -> 12.8 us
    ppermute x6, waiting for transfers between devices: 6.15 us -> 3.49 us  [swap(): return lax.ppermute(array, ('seq', 'tp'), pairs)]
    ppermute x6, starting transfers between devices: 9.85 us -> 10.9 us  [swap(): return lax.ppermute(array, ('seq', 'tp'), pairs)]
  transfers between devices with their start and end apart: 9 -> 9, of which waited for: 4 -> 6; matrix products, arithmetic and copies ran while one was open for 0% -> 0% of each run, Pallas kernels for 16% -> 17%
where the time goes in v3:
time: 25.7 us; the launch traced here: 25.6 us
  starting transfers between devices  12.8 us (50%)
  Pallas kernels  8.36 us (33%)
  waiting for transfers between devices  3.49 us (14%)
  between operations  0.81 us (3%)
    ppermute x6, starting transfers between devices, swap(): return lax.ppermute(array, ('seq', 'tp'), pairs)  10.9 us
    pallas_call x6, Pallas kernels, call(): pl.pallas_call(kernel, out_shape=outs, in_specs=[(specs or {}).get(i, VME...  6.84 us
    ppermute x6, waiting for transfers between devices, swap(): return lax.ppermute(array, ('seq', 'tp'), pairs)  3.49 us
    ppermute x3, starting transfers between devices, body(): lax.ppermute(params, 'dp', flip('dp', k * reach))  1.86 us
    pallas_call x1, Pallas kernels, body(): pl.pallas_call(share_kernel, out_shape=(shape((head_dim, rows), BF16), sh...  1.52 us
  transfers between devices with their start and end apart: 9, of which 6 were waited for; matrix products, arithmetic and copies ran while one was open for 0% of the time, Pallas kernels for 17%

profile of v3, /device:TPU:0, one launch (start us, length us, event | category | flops | bytes accessed | tf_op | source)
XLA Modules:
  0.0 25.6 jit_solution(3990257437035833755)
XLA Ops:
  0.6 0.0 copy-start.1
  0.7 1.5 %shard_map.187 = (bf16[128,128]{1,0:T(8,128)(2,1)S(1)}, bf16[1,784,128]{2,1,0:T(8,128)(2,1)S(1)}) custom-call(f32[1,8,128]{2,1,0:T(8,128)} %refs_0_.2, f32[8]{0:T(128)} %refs_1_.2, f32[8]{0:T(128)} %refs_2_.2, bf16[1,128,512]{2,1,0:T(8,128)(2,1)} %refs_3_.1, bf16[1,128,512]{2,1,0:T(8,128)(2,1)} %refs_4_.1, bf16[1,128,128]{2,1,0:T(8,128)(2,1)} %refs_2_.3, ...), custom_call_target="tpu_custom_call" | custom-call | tf_op jit(solution)/shard_map/pallas_call | solution.py:481
  2.2 0.0 copy-start.5
  2.2 0.0 copy-start.6
  2.2 0.0 copy-start.7
  2.2 0.0 copy-start.8
  2.3 3.0 %collective-permute-start.2 = (bf16[784,128]{1,0:T(8,128)(2,1)S(1)}, bf16[784,128]{1,0:T(8,128)(2,1)S(1)}, u32[]{:S(2)}, u32[]{:S(2)}) collective-permute-start(bf16[784,128]{1,0:T(8,128)(2,1)S(1)} %bitcast.8), channel_id=1, source_target_pairs={{0,16},{4,20},{8,24},{12,28},{16,0},{20,4},{24,8},{28,12},{1,17},{... | collective-permute-start | bytes 602120 | tf_op jit(solution)/shard_map/ppermute | solution.py:444
  5.3 1.5 %collective-permute-start.1 = (bf16[128,128]{1,0:T(8,128)(2,1)S(1)}, bf16[128,128]{1,0:T(8,128)(2,1)S(1)}, u32[]{:S(2)}, u32[]{:S(2)}) collective-permute-start(bf16[128,128]{1,0:T(8,128)(2,1)S(1)} %get-tuple-element.52.refs_13_), channel_id=1, source_target_pairs={{0,20},{4,16},{8,28},{12,24},{16,4},{20,0},{24,12},{28,8},{1,21},{... | collective-permute-start | bytes 98312 | tf_op jit(solution)/shard_map/ppermute | solution.py:444
  6.8 0.1 collective-permute-start
  6.9 0.0 copy-done.4
  6.9 1.4 %shard_map.186 = (f32[128,512]{1,0:T(8,128)S(1)}, f32[128,512]{1,0:T(8,128)S(1)}, f32[128,512]{1,0:T(8,128)S(1)}, f32[128,512]{1,0:T(8,128)S(1)}, f32[128,512]{1...) custom-call(bf16[1,128,512]{2,1,0:T(8,128)(2,1)S(1)} %copy-done.1, ...), custom_call_target="tpu_custom_call" | custom-call | tf_op jit(solution)/shard_map/pallas_call | solution.py:426
  8.3 2.1 %collective-permute-done.1.refs_12_ = bf16[128,128]{1,0:T(8,128)(2,1)S(1)} collective-permute-done((bf16[128,128]{1,0:T(8,128)(2,1)S(1)}, bf16[128,128]{1,0:T(8,128)(2,1)S(1)}, u32[]{:S(2)}, u32[]{:S(2)}) %collective-permute-start.1) | collective-permute-done | bytes 32800 | tf_op jit(solution)/shard_map/ppermute | solution.py:444
  10.4 0.3 %collective-permute-done.refs_3_ = bf16[128,128]{1,0:T(8,128)(2,1)S(1)} collective-permute-done((bf16[128,128]{1,0:T(8,128)(2,1)S(1)}, bf16[128,128]{1,0:T(8,128)(2,1)S(1)}, u32[]{:S(2)}, u32[]{:S(2)}) %collective-permute-start) | collective-permute-done | bytes 32800 | tf_op jit(solution)/shard_map/ppermute | solution.py:444
  10.7 0.3 %collective-permute-done.2.refs_14_ = bf16[784,128]{1,0:T(8,128)(2,1)S(1)} collective-permute-done((bf16[784,128]{1,0:T(8,128)(2,1)S(1)}, bf16[784,128]{1,0:T(8,128)(2,1)S(1)}, u32[]{:S(2)}, u32[]{:S(2)}) %collective-permute-start.2) | collective-permute-done | bytes 200736 | tf_op jit(solution)/shard_map/ppermute | solution.py:444
  11.0 0.0 copy-done
  11.0 1.9 %shard_map.188 = (bf16[2,128,128]{2,1,0:T(8,128)(2,1)S(1)}, bf16[512,128]{1,0:T(8,128)(2,1)S(1)}, bf16[512,256]{1,0:T(8,128)(2,1)S(1)}, bf16[128,256]{1,0:T(8,12...) custom-call(bf16[1,128,512]{2,1,0:T(8,128)(2,1)S(1)} %copy-done, ...), custom_call_target="tpu_custom_call" | custom-call | tf_op jit(solution)/shard_map/pallas_call | solution.py:426
  12.9 1.9 %collective-permute-start.3 = (bf16[512,128]{1,0:T(8,128)(2,1)S(1)}, bf16[512,128]{1,0:T(8,128)(2,1)S(1)}, u32[]{:S(2)}, u32[]{:S(2)}) collective-permute-start(bf16[512,128]{1,0:T(8,128)(2,1)S(1)} %get-tuple-element.66), channel_id=1, source_target_pairs={{0,4},{4,0},{8,12},{12,8},{16,20},{20,16},{24,28},{28,24},{1,5},{5... | collective-permute-start | bytes 393224 | tf_op jit(solution)/shard_map/ppermute | solution.py:444
  14.7 1.2 %shard_map.189 = (f32[1,8,128]{2,1,0:T(8,128)}, f32[8,128]{1,0:T(8,128)S(1)}) custom-call(bf16[640,512]{1,0:T(8,128)(2,1)S(1)} %get-tuple-element.67.products, bf16[128,512]{1,0:T(8,128)(2,1)S(1)} %get-tuple-element.62.scaled.refs_1_, bf16[1024,128]{1,0:T(8,128)(2,1)S(1)} %get-tuple-element.59.refs_10_.halves, f32[1024,128]{1,0:T(8,128)S(1)} %get-tuple-element.68.back, ...), custom_call_target="tpu_custom_call" | custom-call | tf_op jit(solution)/shard_map/pallas_call | solution.py:426
  16.0 0.0 collective-permute-start.6
  16.0 1.5 %collective-permute-start.5 = (f32[8,128]{1,0:T(8,128)S(1)}, f32[8,128]{1,0:T(8,128)S(1)}, u32[]{:S(2)}, u32[]{:S(2)}) collective-permute-start(f32[8,128]{1,0:T(8,128)S(1)} %get-tuple-element.78), channel_id=1, source_target_pairs={{0,2},{1,3},{2,0},{3,1},{4,6},{5,7},{6,4},{7,5},{8,10},{9,11},{10,... | collective-permute-start | bytes 12296 | tf_op jit(solution)/shard_map/ppermute | solution.py:559
  17.5 0.3 %collective-permute-start.4 = (f32[8,128]{1,0:T(8,128)S(1)}, f32[8,128]{1,0:T(8,128)S(1)}, u32[]{:S(2)}, u32[]{:S(2)}) collective-permute-start(f32[8,128]{1,0:T(8,128)S(1)} %get-tuple-element.78), channel_id=1, source_target_pairs={{0,1},{1,0},{2,3},{3,2},{4,5},{5,4},{6,7},{7,6},{8,9},{9,8},{10,11... | collective-permute-start | bytes 12296 | tf_op jit(solution)/shard_map/ppermute | solution.py:559
  17.8 0.1 collective-permute-done.3.refs_2_
  17.9 2.9 %collective-permute-start.7 = (bf16[256,128]{1,0:T(8,128)(2,1)S(1)}, bf16[256,128]{1,0:T(8,128)(2,1)S(1)}, u32[]{:S(2)}, u32[]{:S(2)}) collective-permute-start(bf16[256,128]{1,0:T(8,128)(2,1)S(1)} %add_convert_fusion.mine), channel_id=1, source_target_pairs={{0,8},{4,12},{8,0},{12,4},{16,24},{20,28},{24,16},{28,20},{1,9},{5... | collective-permute-start | bytes 196616 | tf_op jit(solution)/shard_map/ppermute | solution.py:444
  20.8 0.0 collective-permute-done.6
  20.8 0.0 collective-permute-done.5
  20.8 0.0 collective-permute-done.4
  20.9 1.6 %collective-permute-start.8 = (bf16[144,128]{1,0:T(8,128)(2,1)S(1)}, bf16[144,128]{1,0:T(8,128)(2,1)S(1)}, u32[]{:S(2)}, u32[]{:S(2)}) collective-permute-start(bf16[144,128]{1,0:T(8,128)(2,1)S(1)} %pad_maximum_fusion), channel_id=1, source_target_pairs={{0,16},{4,20},{8,24},{12,28},{16,0},{20,4},{24,8},{28,12},{1,17},{... | collective-permute-start | bytes 110600 | tf_op jit(solution)/shard_map/ppermute | solution.py:444
  22.5 1.0 %shard_map.190 = (f32[1,128,512]{2,1,0:T(8,128)}, f32[1,128,512]{2,1,0:T(8,128)}) custom-call(bf16[128,1024]{1,0:T(8,128)(2,1)S(1)} %get-tuple-element.51.refs_0_, bf16[128,512]{1,0:T(8,128)(2,1)S(1)} %get-tuple-element.62.scaled.refs_1_, f32[128,512]{1,0:T(8,128)S(1)} %get-tuple-element.63.refs_2_, f32[128,512]{1,0:T(8,128)S(1)} %get-tuple-element.64.refs_3_, ...), custom_call_target="tpu_custom_call" | custom-call | tf_op jit(solution)/shard_map/pallas_call | solution.py:426
  23.5 0.1 collective-permute-done.7.other
  23.6 0.7 %shard_map.191 = (f32[1,128,128]{2,1,0:T(8,128)}, f32[1,128,128]{2,1,0:T(8,128)}) custom-call(bf16[256,128]{1,0:T(8,128)(2,1)S(1)} %add_convert_fusion.mine, bf16[256,128]{1,0:T(8,128)(2,1)S(1)} %collective-permute-done.7.other), custom_call_target="tpu_custom_call" | custom-call | tf_op jit(solution)/shard_map/pallas_call | solution.py:426
  24.3 0.7 %collective-permute-done.8.refs_0_ = bf16[144,128]{1,0:T(8,128)(2,1)S(1)} collective-permute-done((bf16[144,128]{1,0:T(8,128)(2,1)S(1)}, bf16[144,128]{1,0:T(8,128)(2,1)S(1)}, u32[]{:S(2)}, u32[]{:S(2)}) %collective-permute-start.8) | collective-permute-done | bytes 36896 | tf_op jit(solution)/shard_map/ppermute | solution.py:444
  24.9 0.6 %shard_map.192 = (f32[1,64,128]{2,1,0:T(8,128)}, f32[1,64,128]{2,1,0:T(8,128)}, f32[8]{0:T(128)}, f32[8]{0:T(128)}, f32[8]{0:T(128)}) custom-call(bf16[144,128]{1,0:T(8,128)(2,1)S(1)} %collective-permute-done.8.refs_0_, bf16[2,128,128]{2,1,0:T(8,128)(2,1)S(1)} %get-tuple-element.77.refs_1_, bf16[512,128]{1,0:T(8,128)(2,1)S(1)} %collective-permute-done.3.refs_2_, ...), custom_call_target="tpu_custom_call" | custom-call | tf_op jit(solution)/shard_map/pallas_call | solution.py:426
  (17 shorter events, 0.1 us)
Async XLA Ops:
  0.6 6.2 %copy-start.1 = (bf16[1,128,512]{2,1,0:T(8,128)(2,1)S(1)}, bf16[1,128,512]{2,1,0:T(8,128)(2,1)}, u32[]{:S(2)}) copy-start(bf16[1,128,512]{2,1,0:T(8,128)(2,1)} %refs_3_.1) | copy-start | bytes 393220
  0.7 6.2 %copy-start.2 = (bf16[1,128,512]{2,1,0:T(8,128)(2,1)S(1)}, bf16[1,128,512]{2,1,0:T(8,128)(2,1)}, u32[]{:S(2)}) copy-start(bf16[1,128,512]{2,1,0:T(8,128)(2,1)} %refs_4_.1) | copy-start | bytes 393220
  0.7 6.2 %copy-start.3 = (bf16[1,128,128]{2,1,0:T(8,128)(2,1)S(1)}, bf16[1,128,128]{2,1,0:T(8,128)(2,1)}, u32[]{:S(2)}) copy-start(bf16[1,128,128]{2,1,0:T(8,128)(2,1)} %refs_1_.3) | copy-start | bytes 98308
  0.7 6.2 %copy-start.4 = (bf16[1,128,128]{2,1,0:T(8,128)(2,1)S(1)}, bf16[1,128,128]{2,1,0:T(8,128)(2,1)}, u32[]{:S(2)}) copy-start(bf16[1,128,128]{2,1,0:T(8,128)(2,1)} %refs_2_.3) | copy-start | bytes 98308
  2.2 4.7 %copy-start.5 = (f32[1,8,128]{2,1,0:T(8,128)S(1)}, f32[1,8,128]{2,1,0:T(8,128)}, u32[]{:S(2)}) copy-start(f32[1,8,128]{2,1,0:T(8,128)} %refs_0_.2) | copy-start | bytes 12292
  2.2 4.7 %copy-start.6 = (f32[8]{0:T(128)S(1)}, f32[8]{0:T(128)}, u32[]{:S(2)}) copy-start(f32[8]{0:T(128)} %refs_1_.2) | copy-start | bytes 100
  2.2 4.7 %copy-start.7 = (f32[8]{0:T(128)S(1)}, f32[8]{0:T(128)}, u32[]{:S(2)}) copy-start(f32[8]{0:T(128)} %refs_2_.2) | copy-start | bytes 100
  2.2 4.7 %copy-start.8 = (f32[8]{0:T(128)S(1)}, f32[8]{0:T(128)}, u32[]{:S(2)}) copy-start(f32[8]{0:T(128)} %skip.1) | copy-start | bytes 100
  2.3 8.7 %collective-permute-start.2 = (bf16[784,128]{1,0:T(8,128)(2,1)S(1)}, bf16[784,128]{1,0:T(8,128)(2,1)S(1)}, u32[]{:S(2)}, u32[]{:S(2)}) collective-permute-start(bf16[784,128]{1,0:T(8,128)(2,1)S(1)} %bitcast.8), channel_id=1, source_target_pairs={{0,16},{4,20},{8,24},{12,28},{16,0},{20,4},{24,8},{28,12},{1,17},{... | collective-permute-start | bytes 602120 | tf_op jit(solution)/shard_map/ppermute | solution.py:444
  5.3 5.7 %copy-start = (bf16[1,128,512]{2,1,0:T(8,128)(2,1)S(1)}, bf16[1,128,512]{2,1,0:T(8,128)(2,1)}, u32[]{:S(2)}) copy-start(bf16[1,128,512]{2,1,0:T(8,128)(2,1)} %refs_0_.3) | copy-start | bytes 393220
  5.3 5.2 %collective-permute-start.1 = (bf16[128,128]{1,0:T(8,128)(2,1)S(1)}, bf16[128,128]{1,0:T(8,128)(2,1)S(1)}, u32[]{:S(2)}, u32[]{:S(2)}) collective-permute-start(bf16[128,128]{1,0:T(8,128)(2,1)S(1)} %get-tuple-element.52.refs_13_), channel_id=1, source_target_pairs={{0,20},{4,16},{8,28},{12,24},{16,4},{20,0},{24,12},{28,8},{1,21},{... | collective-permute-start | bytes 98312 | tf_op jit(solution)/shard_map/ppermute | solution.py:444
  6.8 3.9 %collective-permute-start = (bf16[128,128]{1,0:T(8,128)(2,1)S(1)}, bf16[128,128]{1,0:T(8,128)(2,1)S(1)}, u32[]{:S(2)}, u32[]{:S(2)}) collective-permute-start(bf16[128,128]{1,0:T(8,128)(2,1)S(1)} %get-tuple-element.52.refs_13_), channel_id=1, source_target_pairs={{0,4},{4,0},{8,12},{12,8},{16,20},{20,16},{24,28},{28,24},{1,5},{5... | collective-permute-start | bytes 98312 | tf_op jit(solution)/shard_map/ppermute | solution.py:444
  12.9 5.0 %collective-permute-start.3 = (bf16[512,128]{1,0:T(8,128)(2,1)S(1)}, bf16[512,128]{1,0:T(8,128)(2,1)S(1)}, u32[]{:S(2)}, u32[]{:S(2)}) collective-permute-start(bf16[512,128]{1,0:T(8,128)(2,1)S(1)} %get-tuple-element.66), channel_id=1, source_target_pairs={{0,4},{4,0},{8,12},{12,8},{16,20},{20,16},{24,28},{28,24},{1,5},{5... | collective-permute-start | bytes 393224 | tf_op jit(solution)/shard_map/ppermute | solution.py:444
  16.0 4.8 %collective-permute-start.6 = (f32[8,128]{1,0:T(8,128)S(1)}, f32[8,128]{1,0:T(8,128)S(1)}, u32[]{:S(2)}, u32[]{:S(2)}) collective-permute-start(f32[8,128]{1,0:T(8,128)S(1)} %get-tuple-element.78), channel_id=1, source_target_pairs={{0,3},{1,2},{2,1},{3,0},{4,7},{5,6},{6,5},{7,4},{8,11},{9,10},{10,... | collective-permute-start | bytes 12296 | tf_op jit(solution)/shard_map/ppermute | solution.py:559
  16.0 4.8 %collective-permute-start.5 = (f32[8,128]{1,0:T(8,128)S(1)}, f32[8,128]{1,0:T(8,128)S(1)}, u32[]{:S(2)}, u32[]{:S(2)}) collective-permute-start(f32[8,128]{1,0:T(8,128)S(1)} %get-tuple-element.78), channel_id=1, source_target_pairs={{0,2},{1,3},{2,0},{3,1},{4,6},{5,7},{6,4},{7,5},{8,10},{9,11},{10,... | collective-permute-start | bytes 12296 | tf_op jit(solution)/shard_map/ppermute | solution.py:559
  17.5 3.3 %collective-permute-start.4 = (f32[8,128]{1,0:T(8,128)S(1)}, f32[8,128]{1,0:T(8,128)S(1)}, u32[]{:S(2)}, u32[]{:S(2)}) collective-permute-start(f32[8,128]{1,0:T(8,128)S(1)} %get-tuple-element.78), channel_id=1, source_target_pairs={{0,1},{1,0},{2,3},{3,2},{4,5},{5,4},{6,7},{7,6},{8,9},{9,8},{10,11... | collective-permute-start | bytes 12296 | tf_op jit(solution)/shard_map/ppermute | solution.py:559
  17.9 5.7 %collective-permute-start.7 = (bf16[256,128]{1,0:T(8,128)(2,1)S(1)}, bf16[256,128]{1,0:T(8,128)(2,1)S(1)}, u32[]{:S(2)}, u32[]{:S(2)}) collective-permute-start(bf16[256,128]{1,0:T(8,128)(2,1)S(1)} %add_convert_fusion.mine), channel_id=1, source_target_pairs={{0,8},{4,12},{8,0},{12,4},{16,24},{20,28},{24,16},{28,20},{1,9},{5... | collective-permute-start | bytes 196616 | tf_op jit(solution)/shard_map/ppermute | solution.py:444
  20.9 4.0 %collective-permute-start.8 = (bf16[144,128]{1,0:T(8,128)(2,1)S(1)}, bf16[144,128]{1,0:T(8,128)(2,1)S(1)}, u32[]{:S(2)}, u32[]{:S(2)}) collective-permute-start(bf16[144,128]{1,0:T(8,128)(2,1)S(1)} %pad_maximum_fusion), channel_id=1, source_target_pairs={{0,16},{4,20},{8,24},{12,28},{16,0},{20,4},{24,8},{28,12},{1,17},{... | collective-permute-start | bytes 110600 | tf_op jit(solution)/shard_map/ppermute | solution.py:444

commit v4 on v3

--- a/solution.py
+++ b/solution.py
@@ -113,24 +113,24 @@
     for copy in copies:
         copy.start()
     raw, alog, bias, gate, cotangent, read, query, key, value, write = held
-    for copy in copies[:3]:
+    for copy in copies[:6]:
         copy.wait()
     here = lax.axis_index("seq")
     heads, rows = raw.shape[1:]
     wide, states = gate.shape[2], read.shape[2]
     half = key.shape[1]
+    gate_f = gate[0].astype(F32)
+    grad_mixed = cotangent[0].astype(F32) * gate_f * jax.nn.sigmoid(gate_f)
     step, _, cum = rates(raw[0], column(bias, rows), column(alog, rows))
     decay = widen(jnp.exp(-cum), wide // heads)
     to_end = jnp.exp(cum - cum[:, rows - 1 :]) * step
     whole = jnp.broadcast_to(jnp.exp(-cum[:, rows - 1 :]), (heads, rows))
     tail = jnp.concatenate([to_end, whole], axis=0).astype(BF16)
-    for copy in copies[3:]:
+    entry = dot(read[0], grad_mixed * decay, TN).astype(BF16)
+    for copy in copies[6:]:
         copy.wait()
     pack[:half] = key[0]
     pack[half:] = value[0]
-    gate_f = gate[0].astype(F32)
-    grad_mixed = cotangent[0].astype(F32) * gate_f * jax.nn.sigmoid(gate_f)
-    entry = dot(read[0], grad_mixed * decay, TN).astype(BF16)
     for bit in range(message.shape[0]):
         is_early = jnp.bitwise_and(lax.shift_right_logical(here, bit), 1) == 0
         for at in range(0, wide, states):
@@ -199,8 +199,8 @@
     mixed_in, step_in, in_in, out_in, own_in, fall_in, split_in, skip_in = refs[:8]
     refs = refs[8:]
     far, sources, refs = refs[: slots - 1], refs[slots - 1 : 2 * slots - 1], refs[2 * slots - 1 :]
-    kept, sent, scores_out, keys_out, scaled_out, base_out, products_out = refs[:7]
-    (pack, *messages), arrived = refs[7 : 7 + slots], refs[7 + slots]
+    kept, sent, shared, scores_out, keys_out, scaled_out, base_out, products_out = refs[:8]
+    (pack, *messages), arrived = refs[8 : 8 + slots], refs[8 + slots]
     copies = [
         pltpu.make_async_copy(source, held, arrived.at[i])
         for i, (source, held) in enumerate(zip(sources, (pack, *messages)))
@@ -305,8 +305,8 @@
     grad_cross_t = jnp.where(upper, grad_cross_t, 0.0)
     grad_write = dot(grad_cross_t, read_b) + dot(scaled * decay_out, exit_b, NT)
     grad_read = dot(grad_cross_t, write_b, TN) + dot(grad_mixed * decay_in, entry_b, NT)
-    sent[slots * head_dim : slots * head_dim + rows] = grad_write.astype(BF16)
-    sent[slots * head_dim + rows :] = grad_read.astype(BF16)
+    shared[:rows] = grad_write.astype(BF16)
+    shared[rows:] = grad_read.astype(BF16)
     products = (
         inner * grad_scaled,
         inner * from_exit,
@@ -510,11 +510,12 @@
     )
     grad_mixed, slope, step_w, decay_in, decay_out, own, fall, back = prepared[:8]
     ahead, halves, tables, skip_w = prepared[8:]
-    mine, other, scores, keys, scaled, base, products = call(
+    mine, other, shared, scores, keys, scaled, base, products = call(
         lambda *refs: state_kernel(slots, scale, *refs),
         (
             shape((slots, head_dim, rows), BF16),
-            shape((slots * head_dim + 2 * rows, states), BF16),
+            shape((slots * head_dim, rows), BF16),
+            shape((2 * rows, states), BF16),
             shape((wide // head_dim * rows, slots * rows), BF16),
             shape((head_dim, slots * rows), BF16),
             wide_b,
@@ -548,12 +549,13 @@
         (shape((1, heads, rows), F32), shape((8, states), F32)),
         (products, scaled, halves, back, tables),
     )
-    shared, got_shared = other[slots * head_dim :], got[slots * head_dim :]
-    reach = 2
-    while reach < lax.axis_size("tp"):
+    n_tp = lax.axis_size("tp")
+    reaches = [1 << bit for bit in range(1, n_tp.bit_length() - 1)] + [1]
+    got_shared = swap(shared, 0, reaches[0])
+    got, got_shared = lax.optimization_barrier((got, got_shared))
+    for reach in reaches[1:]:
         shared = (shared.astype(F32) + got_shared.astype(F32)).astype(BF16)
         got_shared = swap(shared, 0, reach)
-        reach *= 2
     reach = 1
     while reach < lax.axis_size("dp"):
         near = [params] + [lax.ppermute(params, "dp", flip("dp", k * reach)) for k in (1, 2, 3)]

time: 25.7 us -> 27.3 us (1.062)
  waiting for transfers between devices: 3.49 us -> 4.82 us
    ppermute x3, waiting for transfers between devices: 0.01 us -> 1.23 us  [body(): lax.ppermute(params, 'dp', flip('dp', k * reach))]
    ppermute x6 -> x7, waiting for transfers between devices: 3.49 us -> 3.59 us  [swap(): return lax.ppermute(array, ('seq', 'tp'), pairs)]
    ppermute x6 -> x7, starting transfers between devices: 10.9 us -> 11 us  [swap(): return lax.ppermute(array, ('seq', 'tp'), pairs)]
  transfers between devices with their start and end apart: 9 -> 10, of which waited for: 6 -> 8; matrix products, arithmetic and copies ran while one was open for 0% -> 0% of each run, Pallas kernels for 17% -> 16%
where the time goes in v4:
time: 27.3 us; the launch traced here: 27.1 us
  starting transfers between devices  12.9 us (47%)
  Pallas kernels  8.54 us (31%)
  waiting for transfers between devices  4.82 us (18%)
  between operations  0.81 us (3%)
    ppermute x7, starting transfers between devices, swap(): return lax.ppermute(array, ('seq', 'tp'), pairs)  11 us
    pallas_call x6, Pallas kernels, call(): pl.pallas_call(kernel, out_shape=outs, in_specs=[(specs or {}).get(i, VME...  6.83 us
    ppermute x7, waiting for transfers between devices, swap(): return lax.ppermute(array, ('seq', 'tp'), pairs)  3.59 us
    ppermute x3, starting transfers between devices, body(): lax.ppermute(params, 'dp', flip('dp', k * reach))  1.86 us
    pallas_call x1, Pallas kernels, body(): pl.pallas_call(share_kernel, out_shape=(shape((head_dim, rows), BF16), sh...  1.71 us
    ppermute x3, waiting for transfers between devices, body(): lax.ppermute(params, 'dp', flip('dp', k * reach))  1.23 us
  transfers between devices with their start and end apart: 10, of which 8 were waited for; matrix products, arithmetic and copies ran while one was open for 0% of the time, Pallas kernels for 16%

profile of v4, /device:TPU:0, one launch (start us, length us, event | category | flops | bytes accessed | tf_op | source)
XLA Modules:
  0.0 27.1 jit_solution(13451350297826410421)
XLA Ops:
  0.7 1.7 %shard_map.187 = (bf16[128,128]{1,0:T(8,128)(2,1)S(1)}, bf16[1,784,128]{2,1,0:T(8,128)(2,1)S(1)}) custom-call(f32[1,8,128]{2,1,0:T(8,128)} %refs_0_.2, f32[8]{0:T(128)} %refs_1_.2, f32[8]{0:T(128)} %refs_2_.2, bf16[1,128,512]{2,1,0:T(8,128)(2,1)} %refs_3_.1, bf16[1,128,512]{2,1,0:T(8,128)(2,1)} %refs_4_.1, bf16[1,128,128]{2,1,0:T(8,128)(2,1)} %refs_2_.3, ...), custom_call_target="tpu_custom_call" | custom-call | tf_op jit(solution)/shard_map/pallas_call | solution.py:481
  2.4 0.0 copy-start.5
  2.4 0.0 copy-start.6
  2.4 0.0 copy-start.7
  2.4 0.0 copy-start.8
  2.5 3.0 %collective-permute-start.2 = (bf16[784,128]{1,0:T(8,128)(2,1)S(1)}, bf16[784,128]{1,0:T(8,128)(2,1)S(1)}, u32[]{:S(2)}, u32[]{:S(2)}) collective-permute-start(bf16[784,128]{1,0:T(8,128)(2,1)S(1)} %bitcast.8), channel_id=1, source_target_pairs={{0,16},{4,20},{8,24},{12,28},{16,0},{20,4},{24,8},{28,12},{1,17},{... | collective-permute-start | bytes 602120 | tf_op jit(solution)/shard_map/ppermute | solution.py:444
  5.5 1.5 %collective-permute-start.1 = (bf16[128,128]{1,0:T(8,128)(2,1)S(1)}, bf16[128,128]{1,0:T(8,128)(2,1)S(1)}, u32[]{:S(2)}, u32[]{:S(2)}) collective-permute-start(bf16[128,128]{1,0:T(8,128)(2,1)S(1)} %get-tuple-element.55.refs_13_), channel_id=1, source_target_pairs={{0,20},{4,16},{8,28},{12,24},{16,4},{20,0},{24,12},{28,8},{1,21},{... | collective-permute-start | bytes 98312 | tf_op jit(solution)/shard_map/ppermute | solution.py:444
  7.0 0.1 collective-permute-start
  7.1 0.0 copy-done.2
  7.1 1.4 %shard_map.186 = (f32[128,512]{1,0:T(8,128)S(1)}, f32[128,512]{1,0:T(8,128)S(1)}, f32[128,512]{1,0:T(8,128)S(1)}, f32[128,512]{1,0:T(8,128)S(1)}, f32[128,512]{1...) custom-call(bf16[1,128,512]{2,1,0:T(8,128)(2,1)S(1)} %copy-done.1, ...), custom_call_target="tpu_custom_call" | custom-call | tf_op jit(solution)/shard_map/pallas_call | solution.py:426
  8.5 2.1 %collective-permute-done.1.refs_12_ = bf16[128,128]{1,0:T(8,128)(2,1)S(1)} collective-permute-done((bf16[128,128]{1,0:T(8,128)(2,1)S(1)}, bf16[128,128]{1,0:T(8,128)(2,1)S(1)}, u32[]{:S(2)}, u32[]{:S(2)}) %collective-permute-start.1) | collective-permute-done | bytes 32800 | tf_op jit(solution)/shard_map/ppermute | solution.py:444
  10.6 0.3 %collective-permute-done.refs_3_ = bf16[128,128]{1,0:T(8,128)(2,1)S(1)} collective-permute-done((bf16[128,128]{1,0:T(8,128)(2,1)S(1)}, bf16[128,128]{1,0:T(8,128)(2,1)S(1)}, u32[]{:S(2)}, u32[]{:S(2)}) %collective-permute-start) | collective-permute-done | bytes 32800 | tf_op jit(solution)/shard_map/ppermute | solution.py:444
  10.9 0.3 collective-permute-done.2.refs_14_
  11.2 1.9 %shard_map.188 = (bf16[2,128,128]{2,1,0:T(8,128)(2,1)S(1)}, bf16[256,128]{1,0:T(8,128)(2,1)S(1)}, bf16[256,128]{1,0:T(8,128)(2,1)S(1)}, bf16[512,256]{1,0:T(8,12...) custom-call(bf16[1,128,512]{2,1,0:T(8,128)(2,1)S(1)} %copy-done, ...), custom_call_target="tpu_custom_call" | custom-call | tf_op jit(solution)/shard_map/pallas_call | solution.py:426
  13.1 1.9 %collective-permute-start.3 = (bf16[256,128]{1,0:T(8,128)(2,1)S(1)}, bf16[256,128]{1,0:T(8,128)(2,1)S(1)}, u32[]{:S(2)}, u32[]{:S(2)}) collective-permute-start(bf16[256,128]{1,0:T(8,128)(2,1)S(1)} %get-tuple-element.70), channel_id=1, source_target_pairs={{0,4},{4,0},{8,12},{12,8},{16,20},{20,16},{24,28},{28,24},{1,5},{5... | collective-permute-start | bytes 196616 | tf_op jit(solution)/shard_map/ppermute | solution.py:444
  14.9 2.6 %collective-permute-start.4 = (bf16[256,128]{1,0:T(8,128)(2,1)S(1)}, bf16[256,128]{1,0:T(8,128)(2,1)S(1)}, u32[]{:S(2)}, u32[]{:S(2)}) collective-permute-start(bf16[256,128]{1,0:T(8,128)(2,1)S(1)} %get-tuple-element.69), channel_id=1, source_target_pairs={{0,8},{4,12},{8,0},{12,4},{16,24},{20,28},{24,16},{28,20},{1,9},{5... | collective-permute-start | bytes 196616 | tf_op jit(solution)/shard_map/ppermute | solution.py:444
  17.5 1.2 %shard_map.189 = (f32[1,8,128]{2,1,0:T(8,128)}, f32[8,128]{1,0:T(8,128)S(1)}) custom-call(bf16[640,512]{1,0:T(8,128)(2,1)S(1)} %get-tuple-element.72.products, bf16[128,512]{1,0:T(8,128)(2,1)S(1)} %get-tuple-element.65.scaled.refs_1_, bf16[1024,128]{1,0:T(8,128)(2,1)S(1)} %get-tuple-element.62.refs_10_.halves, f32[1024,128]{1,0:T(8,128)S(1)} %get-tuple-element.73.back, ...), custom_call_target="tpu_custom_call" | custom-call | tf_op jit(solution)/shard_map/pallas_call | solution.py:426
  18.8 0.0 collective-permute-start.7
  18.8 1.5 %collective-permute-start.6 = (f32[8,128]{1,0:T(8,128)S(1)}, f32[8,128]{1,0:T(8,128)S(1)}, u32[]{:S(2)}, u32[]{:S(2)}) collective-permute-start(f32[8,128]{1,0:T(8,128)S(1)} %get-tuple-element.84), channel_id=1, source_target_pairs={{0,2},{1,3},{2,0},{3,1},{4,6},{5,7},{6,4},{7,5},{8,10},{9,11},{10,... | collective-permute-start | bytes 12296 | tf_op jit(solution)/shard_map/ppermute | solution.py:561
  20.3 0.3 %collective-permute-start.5 = (f32[8,128]{1,0:T(8,128)S(1)}, f32[8,128]{1,0:T(8,128)S(1)}, u32[]{:S(2)}, u32[]{:S(2)}) collective-permute-start(f32[8,128]{1,0:T(8,128)S(1)} %get-tuple-element.84), channel_id=1, source_target_pairs={{0,1},{1,0},{2,3},{3,2},{4,5},{5,4},{6,7},{7,6},{8,9},{9,8},{10,11... | collective-permute-start | bytes 12296 | tf_op jit(solution)/shard_map/ppermute | solution.py:561
  20.6 0.0 collective-permute-done.3.refs_2_
  20.6 0.2 collective-permute-done.4
  20.8 0.3 %collective-permute-start.8 = (bf16[256,128]{1,0:T(8,128)(2,1)S(1)}, bf16[256,128]{1,0:T(8,128)(2,1)S(1)}, u32[]{:S(2)}, u32[]{:S(2)}) collective-permute-start(bf16[256,128]{1,0:T(8,128)(2,1)S(1)} %add_convert_fusion.mine), channel_id=1, source_target_pairs={{0,4},{4,0},{8,12},{12,8},{16,20},{20,16},{24,28},{28,24},{1,5},{5... | collective-permute-start | bytes 196616 | tf_op jit(solution)/shard_map/ppermute | solution.py:444
  21.2 0.6 %collective-permute-done.7 = f32[8,128]{1,0:T(8,128)S(1)} collective-permute-done((f32[8,128]{1,0:T(8,128)S(1)}, f32[8,128]{1,0:T(8,128)S(1)}, u32[]{:S(2)}, u32[]{:S(2)}) %collective-permute-start.7) | collective-permute-done | bytes 4128 | tf_op jit(solution)/shard_map/ppermute | solution.py:561
  21.8 0.6 %collective-permute-done.6 = f32[8,128]{1,0:T(8,128)S(1)} collective-permute-done((f32[8,128]{1,0:T(8,128)S(1)}, f32[8,128]{1,0:T(8,128)S(1)}, u32[]{:S(2)}, u32[]{:S(2)}) %collective-permute-start.6) | collective-permute-done | bytes 4128 | tf_op jit(solution)/shard_map/ppermute | solution.py:561
  22.4 0.0 collective-permute-done.5
  22.5 1.6 %collective-permute-start.9 = (bf16[144,128]{1,0:T(8,128)(2,1)S(1)}, bf16[144,128]{1,0:T(8,128)(2,1)S(1)}, u32[]{:S(2)}, u32[]{:S(2)}) collective-permute-start(bf16[144,128]{1,0:T(8,128)(2,1)S(1)} %pad_maximum_fusion), channel_id=1, source_target_pairs={{0,16},{4,20},{8,24},{12,28},{16,0},{20,4},{24,8},{28,12},{1,17},{... | collective-permute-start | bytes 110600 | tf_op jit(solution)/shard_map/ppermute | solution.py:444
  24.1 1.0 %shard_map.190 = (f32[1,128,512]{2,1,0:T(8,128)}, f32[1,128,512]{2,1,0:T(8,128)}) custom-call(bf16[128,1024]{1,0:T(8,128)(2,1)S(1)} %get-tuple-element.54.refs_0_, bf16[128,512]{1,0:T(8,128)(2,1)S(1)} %get-tuple-element.65.scaled.refs_1_, f32[128,512]{1,0:T(8,128)S(1)} %get-tuple-element.66.refs_2_, f32[128,512]{1,0:T(8,128)S(1)} %get-tuple-element.67.refs_3_, ...), custom_call_target="tpu_custom_call" | custom-call | tf_op jit(solution)/shard_map/pallas_call | solution.py:426
  25.1 0.1 collective-permute-done.8.other
  25.2 0.7 %shard_map.191 = (f32[1,128,128]{2,1,0:T(8,128)}, f32[1,128,128]{2,1,0:T(8,128)}) custom-call(bf16[256,128]{1,0:T(8,128)(2,1)S(1)} %add_convert_fusion.mine, bf16[256,128]{1,0:T(8,128)(2,1)S(1)} %collective-permute-done.8.other), custom_call_target="tpu_custom_call" | custom-call | tf_op jit(solution)/shard_map/pallas_call | solution.py:426
  25.8 0.7 %collective-permute-done.9.refs_0_ = bf16[144,128]{1,0:T(8,128)(2,1)S(1)} collective-permute-done((bf16[144,128]{1,0:T(8,128)(2,1)S(1)}, bf16[144,128]{1,0:T(8,128)(2,1)S(1)}, u32[]{:S(2)}, u32[]{:S(2)}) %collective-permute-start.9) | collective-permute-done | bytes 36896 | tf_op jit(solution)/shard_map/ppermute | solution.py:444
  26.5 0.6 %shard_map.192 = (f32[1,64,128]{2,1,0:T(8,128)}, f32[1,64,128]{2,1,0:T(8,128)}, f32[8]{0:T(128)}, f32[8]{0:T(128)}, f32[8]{0:T(128)}) custom-call(bf16[144,128]{1,0:T(8,128)(2,1)S(1)} %collective-permute-done.9.refs_0_, bf16[2,128,128]{2,1,0:T(8,128)(2,1)S(1)} %get-tuple-element.82.refs_1_, bf16[256,128]{1,0:T(8,128)(2,1)S(1)} %collective-permute-done.3.refs_2_, ...), custom_call_target="tpu_custom_call" | custom-call | tf_op jit(solution)/shard_map/pallas_call | solution.py:426
  (19 shorter events, 0.1 us)
Async XLA Ops:
  0.6 6.4 %copy-start.1 = (bf16[1,128,512]{2,1,0:T(8,128)(2,1)S(1)}, bf16[1,128,512]{2,1,0:T(8,128)(2,1)}, u32[]{:S(2)}) copy-start(bf16[1,128,512]{2,1,0:T(8,128)(2,1)} %refs_3_.1) | copy-start | bytes 393220
  0.7 6.4 %copy-start.2 = (bf16[1,128,512]{2,1,0:T(8,128)(2,1)S(1)}, bf16[1,128,512]{2,1,0:T(8,128)(2,1)}, u32[]{:S(2)}) copy-start(bf16[1,128,512]{2,1,0:T(8,128)(2,1)} %refs_4_.1) | copy-start | bytes 393220
  0.7 6.4 %copy-start.3 = (bf16[1,128,128]{2,1,0:T(8,128)(2,1)S(1)}, bf16[1,128,128]{2,1,0:T(8,128)(2,1)}, u32[]{:S(2)}) copy-start(bf16[1,128,128]{2,1,0:T(8,128)(2,1)} %refs_1_.3) | copy-start | bytes 98308
  0.7 6.4 %copy-start.4 = (bf16[1,128,128]{2,1,0:T(8,128)(2,1)S(1)}, bf16[1,128,128]{2,1,0:T(8,128)(2,1)}, u32[]{:S(2)}) copy-start(bf16[1,128,128]{2,1,0:T(8,128)(2,1)} %refs_2_.3) | copy-start | bytes 98308
  2.4 4.7 %copy-start.5 = (f32[1,8,128]{2,1,0:T(8,128)S(1)}, f32[1,8,128]{2,1,0:T(8,128)}, u32[]{:S(2)}) copy-start(f32[1,8,128]{2,1,0:T(8,128)} %refs_0_.2) | copy-start | bytes 12292
  2.4 4.7 %copy-start.6 = (f32[8]{0:T(128)S(1)}, f32[8]{0:T(128)}, u32[]{:S(2)}) copy-start(f32[8]{0:T(128)} %refs_1_.2) | copy-start | bytes 100
  2.4 4.7 %copy-start.7 = (f32[8]{0:T(128)S(1)}, f32[8]{0:T(128)}, u32[]{:S(2)}) copy-start(f32[8]{0:T(128)} %refs_2_.2) | copy-start | bytes 100
  2.4 4.7 %copy-start.8 = (f32[8]{0:T(128)S(1)}, f32[8]{0:T(128)}, u32[]{:S(2)}) copy-start(f32[8]{0:T(128)} %skip.1) | copy-start | bytes 100
  2.5 8.7 %collective-permute-start.2 = (bf16[784,128]{1,0:T(8,128)(2,1)S(1)}, bf16[784,128]{1,0:T(8,128)(2,1)S(1)}, u32[]{:S(2)}, u32[]{:S(2)}) collective-permute-start(bf16[784,128]{1,0:T(8,128)(2,1)S(1)} %bitcast.8), channel_id=1, source_target_pairs={{0,16},{4,20},{8,24},{12,28},{16,0},{20,4},{24,8},{28,12},{1,17},{... | collective-permute-start | bytes 602120 | tf_op jit(solution)/shard_map/ppermute | solution.py:444
  5.5 5.7 %copy-start = (bf16[1,128,512]{2,1,0:T(8,128)(2,1)S(1)}, bf16[1,128,512]{2,1,0:T(8,128)(2,1)}, u32[]{:S(2)}) copy-start(bf16[1,128,512]{2,1,0:T(8,128)(2,1)} %refs_0_.3) | copy-start | bytes 393220
  5.5 5.2 %collective-permute-start.1 = (bf16[128,128]{1,0:T(8,128)(2,1)S(1)}, bf16[128,128]{1,0:T(8,128)(2,1)S(1)}, u32[]{:S(2)}, u32[]{:S(2)}) collective-permute-start(bf16[128,128]{1,0:T(8,128)(2,1)S(1)} %get-tuple-element.55.refs_13_), channel_id=1, source_target_pairs={{0,20},{4,16},{8,28},{12,24},{16,4},{20,0},{24,12},{28,8},{1,21},{... | collective-permute-start | bytes 98312 | tf_op jit(solution)/shard_map/ppermute | solution.py:444
  7.0 3.9 %collective-permute-start = (bf16[128,128]{1,0:T(8,128)(2,1)S(1)}, bf16[128,128]{1,0:T(8,128)(2,1)S(1)}, u32[]{:S(2)}, u32[]{:S(2)}) collective-permute-start(bf16[128,128]{1,0:T(8,128)(2,1)S(1)} %get-tuple-element.55.refs_13_), channel_id=1, source_target_pairs={{0,4},{4,0},{8,12},{12,8},{16,20},{20,16},{24,28},{28,24},{1,5},{5... | collective-permute-start | bytes 98312 | tf_op jit(solution)/shard_map/ppermute | solution.py:444
  13.1 7.6 %collective-permute-start.3 = (bf16[256,128]{1,0:T(8,128)(2,1)S(1)}, bf16[256,128]{1,0:T(8,128)(2,1)S(1)}, u32[]{:S(2)}, u32[]{:S(2)}) collective-permute-start(bf16[256,128]{1,0:T(8,128)(2,1)S(1)} %get-tuple-element.70), channel_id=1, source_target_pairs={{0,4},{4,0},{8,12},{12,8},{16,20},{20,16},{24,28},{28,24},{1,5},{5... | collective-permute-start | bytes 196616 | tf_op jit(solution)/shard_map/ppermute | solution.py:444
  14.9 5.9 %collective-permute-start.4 = (bf16[256,128]{1,0:T(8,128)(2,1)S(1)}, bf16[256,128]{1,0:T(8,128)(2,1)S(1)}, u32[]{:S(2)}, u32[]{:S(2)}) collective-permute-start(bf16[256,128]{1,0:T(8,128)(2,1)S(1)} %get-tuple-element.69), channel_id=1, source_target_pairs={{0,8},{4,12},{8,0},{12,4},{16,24},{20,28},{24,16},{28,20},{1,9},{5... | collective-permute-start | bytes 196616 | tf_op jit(solution)/shard_map/ppermute | solution.py:444
  18.8 3.0 %collective-permute-start.7 = (f32[8,128]{1,0:T(8,128)S(1)}, f32[8,128]{1,0:T(8,128)S(1)}, u32[]{:S(2)}, u32[]{:S(2)}) collective-permute-start(f32[8,128]{1,0:T(8,128)S(1)} %get-tuple-element.84), channel_id=1, source_target_pairs={{0,3},{1,2},{2,1},{3,0},{4,7},{5,6},{6,5},{7,4},{8,11},{9,10},{10,... | collective-permute-start | bytes 12296 | tf_op jit(solution)/shard_map/ppermute | solution.py:561
  18.8 3.6 %collective-permute-start.6 = (f32[8,128]{1,0:T(8,128)S(1)}, f32[8,128]{1,0:T(8,128)S(1)}, u32[]{:S(2)}, u32[]{:S(2)}) collective-permute-start(f32[8,128]{1,0:T(8,128)S(1)} %get-tuple-element.84), channel_id=1, source_target_pairs={{0,2},{1,3},{2,0},{3,1},{4,6},{5,7},{6,4},{7,5},{8,10},{9,11},{10,... | collective-permute-start | bytes 12296 | tf_op jit(solution)/shard_map/ppermute | solution.py:561
  20.3 2.1 %collective-permute-start.5 = (f32[8,128]{1,0:T(8,128)S(1)}, f32[8,128]{1,0:T(8,128)S(1)}, u32[]{:S(2)}, u32[]{:S(2)}) collective-permute-start(f32[8,128]{1,0:T(8,128)S(1)} %get-tuple-element.84), channel_id=1, source_target_pairs={{0,1},{1,0},{2,3},{3,2},{4,5},{5,4},{6,7},{7,6},{8,9},{9,8},{10,11... | collective-permute-start | bytes 12296 | tf_op jit(solution)/shard_map/ppermute | solution.py:561
  20.8 4.3 %collective-permute-start.8 = (bf16[256,128]{1,0:T(8,128)(2,1)S(1)}, bf16[256,128]{1,0:T(8,128)(2,1)S(1)}, u32[]{:S(2)}, u32[]{:S(2)}) collective-permute-start(bf16[256,128]{1,0:T(8,128)(2,1)S(1)} %add_convert_fusion.mine), channel_id=1, source_target_pairs={{0,4},{4,0},{8,12},{12,8},{16,20},{20,16},{24,28},{28,24},{1,5},{5... | collective-permute-start | bytes 196616 | tf_op jit(solution)/shard_map/ppermute | solution.py:444
  22.5 4.0 %collective-permute-start.9 = (bf16[144,128]{1,0:T(8,128)(2,1)S(1)}, bf16[144,128]{1,0:T(8,128)(2,1)S(1)}, u32[]{:S(2)}, u32[]{:S(2)}) collective-permute-start(bf16[144,128]{1,0:T(8,128)(2,1)S(1)} %pad_maximum_fusion), channel_id=1, source_target_pairs={{0,16},{4,20},{8,24},{12,28},{16,0},{20,4},{24,8},{28,12},{1,17},{... | collective-permute-start | bytes 110600 | tf_op jit(solution)/shard_map/ppermute | solution.py:444

commit v5 on v3

--- a/solution.py
+++ b/solution.py
@@ -106,15 +106,15 @@
 
 def share_kernel(*refs):
     sources, (pack, message), held, arrived = refs[:10], refs[10:12], refs[12:22], refs[22]
+    raw, gate, cotangent, read, query, write, alog, bias, key, value = held
     copies = [
         pltpu.make_async_copy(source, here, arrived.at[i])
         for i, (source, here) in enumerate(zip(sources, held))
     ]
-    for copy in copies:
-        copy.start()
-    raw, alog, bias, gate, cotangent, read, query, key, value, write = held
-    for copy in copies[:3]:
-        copy.wait()
+    for place in (0, 6, 7, 1, 2, 3, 4, 8, 9, 5):
+        copies[place].start()
+    for place in (0, 6, 7):
+        copies[place].wait()
     here = lax.axis_index("seq")
     heads, rows = raw.shape[1:]
     wide, states = gate.shape[2], read.shape[2]
@@ -124,13 +124,15 @@
     to_end = jnp.exp(cum - cum[:, rows - 1 :]) * step
     whole = jnp.broadcast_to(jnp.exp(-cum[:, rows - 1 :]), (heads, rows))
     tail = jnp.concatenate([to_end, whole], axis=0).astype(BF16)
-    for copy in copies[3:]:
-        copy.wait()
-    pack[:half] = key[0]
-    pack[half:] = value[0]
+    for place in (1, 2, 3):
+        copies[place].wait()
     gate_f = gate[0].astype(F32)
     grad_mixed = cotangent[0].astype(F32) * gate_f * jax.nn.sigmoid(gate_f)
     entry = dot(read[0], grad_mixed * decay, TN).astype(BF16)
+    for place in (4, 5, 8, 9):
+        copies[place].wait()
+    pack[:half] = key[0]
+    pack[half:] = value[0]
     for bit in range(message.shape[0]):
         is_early = jnp.bitwise_and(lax.shift_right_logical(here, bit), 1) == 0
         for at in range(0, wide, states):
@@ -198,15 +200,9 @@
 def state_kernel(slots, scale, query, write, read, partner, *refs):
     mixed_in, step_in, in_in, out_in, own_in, fall_in, split_in, skip_in = refs[:8]
     refs = refs[8:]
-    far, sources, refs = refs[: slots - 1], refs[slots - 1 : 2 * slots - 1], refs[2 * slots - 1 :]
-    kept, sent, scores_out, keys_out, scaled_out, base_out, products_out = refs[:7]
-    (pack, *messages), arrived = refs[7 : 7 + slots], refs[7 + slots]
-    copies = [
-        pltpu.make_async_copy(source, held, arrived.at[i])
-        for i, (source, held) in enumerate(zip(sources, (pack, *messages)))
-    ]
-    for copy in copies:
-        copy.start()
+    far, (pack, *messages) = refs[: slots - 1], refs[slots - 1 : 2 * slots - 1]
+    refs = refs[2 * slots - 1 :]
+    kept, sent, scores_out, keys_out, scaled_out, base_out, products_out = refs
     here = lax.axis_index("seq")
     parity = lax.axis_index("tp") % 2
     rows, wide = query.shape[1:]
@@ -214,9 +210,6 @@
     channels = wide // heads
     states, head_dim = write.shape[2], pack.shape[0]
     half, pair, count = head_dim // 2, 2 * channels, wide // head_dim
-    for copy in copies:
-        copy.wait()
-
     key_parts, value_parts = [], []
     for slot in range(slots):
         near = messages[slot - 1][wide : wide + head_dim] if slot else pack[...]
@@ -422,15 +415,14 @@
 PARAMS = pltpu.CompilerParams(vmem_limit_bytes=48 * 1024 * 1024)
 
 
-def call(kernel, outs, args, specs=None, scratch=(), flops=0):
+def call(kernel, outs, args, specs=None):
     return pl.pallas_call(
         kernel,
         out_shape=outs,
         in_specs=[(specs or {}).get(i, VMEM) for i in range(len(args))],
         out_specs=jax.tree.map(lambda _: VMEM, outs),
-        scratch_shapes=scratch,
         compiler_params=PARAMS,
-        cost_estimate=pl.CostEstimate(flops=flops, bytes_accessed=0, transcendentals=0),
+        cost_estimate=pl.CostEstimate(flops=0, bytes_accessed=0, transcendentals=0),
     )(*args)
 
 
@@ -466,29 +458,20 @@
 
     bits = slots.bit_length() - 1
     key_t, value_t = key_rows.swapaxes(1, 2), value_rows.swapaxes(1, 2)
-    sources = (
-        dt_raw,
-        a_log,
-        dt_bias,
-        gate_rows,
-        out_grad,
-        read_vec,
-        query_rows,
-        key_t,
-        value_t,
-        write_vec,
-    )
-    pack, message = pl.pallas_call(
+    kept_here = (dt_raw, gate_rows, out_grad, read_vec, query_rows, write_vec)
+    sources = kept_here + (a_log, dt_bias, key_t, value_t)
+    pack, message, dt_raw, gate_rows, out_grad, read_vec, query_rows, write_vec = pl.pallas_call(
         share_kernel,
         out_shape=(
             shape((head_dim, rows), BF16),
             shape((bits, wide + 2 * rows + 2 * heads, head_dim), BF16),
-        ),
+        )
+        + tuple(shape(a.shape, a.dtype) for a in kept_here),
         in_specs=[HBM] * len(sources),
-        out_specs=(VMEM, VMEM),
+        out_specs=(VMEM,) * (2 + len(kept_here)),
         scratch_shapes=[
             pltpu.SMEM(a.shape, a.dtype) if a.ndim == 1 else pltpu.VMEM(a.shape, a.dtype)
-            for a in sources
+            for a in sources[len(kept_here) :]
         ]
         + [pltpu.SemaphoreType.DMA((len(sources),))],
         compiler_params=PARAMS,
@@ -538,9 +521,6 @@
             pack,
             *messages,
         ),
-        {11 + slots + i: HBM for i in range(slots)},
-        [pltpu.VMEM(m.shape, m.dtype) for m in (pack, *messages)]
-        + [pltpu.SemaphoreType.DMA((slots,))],
     )
     got = swap(other, 0, 1)
     grad_dt, params = call(

time: 25.7 us -> 25.4 us (0.988)
  waiting for transfers between devices: 3.49 us -> 2.86 us
  local copies, waits for them, and re-layouts: 0.05 us -> 0.68 us
  Pallas kernels: 8.36 us -> 8.06 us
    unnamed x18 -> x6, local copies, waits for them, and re-layouts: 0.05 us -> 0.68 us
    ppermute x6, waiting for transfers between devices: 3.49 us -> 2.85 us  [swap(): return lax.ppermute(array, ('seq', 'tp'), pairs)]
    pallas_call x6, Pallas kernels: 6.84 us -> 6.51 us  [call(): pl.pallas_call(kernel, out_shape=outs, in_specs=[(specs or {}).get(i, VME...]
where the time goes in v5:
time: 25.4 us; the launch traced here: 25.2 us
  starting transfers between devices  12.8 us (50%)
  Pallas kernels  8.06 us (32%)
  waiting for transfers between devices  2.86 us (11%)
  between operations  0.72 us (3%)
  local copies, waits for them, and re-layouts  0.68 us (3%)
    ppermute x6, starting transfers between devices, swap(): return lax.ppermute(array, ('seq', 'tp'), pairs)  10.9 us
    pallas_call x6, Pallas kernels, call(): pl.pallas_call(kernel, out_shape=outs, in_specs=[(specs or {}).get(i, VME...  6.51 us
    ppermute x6, waiting for transfers between devices, swap(): return lax.ppermute(array, ('seq', 'tp'), pairs)  2.85 us
    ppermute x3, starting transfers between devices, body(): lax.ppermute(params, 'dp', flip('dp', k * reach))  1.86 us
    pallas_call x1, Pallas kernels, body(): pl.pallas_call(share_kernel, out_shape=(shape((head_dim, rows), BF16), sh...  1.55 us
    unnamed x6, local copies, waits for them, and re-layouts  0.68 us
  transfers between devices with their start and end apart: 9, of which 6 were waited for; matrix products, arithmetic and copies ran while one was open for 0% of the time, Pallas kernels for 17%

profile of v5, /device:TPU:0, one launch (start us, length us, event | category | flops | bytes accessed | tf_op | source)
XLA Modules:
  0.0 25.2 jit_solution(8910961362353780939)
XLA Ops:
  0.6 1.6 %shard_map.186 = (bf16[128,128]{1,0:T(8,128)(2,1)S(1)}, bf16[1,784,128]{2,1,0:T(8,128)(2,1)S(1)}, f32[1,8,128]{2,1,0:T(8,128)S(1)}, bf16[1,128,512]{2,1,0:T(8,12...) custom-call(f32[1,8,128]{2,1,0:T(8,128)} %refs_0_.1, ...), custom_call_target="tpu_custom_call" | custom-call | tf_op jit(solution)/shard_map/pallas_call | solution.py:463
  2.2 3.0 %collective-permute-start.2 = (bf16[784,128]{1,0:T(8,128)(2,1)S(1)}, bf16[784,128]{1,0:T(8,128)(2,1)S(1)}, u32[]{:S(2)}, u32[]{:S(2)}) collective-permute-start(bf16[784,128]{1,0:T(8,128)(2,1)S(1)} %bitcast.8), channel_id=1, source_target_pairs={{0,16},{4,20},{8,24},{12,28},{16,0},{20,4},{24,8},{28,12},{1,17},{... | collective-permute-start | bytes 602120 | tf_op jit(solution)/shard_map/ppermute | solution.py:436
  5.2 1.5 %collective-permute-start.1 = (bf16[128,128]{1,0:T(8,128)(2,1)S(1)}, bf16[128,128]{1,0:T(8,128)(2,1)S(1)}, u32[]{:S(2)}, u32[]{:S(2)}) collective-permute-start(bf16[128,128]{1,0:T(8,128)(2,1)S(1)} %get-tuple-element.64.refs_13_), channel_id=1, source_target_pairs={{0,20},{4,16},{8,28},{12,24},{16,4},{20,0},{24,12},{28,8},{1,21},{... | collective-permute-start | bytes 98312 | tf_op jit(solution)/shard_map/ppermute | solution.py:436
  6.8 0.1 collective-permute-start
  6.8 0.0 copy-start
  6.8 0.0 copy-start.1
  6.8 0.0 copy-start.2
  6.8 0.6 %copy-done = f32[8]{0:T(128)S(1)} copy-done((f32[8]{0:T(128)S(1)}, f32[8]{0:T(128)}, u32[]{:S(2)}) %copy-start) | copy-done | bytes 56
  7.5 0.0 copy-done.1
  7.5 0.0 copy-done.2
  7.5 1.4 %shard_map.187 = (f32[128,512]{1,0:T(8,128)S(1)}, f32[128,512]{1,0:T(8,128)S(1)}, f32[128,512]{1,0:T(8,128)S(1)}, f32[128,512]{1,0:T(8,128)S(1)}, f32[128,512]{1...) custom-call(bf16[1,128,512]{2,1,0:T(8,128)(2,1)S(1)} %get-tuple-elem, ...), custom_call_target="tpu_custom_call" | custom-call | tf_op jit(solution)/shard_map/pallas_call | solution.py:419
  8.9 1.5 %collective-permute-done.1.refs_12_ = bf16[128,128]{1,0:T(8,128)(2,1)S(1)} collective-permute-done((bf16[128,128]{1,0:T(8,128)(2,1)S(1)}, bf16[128,128]{1,0:T(8,128)(2,1)S(1)}, u32[]{:S(2)}, u32[]{:S(2)}) %collective-permute-start.1) | collective-permute-done | bytes 32800 | tf_op jit(solution)/shard_map/ppermute | solution.py:436
  10.4 0.3 %collective-permute-done.refs_3_ = bf16[128,128]{1,0:T(8,128)(2,1)S(1)} collective-permute-done((bf16[128,128]{1,0:T(8,128)(2,1)S(1)}, bf16[128,128]{1,0:T(8,128)(2,1)S(1)}, u32[]{:S(2)}, u32[]{:S(2)}) %collective-permute-start) | collective-permute-done | bytes 32800 | tf_op jit(solution)/shard_map/ppermute | solution.py:436
  10.7 0.3 %collective-permute-done.2.refs_14_ = bf16[784,128]{1,0:T(8,128)(2,1)S(1)} collective-permute-done((bf16[784,128]{1,0:T(8,128)(2,1)S(1)}, bf16[784,128]{1,0:T(8,128)(2,1)S(1)}, u32[]{:S(2)}, u32[]{:S(2)}) %collective-permute-start.2) | collective-permute-done | bytes 200736 | tf_op jit(solution)/shard_map/ppermute | solution.py:436
  10.9 1.6 %shard_map.188 = (bf16[2,128,128]{2,1,0:T(8,128)(2,1)S(1)}, bf16[512,128]{1,0:T(8,128)(2,1)S(1)}, bf16[512,256]{1,0:T(8,128)(2,1)S(1)}, bf16[128,256]{1,0:T(8,12...) custom-call(bf16[1,128,512]{2,1,0:T(8,128)(2,1)S(1)} %get-tuple-element.63.refs_0_, ...), custom_call_target="tpu_custom_call" | custom-call | tf_op jit(solution)/shard_map/pallas_call | solution.py:419
  12.5 1.9 %collective-permute-start.3 = (bf16[512,128]{1,0:T(8,128)(2,1)S(1)}, bf16[512,128]{1,0:T(8,128)(2,1)S(1)}, u32[]{:S(2)}, u32[]{:S(2)}) collective-permute-start(bf16[512,128]{1,0:T(8,128)(2,1)S(1)} %get-tuple-element.78), channel_id=1, source_target_pairs={{0,4},{4,0},{8,12},{12,8},{16,20},{20,16},{24,28},{28,24},{1,5},{5... | collective-permute-start | bytes 393224 | tf_op jit(solution)/shard_map/ppermute | solution.py:436
  14.4 1.2 %shard_map.189 = (f32[1,8,128]{2,1,0:T(8,128)}, f32[8,128]{1,0:T(8,128)S(1)}) custom-call(bf16[640,512]{1,0:T(8,128)(2,1)S(1)} %get-tuple-element.79.products, bf16[128,512]{1,0:T(8,128)(2,1)S(1)} %get-tuple-element.74.scaled.refs_1_, bf16[1024,128]{1,0:T(8,128)(2,1)S(1)} %get-tuple-element.71.refs_10_.halves, f32[1024,128]{1,0:T(8,128)S(1)} %get-tuple-element.80.back, ...), custom_call_target="tpu_custom_call" | custom-call | tf_op jit(solution)/shard_map/pallas_call | solution.py:419
  15.6 0.0 collective-permute-start.6
  15.6 1.5 %collective-permute-start.5 = (f32[8,128]{1,0:T(8,128)S(1)}, f32[8,128]{1,0:T(8,128)S(1)}, u32[]{:S(2)}, u32[]{:S(2)}) collective-permute-start(f32[8,128]{1,0:T(8,128)S(1)} %get-tuple-element.90), channel_id=1, source_target_pairs={{0,2},{1,3},{2,0},{3,1},{4,6},{5,7},{6,4},{7,5},{8,10},{9,11},{10,... | collective-permute-start | bytes 12296 | tf_op jit(solution)/shard_map/ppermute | solution.py:539
  17.1 0.3 %collective-permute-start.4 = (f32[8,128]{1,0:T(8,128)S(1)}, f32[8,128]{1,0:T(8,128)S(1)}, u32[]{:S(2)}, u32[]{:S(2)}) collective-permute-start(f32[8,128]{1,0:T(8,128)S(1)} %get-tuple-element.90), channel_id=1, source_target_pairs={{0,1},{1,0},{2,3},{3,2},{4,5},{5,4},{6,7},{7,6},{8,9},{9,8},{10,11... | collective-permute-start | bytes 12296 | tf_op jit(solution)/shard_map/ppermute | solution.py:539
  17.5 0.1 collective-permute-done.3.refs_2_
  17.6 2.9 %collective-permute-start.7 = (bf16[256,128]{1,0:T(8,128)(2,1)S(1)}, bf16[256,128]{1,0:T(8,128)(2,1)S(1)}, u32[]{:S(2)}, u32[]{:S(2)}) collective-permute-start(bf16[256,128]{1,0:T(8,128)(2,1)S(1)} %add_convert_fusion.mine), channel_id=1, source_target_pairs={{0,8},{4,12},{8,0},{12,4},{16,24},{20,28},{24,16},{28,20},{1,9},{5... | collective-permute-start | bytes 196616 | tf_op jit(solution)/shard_map/ppermute | solution.py:436
  20.4 0.0 collective-permute-done.6
  20.4 0.0 collective-permute-done.5
  20.4 0.0 collective-permute-done.4
  20.5 1.6 %collective-permute-start.8 = (bf16[144,128]{1,0:T(8,128)(2,1)S(1)}, bf16[144,128]{1,0:T(8,128)(2,1)S(1)}, u32[]{:S(2)}, u32[]{:S(2)}) collective-permute-start(bf16[144,128]{1,0:T(8,128)(2,1)S(1)} %pad_maximum_fusion), channel_id=1, source_target_pairs={{0,16},{4,20},{8,24},{12,28},{16,0},{20,4},{24,8},{28,12},{1,17},{... | collective-permute-start | bytes 110600 | tf_op jit(solution)/shard_map/ppermute | solution.py:436
  22.1 1.0 %shard_map.190 = (f32[1,128,512]{2,1,0:T(8,128)}, f32[1,128,512]{2,1,0:T(8,128)}) custom-call(bf16[128,1024]{1,0:T(8,128)(2,1)S(1)} %get-tuple-element.62.refs_0_, bf16[128,512]{1,0:T(8,128)(2,1)S(1)} %get-tuple-element.74.scaled.refs_1_, f32[128,512]{1,0:T(8,128)S(1)} %get-tuple-element.75.refs_2_, f32[128,512]{1,0:T(8,128)S(1)} %get-tuple-element.76.refs_3_, ...), custom_call_target="tpu_custom_call" | custom-call | tf_op jit(solution)/shard_map/pallas_call | solution.py:419
  23.1 0.1 collective-permute-done.7.other
  23.2 0.7 %shard_map.191 = (f32[1,128,128]{2,1,0:T(8,128)}, f32[1,128,128]{2,1,0:T(8,128)}) custom-call(bf16[256,128]{1,0:T(8,128)(2,1)S(1)} %add_convert_fusion.mine, bf16[256,128]{1,0:T(8,128)(2,1)S(1)} %collective-permute-done.7.other), custom_call_target="tpu_custom_call" | custom-call | tf_op jit(solution)/shard_map/pallas_call | solution.py:419
  23.9 0.7 %collective-permute-done.8.refs_0_ = bf16[144,128]{1,0:T(8,128)(2,1)S(1)} collective-permute-done((bf16[144,128]{1,0:T(8,128)(2,1)S(1)}, bf16[144,128]{1,0:T(8,128)(2,1)S(1)}, u32[]{:S(2)}, u32[]{:S(2)}) %collective-permute-start.8) | collective-permute-done | bytes 36896 | tf_op jit(solution)/shard_map/ppermute | solution.py:436
  24.5 0.6 %shard_map.192 = (f32[1,64,128]{2,1,0:T(8,128)}, f32[1,64,128]{2,1,0:T(8,128)}, f32[8]{0:T(128)}, f32[8]{0:T(128)}, f32[8]{0:T(128)}) custom-call(bf16[144,128]{1,0:T(8,128)(2,1)S(1)} %collective-permute-done.8.refs_0_, bf16[2,128,128]{2,1,0:T(8,128)(2,1)S(1)} %get-tuple-element.89.refs_1_, bf16[512,128]{1,0:T(8,128)(2,1)S(1)} %collective-permute-done.3.refs_2_, ...), custom_call_target="tpu_custom_call" | custom-call | tf_op jit(solution)/shard_map/pallas_call | solution.py:419
  (6 shorter events, 0.1 us)
Async XLA Ops:
  2.2 8.7 %collective-permute-start.2 = (bf16[784,128]{1,0:T(8,128)(2,1)S(1)}, bf16[784,128]{1,0:T(8,128)(2,1)S(1)}, u32[]{:S(2)}, u32[]{:S(2)}) collective-permute-start(bf16[784,128]{1,0:T(8,128)(2,1)S(1)} %bitcast.8), channel_id=1, source_target_pairs={{0,16},{4,20},{8,24},{12,28},{16,0},{20,4},{24,8},{28,12},{1,17},{... | collective-permute-start | bytes 602120 | tf_op jit(solution)/shard_map/ppermute | solution.py:436
  5.2 5.2 %collective-permute-start.1 = (bf16[128,128]{1,0:T(8,128)(2,1)S(1)}, bf16[128,128]{1,0:T(8,128)(2,1)S(1)}, u32[]{:S(2)}, u32[]{:S(2)}) collective-permute-start(bf16[128,128]{1,0:T(8,128)(2,1)S(1)} %get-tuple-element.64.refs_13_), channel_id=1, source_target_pairs={{0,20},{4,16},{8,28},{12,24},{16,4},{20,0},{24,12},{28,8},{1,21},{... | collective-permute-start | bytes 98312 | tf_op jit(solution)/shard_map/ppermute | solution.py:436
  6.8 3.9 %collective-permute-start = (bf16[128,128]{1,0:T(8,128)(2,1)S(1)}, bf16[128,128]{1,0:T(8,128)(2,1)S(1)}, u32[]{:S(2)}, u32[]{:S(2)}) collective-permute-start(bf16[128,128]{1,0:T(8,128)(2,1)S(1)} %get-tuple-element.64.refs_13_), channel_id=1, source_target_pairs={{0,4},{4,0},{8,12},{12,8},{16,20},{20,16},{24,28},{28,24},{1,5},{5... | collective-permute-start | bytes 98312 | tf_op jit(solution)/shard_map/ppermute | solution.py:436
  6.8 0.7 %copy-start = (f32[8]{0:T(128)S(1)}, f32[8]{0:T(128)}, u32[]{:S(2)}) copy-start(f32[8]{0:T(128)} %alog.1) | copy-start | bytes 100
  6.8 0.7 %copy-start.1 = (f32[8]{0:T(128)S(1)}, f32[8]{0:T(128)}, u32[]{:S(2)}) copy-start(f32[8]{0:T(128)} %bias.1) | copy-start | bytes 100
  6.8 0.7 %copy-start.2 = (f32[8]{0:T(128)S(1)}, f32[8]{0:T(128)}, u32[]{:S(2)}) copy-start(f32[8]{0:T(128)} %skip.1) | copy-start | bytes 100
  12.5 5.0 %collective-permute-start.3 = (bf16[512,128]{1,0:T(8,128)(2,1)S(1)}, bf16[512,128]{1,0:T(8,128)(2,1)S(1)}, u32[]{:S(2)}, u32[]{:S(2)}) collective-permute-start(bf16[512,128]{1,0:T(8,128)(2,1)S(1)} %get-tuple-element.78), channel_id=1, source_target_pairs={{0,4},{4,0},{8,12},{12,8},{16,20},{20,16},{24,28},{28,24},{1,5},{5... | collective-permute-start | bytes 393224 | tf_op jit(solution)/shard_map/ppermute | solution.py:436
  15.6 4.8 %collective-permute-start.6 = (f32[8,128]{1,0:T(8,128)S(1)}, f32[8,128]{1,0:T(8,128)S(1)}, u32[]{:S(2)}, u32[]{:S(2)}) collective-permute-start(f32[8,128]{1,0:T(8,128)S(1)} %get-tuple-element.90), channel_id=1, source_target_pairs={{0,3},{1,2},{2,1},{3,0},{4,7},{5,6},{6,5},{7,4},{8,11},{9,10},{10,... | collective-permute-start | bytes 12296 | tf_op jit(solution)/shard_map/ppermute | solution.py:539
  15.6 4.8 %collective-permute-start.5 = (f32[8,128]{1,0:T(8,128)S(1)}, f32[8,128]{1,0:T(8,128)S(1)}, u32[]{:S(2)}, u32[]{:S(2)}) collective-permute-start(f32[8,128]{1,0:T(8,128)S(1)} %get-tuple-element.90), channel_id=1, source_target_pairs={{0,2},{1,3},{2,0},{3,1},{4,6},{5,7},{6,4},{7,5},{8,10},{9,11},{10,... | collective-permute-start | bytes 12296 | tf_op jit(solution)/shard_map/ppermute | solution.py:539
  17.1 3.3 %collective-permute-start.4 = (f32[8,128]{1,0:T(8,128)S(1)}, f32[8,128]{1,0:T(8,128)S(1)}, u32[]{:S(2)}, u32[]{:S(2)}) collective-permute-start(f32[8,128]{1,0:T(8,128)S(1)} %get-tuple-element.90), channel_id=1, source_target_pairs={{0,1},{1,0},{2,3},{3,2},{4,5},{5,4},{6,7},{7,6},{8,9},{9,8},{10,11... | collective-permute-start | bytes 12296 | tf_op jit(solution)/shard_map/ppermute | solution.py:539
  17.6 5.7 %collective-permute-start.7 = (bf16[256,128]{1,0:T(8,128)(2,1)S(1)}, bf16[256,128]{1,0:T(8,128)(2,1)S(1)}, u32[]{:S(2)}, u32[]{:S(2)}) collective-permute-start(bf16[256,128]{1,0:T(8,128)(2,1)S(1)} %add_convert_fusion.mine), channel_id=1, source_target_pairs={{0,8},{4,12},{8,0},{12,4},{16,24},{20,28},{24,16},{28,20},{1,9},{5... | collective-permute-start | bytes 196616 | tf_op jit(solution)/shard_map/ppermute | solution.py:436
  20.5 4.0 %collective-permute-start.8 = (bf16[144,128]{1,0:T(8,128)(2,1)S(1)}, bf16[144,128]{1,0:T(8,128)(2,1)S(1)}, u32[]{:S(2)}, u32[]{:S(2)}) collective-permute-start(bf16[144,128]{1,0:T(8,128)(2,1)S(1)} %pad_maximum_fusion), channel_id=1, source_target_pairs={{0,16},{4,20},{8,24},{12,28},{16,0},{20,4},{24,8},{28,12},{1,17},{... | collective-permute-start | bytes 110600 | tf_op jit(solution)/shard_map/ppermute | solution.py:436

commit v6 on v5

--- a/solution.py
+++ b/solution.py
@@ -44,6 +44,13 @@
     for m in range(1, heads):
         out = jnp.where(at == m, ref[m], out)
     return out
+
+
+def upright(vector, width):
+    heads = vector.shape[0]
+    square = jnp.broadcast_to(vector[...].reshape(1, heads), (heads, heads))
+    square = jnp.where(iota((heads, heads), 0) == iota((heads, heads), 1), square, 0.0)
+    return jnp.broadcast_to(jnp.sum(square, axis=1, keepdims=True), (heads, width))
 
 
 def rates(raw, bias, alog):
@@ -119,7 +126,7 @@
     heads, rows = raw.shape[1:]
     wide, states = gate.shape[2], read.shape[2]
     half = key.shape[1]
-    step, _, cum = rates(raw[0], column(bias, rows), column(alog, rows))
+    step, _, cum = rates(raw[0], upright(bias, rows), upright(alog, rows))
     decay = widen(jnp.exp(-cum), wide // heads)
     to_end = jnp.exp(cum - cum[:, rows - 1 :]) * step
     whole = jnp.broadcast_to(jnp.exp(-cum[:, rows - 1 :]), (heads, rows))
@@ -300,15 +307,15 @@
     grad_read = dot(grad_cross_t, write_b, TN) + dot(grad_mixed * decay_in, entry_b, NT)
     sent[slots * head_dim : slots * head_dim + rows] = grad_write.astype(BF16)
     sent[slots * head_dim + rows :] = grad_read.astype(BF16)
-    products = (
-        inner * grad_scaled,
-        inner * from_exit,
-        grad_mixed * from_entry,
-        grad_mixed * inner,
-        exit_t * entry_t,
-    )
+    products = (inner * grad_scaled, inner * from_exit, grad_mixed * from_entry)
     for i, product in enumerate(products):
         products_out[i * rows : (i + 1) * rows] = product.astype(BF16)
+    totals = [
+        jnp.sum(grad_mixed * inner, axis=0, keepdims=True),
+        jnp.sum(exit_t * entry_t, axis=0, keepdims=True),
+    ]
+    totals = jnp.concatenate(totals + [jnp.zeros((6, wide), F32)], axis=0)
+    products_out[len(products) * rows :] = jnp.concatenate(parts_of(totals, 2), axis=0)
 
 
 def rates_kernel(products, scaled, halves, back, tables, grad_raw, params):
@@ -335,8 +342,9 @@
     grad_step = sums[:, :rows]
     exit_sum = sums[:, rows : 2 * rows] * step
     entry_sum = sums[:, 2 * rows : 3 * rows]
-    skip_sum = sums[:, 3 * rows : 4 * rows]
-    carry_sum = jnp.sum(sums[:, 4 * rows :], axis=1, keepdims=True) * jnp.exp(-cum[:, rows - 1 :])
+    totals = sums[:, 3 * rows : 3 * rows + 8] + sums[:, 3 * rows + 8 :]
+    skip_sum = jnp.where(iota((heads, rows), 1) == 0, totals[:, :1], 0.0)
+    carry_sum = totals[:, 1:2] * jnp.exp(-cum[:, rows - 1 :])
     grad_rate = -(
         jnp.concatenate(rate_rows, axis=0)
         + dot_flags([entry_sum, exit_sum], [lower, strict])
@@ -470,8 +478,7 @@
         in_specs=[HBM] * len(sources),
         out_specs=(VMEM,) * (2 + len(kept_here)),
         scratch_shapes=[
-            pltpu.SMEM(a.shape, a.dtype) if a.ndim == 1 else pltpu.VMEM(a.shape, a.dtype)
-            for a in sources[len(kept_here) :]
+            pltpu.VMEM(a.shape, a.dtype) for a in sources[len(kept_here) :]
         ]
         + [pltpu.SemaphoreType.DMA((len(sources),))],
         compiler_params=PARAMS,
@@ -502,7 +509,7 @@
             shape((head_dim, slots * rows), BF16),
             wide_b,
             wide_f,
-            shape((5 * rows, wide), BF16),
+            shape((3 * rows + 16, wide), BF16),
         ),
         (
             query_rows,

time: 25.4 us -> 25.4 us (level)
  no operation moved by 1% of the time
where the time goes in v6:
time: 25.4 us; the launch traced here: 25.2 us
  starting transfers between devices  12.8 us (50%)
  Pallas kernels  8.03 us (32%)
  waiting for transfers between devices  2.88 us (11%)
  between operations  0.72 us (3%)
  local copies, waits for them, and re-layouts  0.68 us (3%)
    ppermute x6, starting transfers between devices, swap(): return lax.ppermute(array, ('seq', 'tp'), pairs)  10.9 us
    pallas_call x6, Pallas kernels, call(): pl.pallas_call(kernel, out_shape=outs, in_specs=[(specs or {}).get(i, VME...  6.51 us
    ppermute x6, waiting for transfers between devices, swap(): return lax.ppermute(array, ('seq', 'tp'), pairs)  2.87 us
    ppermute x3, starting transfers between devices, body(): lax.ppermute(params, 'dp', flip('dp', k * reach))  1.86 us
    pallas_call x1, Pallas kernels, body(): pl.pallas_call(share_kernel, out_shape=(shape((head_dim, rows), BF16), sh...  1.52 us
    unnamed x6, local copies, waits for them, and re-layouts  0.68 us
  transfers between devices with their start and end apart: 9, of which 6 were waited for; matrix products, arithmetic and copies ran while one was open for 0% of the time, Pallas kernels for 17%

profile of v6, /device:TPU:0, one launch (start us, length us, event | category | flops | bytes accessed | tf_op | source)
XLA Modules:
  0.0 25.2 jit_solution(3973458071101908470)
XLA Ops:
  0.6 1.5 %shard_map.186 = (bf16[128,128]{1,0:T(8,128)(2,1)S(1)}, bf16[1,784,128]{2,1,0:T(8,128)(2,1)S(1)}, f32[1,8,128]{2,1,0:T(8,128)S(1)}, bf16[1,128,512]{2,1,0:T(8,12...) custom-call(f32[1,8,128]{2,1,0:T(8,128)} %refs_0_.1, ...), custom_call_target="tpu_custom_call" | custom-call | tf_op jit(solution)/shard_map/pallas_call | solution.py:471
  2.2 3.0 %collective-permute-start.2 = (bf16[784,128]{1,0:T(8,128)(2,1)S(1)}, bf16[784,128]{1,0:T(8,128)(2,1)S(1)}, u32[]{:S(2)}, u32[]{:S(2)}) collective-permute-start(bf16[784,128]{1,0:T(8,128)(2,1)S(1)} %bitcast.8), channel_id=1, source_target_pairs={{0,16},{4,20},{8,24},{12,28},{16,0},{20,4},{24,8},{28,12},{1,17},{... | collective-permute-start | bytes 602120 | tf_op jit(solution)/shard_map/ppermute | solution.py:444
  5.2 1.5 %collective-permute-start.1 = (bf16[128,128]{1,0:T(8,128)(2,1)S(1)}, bf16[128,128]{1,0:T(8,128)(2,1)S(1)}, u32[]{:S(2)}, u32[]{:S(2)}) collective-permute-start(bf16[128,128]{1,0:T(8,128)(2,1)S(1)} %get-tuple-element.64.refs_13_), channel_id=1, source_target_pairs={{0,20},{4,16},{8,28},{12,24},{16,4},{20,0},{24,12},{28,8},{1,21},{... | collective-permute-start | bytes 98312 | tf_op jit(solution)/shard_map/ppermute | solution.py:444
  6.7 0.1 collective-permute-start
  6.8 0.0 copy-start
  6.8 0.0 copy-start.1
  6.8 0.0 copy-start.2
  6.8 0.6 %copy-done = f32[8]{0:T(128)S(1)} copy-done((f32[8]{0:T(128)S(1)}, f32[8]{0:T(128)}, u32[]{:S(2)}) %copy-start) | copy-done | bytes 56
  7.4 0.0 copy-done.1
  7.5 0.0 copy-done.2
  7.5 1.4 %shard_map.187 = (f32[128,512]{1,0:T(8,128)S(1)}, f32[128,512]{1,0:T(8,128)S(1)}, f32[128,512]{1,0:T(8,128)S(1)}, f32[128,512]{1,0:T(8,128)S(1)}, f32[128,512]{1...) custom-call(bf16[1,128,512]{2,1,0:T(8,128)(2,1)S(1)} %get-tuple-elem, ...), custom_call_target="tpu_custom_call" | custom-call | tf_op jit(solution)/shard_map/pallas_call | solution.py:427
  8.9 1.5 %collective-permute-done.1.refs_12_ = bf16[128,128]{1,0:T(8,128)(2,1)S(1)} collective-permute-done((bf16[128,128]{1,0:T(8,128)(2,1)S(1)}, bf16[128,128]{1,0:T(8,128)(2,1)S(1)}, u32[]{:S(2)}, u32[]{:S(2)}) %collective-permute-start.1) | collective-permute-done | bytes 32800 | tf_op jit(solution)/shard_map/ppermute | solution.py:444
  10.4 0.3 %collective-permute-done.refs_3_ = bf16[128,128]{1,0:T(8,128)(2,1)S(1)} collective-permute-done((bf16[128,128]{1,0:T(8,128)(2,1)S(1)}, bf16[128,128]{1,0:T(8,128)(2,1)S(1)}, u32[]{:S(2)}, u32[]{:S(2)}) %collective-permute-start) | collective-permute-done | bytes 32800 | tf_op jit(solution)/shard_map/ppermute | solution.py:444
  10.6 0.3 %collective-permute-done.2.refs_14_ = bf16[784,128]{1,0:T(8,128)(2,1)S(1)} collective-permute-done((bf16[784,128]{1,0:T(8,128)(2,1)S(1)}, bf16[784,128]{1,0:T(8,128)(2,1)S(1)}, u32[]{:S(2)}, u32[]{:S(2)}) %collective-permute-start.2) | collective-permute-done | bytes 200736 | tf_op jit(solution)/shard_map/ppermute | solution.py:444
  10.9 1.6 %shard_map.188 = (bf16[2,128,128]{2,1,0:T(8,128)(2,1)S(1)}, bf16[512,128]{1,0:T(8,128)(2,1)S(1)}, bf16[512,256]{1,0:T(8,128)(2,1)S(1)}, bf16[128,256]{1,0:T(8,12...) custom-call(bf16[1,128,512]{2,1,0:T(8,128)(2,1)S(1)} %get-tuple-element.63.refs_0_, ...), custom_call_target="tpu_custom_call" | custom-call | tf_op jit(solution)/shard_map/pallas_call | solution.py:427
  12.5 1.9 %collective-permute-start.3 = (bf16[512,128]{1,0:T(8,128)(2,1)S(1)}, bf16[512,128]{1,0:T(8,128)(2,1)S(1)}, u32[]{:S(2)}, u32[]{:S(2)}) collective-permute-start(bf16[512,128]{1,0:T(8,128)(2,1)S(1)} %get-tuple-element.78), channel_id=1, source_target_pairs={{0,4},{4,0},{8,12},{12,8},{16,20},{20,16},{24,28},{28,24},{1,5},{5... | collective-permute-start | bytes 393224 | tf_op jit(solution)/shard_map/ppermute | solution.py:444
  14.3 1.2 %shard_map.189 = (f32[1,8,128]{2,1,0:T(8,128)}, f32[8,128]{1,0:T(8,128)S(1)}) custom-call(bf16[400,512]{1,0:T(8,128)(2,1)S(1)} %get-tuple-element.79.products, bf16[128,512]{1,0:T(8,128)(2,1)S(1)} %get-tuple-element.74.scaled.refs_1_, bf16[1024,128]{1,0:T(8,128)(2,1)S(1)} %get-tuple-element.71.refs_10_.halves, f32[1024,128]{1,0:T(8,128)S(1)} %get-tuple-element.80.back, ...), custom_call_target="tpu_custom_call" | custom-call | tf_op jit(solution)/shard_map/pallas_call | solution.py:427
  15.6 0.0 collective-permute-start.6
  15.6 1.5 %collective-permute-start.5 = (f32[8,128]{1,0:T(8,128)S(1)}, f32[8,128]{1,0:T(8,128)S(1)}, u32[]{:S(2)}, u32[]{:S(2)}) collective-permute-start(f32[8,128]{1,0:T(8,128)S(1)} %get-tuple-element.90), channel_id=1, source_target_pairs={{0,2},{1,3},{2,0},{3,1},{4,6},{5,7},{6,4},{7,5},{8,10},{9,11},{10,... | collective-permute-start | bytes 12296 | tf_op jit(solution)/shard_map/ppermute | solution.py:546
  17.1 0.3 %collective-permute-start.4 = (f32[8,128]{1,0:T(8,128)S(1)}, f32[8,128]{1,0:T(8,128)S(1)}, u32[]{:S(2)}, u32[]{:S(2)}) collective-permute-start(f32[8,128]{1,0:T(8,128)S(1)} %get-tuple-element.90), channel_id=1, source_target_pairs={{0,1},{1,0},{2,3},{3,2},{4,5},{5,4},{6,7},{7,6},{8,9},{9,8},{10,11... | collective-permute-start | bytes 12296 | tf_op jit(solution)/shard_map/ppermute | solution.py:546
  17.4 0.1 collective-permute-done.3.refs_2_
  17.5 2.9 %collective-permute-start.7 = (bf16[256,128]{1,0:T(8,128)(2,1)S(1)}, bf16[256,128]{1,0:T(8,128)(2,1)S(1)}, u32[]{:S(2)}, u32[]{:S(2)}) collective-permute-start(bf16[256,128]{1,0:T(8,128)(2,1)S(1)} %add_convert_fusion.mine), channel_id=1, source_target_pairs={{0,8},{4,12},{8,0},{12,4},{16,24},{20,28},{24,16},{28,20},{1,9},{5... | collective-permute-start | bytes 196616 | tf_op jit(solution)/shard_map/ppermute | solution.py:444
  20.4 0.0 collective-permute-done.6
  20.4 0.0 collective-permute-done.5
  20.4 0.0 collective-permute-done.4
  20.5 1.6 %collective-permute-start.8 = (bf16[144,128]{1,0:T(8,128)(2,1)S(1)}, bf16[144,128]{1,0:T(8,128)(2,1)S(1)}, u32[]{:S(2)}, u32[]{:S(2)}) collective-permute-start(bf16[144,128]{1,0:T(8,128)(2,1)S(1)} %pad_maximum_fusion), channel_id=1, source_target_pairs={{0,16},{4,20},{8,24},{12,28},{16,0},{20,4},{24,8},{28,12},{1,17},{... | collective-permute-start | bytes 110600 | tf_op jit(solution)/shard_map/ppermute | solution.py:444
  22.1 1.0 %shard_map.190 = (f32[1,128,512]{2,1,0:T(8,128)}, f32[1,128,512]{2,1,0:T(8,128)}) custom-call(bf16[128,1024]{1,0:T(8,128)(2,1)S(1)} %get-tuple-element.62.refs_0_, bf16[128,512]{1,0:T(8,128)(2,1)S(1)} %get-tuple-element.74.scaled.refs_1_, f32[128,512]{1,0:T(8,128)S(1)} %get-tuple-element.75.refs_2_, f32[128,512]{1,0:T(8,128)S(1)} %get-tuple-element.76.refs_3_, ...), custom_call_target="tpu_custom_call" | custom-call | tf_op jit(solution)/shard_map/pallas_call | solution.py:427
  23.1 0.1 collective-permute-done.7.other
  23.2 0.7 %shard_map.191 = (f32[1,128,128]{2,1,0:T(8,128)}, f32[1,128,128]{2,1,0:T(8,128)}) custom-call(bf16[256,128]{1,0:T(8,128)(2,1)S(1)} %add_convert_fusion.mine, bf16[256,128]{1,0:T(8,128)(2,1)S(1)} %collective-permute-done.7.other), custom_call_target="tpu_custom_call" | custom-call | tf_op jit(solution)/shard_map/pallas_call | solution.py:427
  23.8 0.7 %collective-permute-done.8.refs_0_ = bf16[144,128]{1,0:T(8,128)(2,1)S(1)} collective-permute-done((bf16[144,128]{1,0:T(8,128)(2,1)S(1)}, bf16[144,128]{1,0:T(8,128)(2,1)S(1)}, u32[]{:S(2)}, u32[]{:S(2)}) %collective-permute-start.8) | collective-permute-done | bytes 36896 | tf_op jit(solution)/shard_map/ppermute | solution.py:444
  24.5 0.6 %shard_map.192 = (f32[1,64,128]{2,1,0:T(8,128)}, f32[1,64,128]{2,1,0:T(8,128)}, f32[8]{0:T(128)}, f32[8]{0:T(128)}, f32[8]{0:T(128)}) custom-call(bf16[144,128]{1,0:T(8,128)(2,1)S(1)} %collective-permute-done.8.refs_0_, bf16[2,128,128]{2,1,0:T(8,128)(2,1)S(1)} %get-tuple-element.89.refs_1_, bf16[512,128]{1,0:T(8,128)(2,1)S(1)} %collective-permute-done.3.refs_2_, ...), custom_call_target="tpu_custom_call" | custom-call | tf_op jit(solution)/shard_map/pallas_call | solution.py:427
  (6 shorter events, 0.1 us)
Async XLA Ops:
  2.2 8.7 %collective-permute-start.2 = (bf16[784,128]{1,0:T(8,128)(2,1)S(1)}, bf16[784,128]{1,0:T(8,128)(2,1)S(1)}, u32[]{:S(2)}, u32[]{:S(2)}) collective-permute-start(bf16[784,128]{1,0:T(8,128)(2,1)S(1)} %bitcast.8), channel_id=1, source_target_pairs={{0,16},{4,20},{8,24},{12,28},{16,0},{20,4},{24,8},{28,12},{1,17},{... | collective-permute-start | bytes 602120 | tf_op jit(solution)/shard_map/ppermute | solution.py:444
  5.2 5.2 %collective-permute-start.1 = (bf16[128,128]{1,0:T(8,128)(2,1)S(1)}, bf16[128,128]{1,0:T(8,128)(2,1)S(1)}, u32[]{:S(2)}, u32[]{:S(2)}) collective-permute-start(bf16[128,128]{1,0:T(8,128)(2,1)S(1)} %get-tuple-element.64.refs_13_), channel_id=1, source_target_pairs={{0,20},{4,16},{8,28},{12,24},{16,4},{20,0},{24,12},{28,8},{1,21},{... | collective-permute-start | bytes 98312 | tf_op jit(solution)/shard_map/ppermute | solution.py:444
  6.7 3.9 %collective-permute-start = (bf16[128,128]{1,0:T(8,128)(2,1)S(1)}, bf16[128,128]{1,0:T(8,128)(2,1)S(1)}, u32[]{:S(2)}, u32[]{:S(2)}) collective-permute-start(bf16[128,128]{1,0:T(8,128)(2,1)S(1)} %get-tuple-element.64.refs_13_), channel_id=1, source_target_pairs={{0,4},{4,0},{8,12},{12,8},{16,20},{20,16},{24,28},{28,24},{1,5},{5... | collective-permute-start | bytes 98312 | tf_op jit(solution)/shard_map/ppermute | solution.py:444
  6.8 0.7 %copy-start = (f32[8]{0:T(128)S(1)}, f32[8]{0:T(128)}, u32[]{:S(2)}) copy-start(f32[8]{0:T(128)} %alog.1) | copy-start | bytes 100
  6.8 0.7 %copy-start.1 = (f32[8]{0:T(128)S(1)}, f32[8]{0:T(128)}, u32[]{:S(2)}) copy-start(f32[8]{0:T(128)} %bias.1) | copy-start | bytes 100
  6.8 0.7 %copy-start.2 = (f32[8]{0:T(128)S(1)}, f32[8]{0:T(128)}, u32[]{:S(2)}) copy-start(f32[8]{0:T(128)} %skip.1) | copy-start | bytes 100
  12.5 5.0 %collective-permute-start.3 = (bf16[512,128]{1,0:T(8,128)(2,1)S(1)}, bf16[512,128]{1,0:T(8,128)(2,1)S(1)}, u32[]{:S(2)}, u32[]{:S(2)}) collective-permute-start(bf16[512,128]{1,0:T(8,128)(2,1)S(1)} %get-tuple-element.78), channel_id=1, source_target_pairs={{0,4},{4,0},{8,12},{12,8},{16,20},{20,16},{24,28},{28,24},{1,5},{5... | collective-permute-start | bytes 393224 | tf_op jit(solution)/shard_map/ppermute | solution.py:444
  15.6 4.9 %collective-permute-start.6 = (f32[8,128]{1,0:T(8,128)S(1)}, f32[8,128]{1,0:T(8,128)S(1)}, u32[]{:S(2)}, u32[]{:S(2)}) collective-permute-start(f32[8,128]{1,0:T(8,128)S(1)} %get-tuple-element.90), channel_id=1, source_target_pairs={{0,3},{1,2},{2,1},{3,0},{4,7},{5,6},{6,5},{7,4},{8,11},{9,10},{10,... | collective-permute-start | bytes 12296 | tf_op jit(solution)/shard_map/ppermute | solution.py:546
  15.6 4.9 %collective-permute-start.5 = (f32[8,128]{1,0:T(8,128)S(1)}, f32[8,128]{1,0:T(8,128)S(1)}, u32[]{:S(2)}, u32[]{:S(2)}) collective-permute-start(f32[8,128]{1,0:T(8,128)S(1)} %get-tuple-element.90), channel_id=1, source_target_pairs={{0,2},{1,3},{2,0},{3,1},{4,6},{5,7},{6,4},{7,5},{8,10},{9,11},{10,... | collective-permute-start | bytes 12296 | tf_op jit(solution)/shard_map/ppermute | solution.py:546
  17.1 3.3 %collective-permute-start.4 = (f32[8,128]{1,0:T(8,128)S(1)}, f32[8,128]{1,0:T(8,128)S(1)}, u32[]{:S(2)}, u32[]{:S(2)}) collective-permute-start(f32[8,128]{1,0:T(8,128)S(1)} %get-tuple-element.90), channel_id=1, source_target_pairs={{0,1},{1,0},{2,3},{3,2},{4,5},{5,4},{6,7},{7,6},{8,9},{9,8},{10,11... | collective-permute-start | bytes 12296 | tf_op jit(solution)/shard_map/ppermute | solution.py:546
  17.5 5.6 %collective-permute-start.7 = (bf16[256,128]{1,0:T(8,128)(2,1)S(1)}, bf16[256,128]{1,0:T(8,128)(2,1)S(1)}, u32[]{:S(2)}, u32[]{:S(2)}) collective-permute-start(bf16[256,128]{1,0:T(8,128)(2,1)S(1)} %add_convert_fusion.mine), channel_id=1, source_target_pairs={{0,8},{4,12},{8,0},{12,4},{16,24},{20,28},{24,16},{28,20},{1,9},{5... | collective-permute-start | bytes 196616 | tf_op jit(solution)/shard_map/ppermute | solution.py:444
  20.5 4.0 %collective-permute-start.8 = (bf16[144,128]{1,0:T(8,128)(2,1)S(1)}, bf16[144,128]{1,0:T(8,128)(2,1)S(1)}, u32[]{:S(2)}, u32[]{:S(2)}) collective-permute-start(bf16[144,128]{1,0:T(8,128)(2,1)S(1)} %pad_maximum_fusion), channel_id=1, source_target_pairs={{0,16},{4,20},{8,24},{12,28},{16,0},{20,4},{24,8},{28,12},{1,17},{... | collective-permute-start | bytes 110600 | tf_op jit(solution)/shard_map/ppermute | solution.py:444

commit v7 on v6

--- a/solution.py
+++ b/solution.py
@@ -26,11 +26,33 @@
     return parts
 
 
-def dot_flags(arrays, flags, count=3):
-    split_up = [parts_of(a, count) for a in arrays]
-    left = [parts[i] for i in range(count) for parts in split_up]
-    right = jnp.concatenate([jnp.where(f, 1.0, 0.0) for f in flags] * count, axis=0)
-    return dot(jnp.concatenate(left, axis=1), right)
+PARTS = 3
+
+
+def flag_rows(*flags):
+    return jnp.concatenate([jnp.where(f, 1.0, 0.0).astype(BF16) for f in flags] * PARTS, axis=0)
+
+
+def dot_flags(arrays, rows):
+    split_up = [parts_of(a, PARTS) for a in arrays]
+    left = [parts[i] for i in range(PARTS) for parts in split_up]
+    return dot(jnp.concatenate(left, axis=1), rows)
+
+
+def over(index, size):
+    if size & (size - 1):
+        return index // size
+    return lax.shift_right_logical(index, size.bit_length() - 1)
+
+
+def upto_rows(rows):
+    return flag_rows(iota((rows, rows), 0) <= iota((rows, rows), 1))
+
+
+def head_rows(heads, channels):
+    shape = (heads, heads * channels)
+    one = jnp.where(over(iota(shape, 1), channels) == iota(shape, 0), 1.0, 0.0)
+    return jnp.concatenate([one.astype(BF16)] * PARTS, axis=0)
 
 
 def iota(shape, axis):
@@ -53,23 +75,21 @@
     return jnp.broadcast_to(jnp.sum(square, axis=1, keepdims=True), (heads, width))
 
 
-def rates(raw, bias, alog):
-    rows = raw.shape[1]
+def rates(raw, bias, alog, upto):
     shifted = raw + bias
     step = jnp.maximum(shifted, 0.0) + jnp.log1p(jnp.exp(-jnp.abs(shifted)))
     rate = step * jnp.exp(alog)
-    return step, rate, dot_flags([rate], [iota((rows, rows), 0) <= iota((rows, rows), 1)])
+    return step, rate, dot_flags([rate], upto)
 
 
 def spread(cols, m, width):
     return jnp.broadcast_to(cols[:, m : m + 1], (cols.shape[0], width))
 
 
-def widen(factors, channels):
-    heads = factors.shape[0]
-    shape = (3 * heads, heads * channels)
-    pick = (iota(shape, 1) // channels == iota(shape, 0) % heads).astype(BF16)
-    return dot(jnp.concatenate(parts_of(factors, 3), axis=0), pick, TN)
+def widen(factors, channels, picked=None):
+    if picked is None:
+        picked = head_rows(factors.shape[0], channels)
+    return dot(jnp.concatenate(parts_of(factors, PARTS), axis=0), picked, TN)
 
 
 def stack(wide, width):
@@ -120,14 +140,15 @@
     ]
     for place in (0, 6, 7, 1, 2, 3, 4, 8, 9, 5):
         copies[place].start()
-    for place in (0, 6, 7):
-        copies[place].wait()
     here = lax.axis_index("seq")
     heads, rows = raw.shape[1:]
     wide, states = gate.shape[2], read.shape[2]
     half = key.shape[1]
-    step, _, cum = rates(raw[0], upright(bias, rows), upright(alog, rows))
-    decay = widen(jnp.exp(-cum), wide // heads)
+    upto, picked = upto_rows(rows), head_rows(heads, wide // heads)
+    for place in (0, 6, 7):
+        copies[place].wait()
+    step, _, cum = rates(raw[0], upright(bias, rows), upright(alog, rows), upto)
+    decay = widen(jnp.exp(-cum), wide // heads, picked)
     to_end = jnp.exp(cum - cum[:, rows - 1 :]) * step
     whole = jnp.broadcast_to(jnp.exp(-cum[:, rows - 1 :]), (heads, rows))
     tail = jnp.concatenate([to_end, whole], axis=0).astype(BF16)
@@ -160,10 +181,10 @@
     channels = wide // heads
     pair = 2 * channels
     alog_c, bias_c = column(alog, rows), column(bias, rows)
-    step, rate, cum = rates(raw[0], bias_c, alog_c)
+    step, rate, cum = rates(raw[0], bias_c, alog_c, upto_rows(rows))
     for i, table in enumerate((step, rate, cum, jnp.exp(alog_c), jax.nn.sigmoid(raw[0] + bias_c))):
         rates_out[i * heads : (i + 1) * heads] = table
-    head_of = iota(skip_out.shape, 1) // channels
+    head_of = over(iota(skip_out.shape, 1), channels)
     skip_w = jnp.full(skip_out.shape, skip[0], F32)
     for m in range(1, heads):
         skip_w = jnp.where(head_of == m, skip[m], skip_w)
@@ -337,7 +358,7 @@
         jnp.sum(jnp.where(strict, later[m * rows : (m + 1) * rows], 0.0), axis=0, keepdims=True)
         for m in range(heads)
     ]
-    pick = (iota((heads, wide), 1) // channels == iota((heads, wide), 0)).astype(BF16)
+    pick = (over(iota((heads, wide), 1), channels) == iota((heads, wide), 0)).astype(BF16)
     sums = dot(pick, products[...], NT)
     grad_step = sums[:, :rows]
     exit_sum = sums[:, rows : 2 * rows] * step
@@ -347,7 +368,7 @@
     carry_sum = totals[:, 1:2] * jnp.exp(-cum[:, rows - 1 :])
     grad_rate = -(
         jnp.concatenate(rate_rows, axis=0)
-        + dot_flags([entry_sum, exit_sum], [lower, strict])
+        + dot_flags([entry_sum, exit_sum], flag_rows(lower, strict))
         + carry_sum
     )
     grad_shift = (grad_step + grad_rate * grow) * slope

time: 25.4 us -> 25.4 us (level)
  no operation moved by 1% of the time
where the time goes in v7:
time: 25.4 us; the launch traced here: 25.2 us
  starting transfers between devices  12.8 us (50%)
  Pallas kernels  8.04 us (32%)
  waiting for transfers between devices  2.88 us (11%)
  between operations  0.72 us (3%)
  local copies, waits for them, and re-layouts  0.68 us (3%)
    ppermute x6, starting transfers between devices, swap(): return lax.ppermute(array, ('seq', 'tp'), pairs)  10.9 us
    pallas_call x6, Pallas kernels, call(): pl.pallas_call(kernel, out_shape=outs, in_specs=[(specs or {}).get(i, VME...  6.51 us
    ppermute x6, waiting for transfers between devices, swap(): return lax.ppermute(array, ('seq', 'tp'), pairs)  2.87 us
    ppermute x3, starting transfers between devices, body(): lax.ppermute(params, 'dp', flip('dp', k * reach))  1.86 us
    pallas_call x1, Pallas kernels, body(): pl.pallas_call(share_kernel, out_shape=(shape((head_dim, rows), BF16), sh...  1.52 us
    unnamed x6, local copies, waits for them, and re-layouts  0.68 us
  transfers between devices with their start and end apart: 9, of which 6 were waited for; matrix products, arithmetic and copies ran while one was open for 0% of the time, Pallas kernels for 17%

profile of v7, /device:TPU:0, one launch (start us, length us, event | category | flops | bytes accessed | tf_op | source)
XLA Modules:
  0.0 25.2 jit_solution(14006196823760124179)
XLA Ops:
  0.6 1.5 %shard_map.186 = (bf16[128,128]{1,0:T(8,128)(2,1)S(1)}, bf16[1,784,128]{2,1,0:T(8,128)(2,1)S(1)}, f32[1,8,128]{2,1,0:T(8,128)S(1)}, bf16[1,128,512]{2,1,0:T(8,12...) custom-call(f32[1,8,128]{2,1,0:T(8,128)} %refs_0_.1, ...), custom_call_target="tpu_custom_call" | custom-call | tf_op jit(solution)/shard_map/pallas_call | solution.py:492
  2.2 3.0 %collective-permute-start.2 = (bf16[784,128]{1,0:T(8,128)(2,1)S(1)}, bf16[784,128]{1,0:T(8,128)(2,1)S(1)}, u32[]{:S(2)}, u32[]{:S(2)}) collective-permute-start(bf16[784,128]{1,0:T(8,128)(2,1)S(1)} %bitcast.8), channel_id=1, source_target_pairs={{0,16},{4,20},{8,24},{12,28},{16,0},{20,4},{24,8},{28,12},{1,17},{... | collective-permute-start | bytes 602120 | tf_op jit(solution)/shard_map/ppermute | solution.py:465
  5.2 1.5 %collective-permute-start.1 = (bf16[128,128]{1,0:T(8,128)(2,1)S(1)}, bf16[128,128]{1,0:T(8,128)(2,1)S(1)}, u32[]{:S(2)}, u32[]{:S(2)}) collective-permute-start(bf16[128,128]{1,0:T(8,128)(2,1)S(1)} %get-tuple-element.64.refs_13_), channel_id=1, source_target_pairs={{0,20},{4,16},{8,28},{12,24},{16,4},{20,0},{24,12},{28,8},{1,21},{... | collective-permute-start | bytes 98312 | tf_op jit(solution)/shard_map/ppermute | solution.py:465
  6.7 0.1 collective-permute-start
  6.8 0.0 copy-start
  6.8 0.0 copy-start.1
  6.8 0.0 copy-start.2
  6.8 0.6 %copy-done = f32[8]{0:T(128)S(1)} copy-done((f32[8]{0:T(128)S(1)}, f32[8]{0:T(128)}, u32[]{:S(2)}) %copy-start) | copy-done | bytes 56
  7.4 0.0 copy-done.1
  7.5 0.0 copy-done.2
  7.5 1.4 %shard_map.187 = (f32[128,512]{1,0:T(8,128)S(1)}, f32[128,512]{1,0:T(8,128)S(1)}, f32[128,512]{1,0:T(8,128)S(1)}, f32[128,512]{1,0:T(8,128)S(1)}, f32[128,512]{1...) custom-call(bf16[1,128,512]{2,1,0:T(8,128)(2,1)S(1)} %get-tuple-elem, ...), custom_call_target="tpu_custom_call" | custom-call | tf_op jit(solution)/shard_map/pallas_call | solution.py:448
  8.9 1.5 %collective-permute-done.1.refs_12_ = bf16[128,128]{1,0:T(8,128)(2,1)S(1)} collective-permute-done((bf16[128,128]{1,0:T(8,128)(2,1)S(1)}, bf16[128,128]{1,0:T(8,128)(2,1)S(1)}, u32[]{:S(2)}, u32[]{:S(2)}) %collective-permute-start.1) | collective-permute-done | bytes 32800 | tf_op jit(solution)/shard_map/ppermute | solution.py:465
  10.4 0.3 %collective-permute-done.refs_3_ = bf16[128,128]{1,0:T(8,128)(2,1)S(1)} collective-permute-done((bf16[128,128]{1,0:T(8,128)(2,1)S(1)}, bf16[128,128]{1,0:T(8,128)(2,1)S(1)}, u32[]{:S(2)}, u32[]{:S(2)}) %collective-permute-start) | collective-permute-done | bytes 32800 | tf_op jit(solution)/shard_map/ppermute | solution.py:465
  10.6 0.3 %collective-permute-done.2.refs_14_ = bf16[784,128]{1,0:T(8,128)(2,1)S(1)} collective-permute-done((bf16[784,128]{1,0:T(8,128)(2,1)S(1)}, bf16[784,128]{1,0:T(8,128)(2,1)S(1)}, u32[]{:S(2)}, u32[]{:S(2)}) %collective-permute-start.2) | collective-permute-done | bytes 200736 | tf_op jit(solution)/shard_map/ppermute | solution.py:465
  10.9 1.6 %shard_map.188 = (bf16[2,128,128]{2,1,0:T(8,128)(2,1)S(1)}, bf16[512,128]{1,0:T(8,128)(2,1)S(1)}, bf16[512,256]{1,0:T(8,128)(2,1)S(1)}, bf16[128,256]{1,0:T(8,12...) custom-call(bf16[1,128,512]{2,1,0:T(8,128)(2,1)S(1)} %get-tuple-element.63.refs_0_, ...), custom_call_target="tpu_custom_call" | custom-call | tf_op jit(solution)/shard_map/pallas_call | solution.py:448
  12.5 1.9 %collective-permute-start.3 = (bf16[512,128]{1,0:T(8,128)(2,1)S(1)}, bf16[512,128]{1,0:T(8,128)(2,1)S(1)}, u32[]{:S(2)}, u32[]{:S(2)}) collective-permute-start(bf16[512,128]{1,0:T(8,128)(2,1)S(1)} %get-tuple-element.78), channel_id=1, source_target_pairs={{0,4},{4,0},{8,12},{12,8},{16,20},{20,16},{24,28},{28,24},{1,5},{5... | collective-permute-start | bytes 393224 | tf_op jit(solution)/shard_map/ppermute | solution.py:465
  14.3 1.2 %shard_map.189 = (f32[1,8,128]{2,1,0:T(8,128)}, f32[8,128]{1,0:T(8,128)S(1)}) custom-call(bf16[400,512]{1,0:T(8,128)(2,1)S(1)} %get-tuple-element.79.products, bf16[128,512]{1,0:T(8,128)(2,1)S(1)} %get-tuple-element.74.scaled.refs_1_, bf16[1024,128]{1,0:T(8,128)(2,1)S(1)} %get-tuple-element.71.refs_10_.halves, f32[1024,128]{1,0:T(8,128)S(1)} %get-tuple-element.80.back, ...), custom_call_target="tpu_custom_call" | custom-call | tf_op jit(solution)/shard_map/pallas_call | solution.py:448
  15.6 0.0 collective-permute-start.6
  15.6 1.5 %collective-permute-start.5 = (f32[8,128]{1,0:T(8,128)S(1)}, f32[8,128]{1,0:T(8,128)S(1)}, u32[]{:S(2)}, u32[]{:S(2)}) collective-permute-start(f32[8,128]{1,0:T(8,128)S(1)} %get-tuple-element.90), channel_id=1, source_target_pairs={{0,2},{1,3},{2,0},{3,1},{4,6},{5,7},{6,4},{7,5},{8,10},{9,11},{10,... | collective-permute-start | bytes 12296 | tf_op jit(solution)/shard_map/ppermute | solution.py:567
  17.1 0.3 %collective-permute-start.4 = (f32[8,128]{1,0:T(8,128)S(1)}, f32[8,128]{1,0:T(8,128)S(1)}, u32[]{:S(2)}, u32[]{:S(2)}) collective-permute-start(f32[8,128]{1,0:T(8,128)S(1)} %get-tuple-element.90), channel_id=1, source_target_pairs={{0,1},{1,0},{2,3},{3,2},{4,5},{5,4},{6,7},{7,6},{8,9},{9,8},{10,11... | collective-permute-start | bytes 12296 | tf_op jit(solution)/shard_map/ppermute | solution.py:567
  17.4 0.1 collective-permute-done.3.refs_2_
  17.5 2.9 %collective-permute-start.7 = (bf16[256,128]{1,0:T(8,128)(2,1)S(1)}, bf16[256,128]{1,0:T(8,128)(2,1)S(1)}, u32[]{:S(2)}, u32[]{:S(2)}) collective-permute-start(bf16[256,128]{1,0:T(8,128)(2,1)S(1)} %add_convert_fusion.mine), channel_id=1, source_target_pairs={{0,8},{4,12},{8,0},{12,4},{16,24},{20,28},{24,16},{28,20},{1,9},{5... | collective-permute-start | bytes 196616 | tf_op jit(solution)/shard_map/ppermute | solution.py:465
  20.4 0.0 collective-permute-done.6
  20.4 0.0 collective-permute-done.5
  20.4 0.0 collective-permute-done.4
  20.5 1.6 %collective-permute-start.8 = (bf16[144,128]{1,0:T(8,128)(2,1)S(1)}, bf16[144,128]{1,0:T(8,128)(2,1)S(1)}, u32[]{:S(2)}, u32[]{:S(2)}) collective-permute-start(bf16[144,128]{1,0:T(8,128)(2,1)S(1)} %pad_maximum_fusion), channel_id=1, source_target_pairs={{0,16},{4,20},{8,24},{12,28},{16,0},{20,4},{24,8},{28,12},{1,17},{... | collective-permute-start | bytes 110600 | tf_op jit(solution)/shard_map/ppermute | solution.py:465
  22.1 1.0 %shard_map.190 = (f32[1,128,512]{2,1,0:T(8,128)}, f32[1,128,512]{2,1,0:T(8,128)}) custom-call(bf16[128,1024]{1,0:T(8,128)(2,1)S(1)} %get-tuple-element.62.refs_0_, bf16[128,512]{1,0:T(8,128)(2,1)S(1)} %get-tuple-element.74.scaled.refs_1_, f32[128,512]{1,0:T(8,128)S(1)} %get-tuple-element.75.refs_2_, f32[128,512]{1,0:T(8,128)S(1)} %get-tuple-element.76.refs_3_, ...), custom_call_target="tpu_custom_call" | custom-call | tf_op jit(solution)/shard_map/pallas_call | solution.py:448
  23.1 0.1 collective-permute-done.7.other
  23.2 0.7 %shard_map.191 = (f32[1,128,128]{2,1,0:T(8,128)}, f32[1,128,128]{2,1,0:T(8,128)}) custom-call(bf16[256,128]{1,0:T(8,128)(2,1)S(1)} %add_convert_fusion.mine, bf16[256,128]{1,0:T(8,128)(2,1)S(1)} %collective-permute-done.7.other), custom_call_target="tpu_custom_call" | custom-call | tf_op jit(solution)/shard_map/pallas_call | solution.py:448
  23.8 0.7 %collective-permute-done.8.refs_0_ = bf16[144,128]{1,0:T(8,128)(2,1)S(1)} collective-permute-done((bf16[144,128]{1,0:T(8,128)(2,1)S(1)}, bf16[144,128]{1,0:T(8,128)(2,1)S(1)}, u32[]{:S(2)}, u32[]{:S(2)}) %collective-permute-start.8) | collective-permute-done | bytes 36896 | tf_op jit(solution)/shard_map/ppermute | solution.py:465
  24.5 0.6 %shard_map.192 = (f32[1,64,128]{2,1,0:T(8,128)}, f32[1,64,128]{2,1,0:T(8,128)}, f32[8]{0:T(128)}, f32[8]{0:T(128)}, f32[8]{0:T(128)}) custom-call(bf16[144,128]{1,0:T(8,128)(2,1)S(1)} %collective-permute-done.8.refs_0_, bf16[2,128,128]{2,1,0:T(8,128)(2,1)S(1)} %get-tuple-element.89.refs_1_, bf16[512,128]{1,0:T(8,128)(2,1)S(1)} %collective-permute-done.3.refs_2_, ...), custom_call_target="tpu_custom_call" | custom-call | tf_op jit(solution)/shard_map/pallas_call | solution.py:448
  (6 shorter events, 0.1 us)
Async XLA Ops:
  2.2 8.7 %collective-permute-start.2 = (bf16[784,128]{1,0:T(8,128)(2,1)S(1)}, bf16[784,128]{1,0:T(8,128)(2,1)S(1)}, u32[]{:S(2)}, u32[]{:S(2)}) collective-permute-start(bf16[784,128]{1,0:T(8,128)(2,1)S(1)} %bitcast.8), channel_id=1, source_target_pairs={{0,16},{4,20},{8,24},{12,28},{16,0},{20,4},{24,8},{28,12},{1,17},{... | collective-permute-start | bytes 602120 | tf_op jit(solution)/shard_map/ppermute | solution.py:465
  5.2 5.1 %collective-permute-start.1 = (bf16[128,128]{1,0:T(8,128)(2,1)S(1)}, bf16[128,128]{1,0:T(8,128)(2,1)S(1)}, u32[]{:S(2)}, u32[]{:S(2)}) collective-permute-start(bf16[128,128]{1,0:T(8,128)(2,1)S(1)} %get-tuple-element.64.refs_13_), channel_id=1, source_target_pairs={{0,20},{4,16},{8,28},{12,24},{16,4},{20,0},{24,12},{28,8},{1,21},{... | collective-permute-start | bytes 98312 | tf_op jit(solution)/shard_map/ppermute | solution.py:465
  6.7 3.9 %collective-permute-start = (bf16[128,128]{1,0:T(8,128)(2,1)S(1)}, bf16[128,128]{1,0:T(8,128)(2,1)S(1)}, u32[]{:S(2)}, u32[]{:S(2)}) collective-permute-start(bf16[128,128]{1,0:T(8,128)(2,1)S(1)} %get-tuple-element.64.refs_13_), channel_id=1, source_target_pairs={{0,4},{4,0},{8,12},{12,8},{16,20},{20,16},{24,28},{28,24},{1,5},{5... | collective-permute-start | bytes 98312 | tf_op jit(solution)/shard_map/ppermute | solution.py:465
  6.8 0.7 %copy-start = (f32[8]{0:T(128)S(1)}, f32[8]{0:T(128)}, u32[]{:S(2)}) copy-start(f32[8]{0:T(128)} %alog.1) | copy-start | bytes 100
  6.8 0.7 %copy-start.1 = (f32[8]{0:T(128)S(1)}, f32[8]{0:T(128)}, u32[]{:S(2)}) copy-start(f32[8]{0:T(128)} %bias.1) | copy-start | bytes 100
  6.8 0.7 %copy-start.2 = (f32[8]{0:T(128)S(1)}, f32[8]{0:T(128)}, u32[]{:S(2)}) copy-start(f32[8]{0:T(128)} %skip.1) | copy-start | bytes 100
  12.5 5.0 %collective-permute-start.3 = (bf16[512,128]{1,0:T(8,128)(2,1)S(1)}, bf16[512,128]{1,0:T(8,128)(2,1)S(1)}, u32[]{:S(2)}, u32[]{:S(2)}) collective-permute-start(bf16[512,128]{1,0:T(8,128)(2,1)S(1)} %get-tuple-element.78), channel_id=1, source_target_pairs={{0,4},{4,0},{8,12},{12,8},{16,20},{20,16},{24,28},{28,24},{1,5},{5... | collective-permute-start | bytes 393224 | tf_op jit(solution)/shard_map/ppermute | solution.py:465
  15.6 4.8 %collective-permute-start.6 = (f32[8,128]{1,0:T(8,128)S(1)}, f32[8,128]{1,0:T(8,128)S(1)}, u32[]{:S(2)}, u32[]{:S(2)}) collective-permute-start(f32[8,128]{1,0:T(8,128)S(1)} %get-tuple-element.90), channel_id=1, source_target_pairs={{0,3},{1,2},{2,1},{3,0},{4,7},{5,6},{6,5},{7,4},{8,11},{9,10},{10,... | collective-permute-start | bytes 12296 | tf_op jit(solution)/shard_map/ppermute | solution.py:567
  15.6 4.8 %collective-permute-start.5 = (f32[8,128]{1,0:T(8,128)S(1)}, f32[8,128]{1,0:T(8,128)S(1)}, u32[]{:S(2)}, u32[]{:S(2)}) collective-permute-start(f32[8,128]{1,0:T(8,128)S(1)} %get-tuple-element.90), channel_id=1, source_target_pairs={{0,2},{1,3},{2,0},{3,1},{4,6},{5,7},{6,4},{7,5},{8,10},{9,11},{10,... | collective-permute-start | bytes 12296 | tf_op jit(solution)/shard_map/ppermute | solution.py:567
  17.1 3.3 %collective-permute-start.4 = (f32[8,128]{1,0:T(8,128)S(1)}, f32[8,128]{1,0:T(8,128)S(1)}, u32[]{:S(2)}, u32[]{:S(2)}) collective-permute-start(f32[8,128]{1,0:T(8,128)S(1)} %get-tuple-element.90), channel_id=1, source_target_pairs={{0,1},{1,0},{2,3},{3,2},{4,5},{5,4},{6,7},{7,6},{8,9},{9,8},{10,11... | collective-permute-start | bytes 12296 | tf_op jit(solution)/shard_map/ppermute | solution.py:567
  17.5 5.6 %collective-permute-start.7 = (bf16[256,128]{1,0:T(8,128)(2,1)S(1)}, bf16[256,128]{1,0:T(8,128)(2,1)S(1)}, u32[]{:S(2)}, u32[]{:S(2)}) collective-permute-start(bf16[256,128]{1,0:T(8,128)(2,1)S(1)} %add_convert_fusion.mine), channel_id=1, source_target_pairs={{0,8},{4,12},{8,0},{12,4},{16,24},{20,28},{24,16},{28,20},{1,9},{5... | collective-permute-start | bytes 196616 | tf_op jit(solution)/shard_map/ppermute | solution.py:465
  20.5 4.0 %collective-permute-start.8 = (bf16[144,128]{1,0:T(8,128)(2,1)S(1)}, bf16[144,128]{1,0:T(8,128)(2,1)S(1)}, u32[]{:S(2)}, u32[]{:S(2)}) collective-permute-start(bf16[144,128]{1,0:T(8,128)(2,1)S(1)} %pad_maximum_fusion), channel_id=1, source_target_pairs={{0,16},{4,20},{8,24},{12,28},{16,0},{20,4},{24,8},{28,12},{1,17},{... | collective-permute-start | bytes 110600 | tf_op jit(solution)/shard_map/ppermute | solution.py:465

commit v8 on v7

--- a/solution.py
+++ b/solution.py
@@ -29,13 +29,13 @@
 PARTS = 3
 
 
-def flag_rows(*flags):
-    return jnp.concatenate([jnp.where(f, 1.0, 0.0).astype(BF16) for f in flags] * PARTS, axis=0)
-
-
-def dot_flags(arrays, rows):
-    split_up = [parts_of(a, PARTS) for a in arrays]
-    left = [parts[i] for i in range(PARTS) for parts in split_up]
+def flag_rows(*flags, count=PARTS):
+    return jnp.concatenate([jnp.where(f, 1.0, 0.0).astype(BF16) for f in flags] * count, axis=0)
+
+
+def dot_flags(arrays, rows, count=PARTS):
+    split_up = [parts_of(a, count) for a in arrays]
+    left = [parts[i] for i in range(count) for parts in split_up]
     return dot(jnp.concatenate(left, axis=1), rows)
 
 
@@ -45,14 +45,14 @@
     return lax.shift_right_logical(index, size.bit_length() - 1)
 
 
-def upto_rows(rows):
-    return flag_rows(iota((rows, rows), 0) <= iota((rows, rows), 1))
-
-
-def head_rows(heads, channels):
+def upto_rows(rows, count=PARTS):
+    return flag_rows(iota((rows, rows), 0) <= iota((rows, rows), 1), count=count)
+
+
+def head_rows(heads, channels, count=PARTS):
     shape = (heads, heads * channels)
     one = jnp.where(over(iota(shape, 1), channels) == iota(shape, 0), 1.0, 0.0)
-    return jnp.concatenate([one.astype(BF16)] * PARTS, axis=0)
+    return jnp.concatenate([one.astype(BF16)] * count, axis=0)
 
 
 def iota(shape, axis):
@@ -75,21 +75,23 @@
     return jnp.broadcast_to(jnp.sum(square, axis=1, keepdims=True), (heads, width))
 
 
-def rates(raw, bias, alog, upto):
+def rates(raw, bias, alog, upto, count=PARTS):
     shifted = raw + bias
-    step = jnp.maximum(shifted, 0.0) + jnp.log1p(jnp.exp(-jnp.abs(shifted)))
+    small = jnp.exp(-jnp.abs(shifted))
+    log_one = jnp.log1p(small) if count == PARTS else jnp.log(1.0 + small)
+    step = jnp.maximum(shifted, 0.0) + log_one
     rate = step * jnp.exp(alog)
-    return step, rate, dot_flags([rate], upto)
+    return step, rate, dot_flags([rate], upto, count)
 
 
 def spread(cols, m, width):
     return jnp.broadcast_to(cols[:, m : m + 1], (cols.shape[0], width))
 
 
-def widen(factors, channels, picked=None):
+def widen(factors, channels, picked=None, count=PARTS):
     if picked is None:
         picked = head_rows(factors.shape[0], channels)
-    return dot(jnp.concatenate(parts_of(factors, PARTS), axis=0), picked, TN)
+    return dot(jnp.concatenate(parts_of(factors, count), axis=0), picked, TN)
 
 
 def stack(wide, width):
@@ -144,11 +146,11 @@
     heads, rows = raw.shape[1:]
     wide, states = gate.shape[2], read.shape[2]
     half = key.shape[1]
-    upto, picked = upto_rows(rows), head_rows(heads, wide // heads)
+    upto, picked = upto_rows(rows, 2), head_rows(heads, wide // heads, 2)
     for place in (0, 6, 7):
         copies[place].wait()
-    step, _, cum = rates(raw[0], upright(bias, rows), upright(alog, rows), upto)
-    decay = widen(jnp.exp(-cum), wide // heads, picked)
+    step, _, cum = rates(raw[0], upright(bias, rows), upright(alog, rows), upto, 2)
+    decay = widen(jnp.exp(-cum), wide // heads, picked, 2)
     to_end = jnp.exp(cum - cum[:, rows - 1 :]) * step
     whole = jnp.broadcast_to(jnp.exp(-cum[:, rows - 1 :]), (heads, rows))
     tail = jnp.concatenate([to_end, whole], axis=0).astype(BF16)

time: 25.4 us -> 25.4 us (level)
  no operation moved by 1% of the time
where the time goes in v8:
time: 25.4 us; the launch traced here: 25.2 us
  starting transfers between devices  12.8 us (50%)
  Pallas kernels  8.03 us (32%)
  waiting for transfers between devices  2.88 us (11%)
  between operations  0.72 us (3%)
  local copies, waits for them, and re-layouts  0.68 us (3%)
    ppermute x6, starting transfers between devices, swap(): return lax.ppermute(array, ('seq', 'tp'), pairs)  10.9 us
    pallas_call x6, Pallas kernels, call(): pl.pallas_call(kernel, out_shape=outs, in_specs=[(specs or {}).get(i, VME...  6.51 us
    ppermute x6, waiting for transfers between devices, swap(): return lax.ppermute(array, ('seq', 'tp'), pairs)  2.87 us
    ppermute x3, starting transfers between devices, body(): lax.ppermute(params, 'dp', flip('dp', k * reach))  1.86 us
    pallas_call x1, Pallas kernels, body(): pl.pallas_call(share_kernel, out_shape=(shape((head_dim, rows), BF16), sh...  1.52 us
    unnamed x6, local copies, waits for them, and re-layouts  0.68 us
  transfers between devices with their start and end apart: 9, of which 6 were waited for; matrix products, arithmetic and copies ran while one was open for 0% of the time, Pallas kernels for 17%

profile of v8, /device:TPU:0, one launch (start us, length us, event | category | flops | bytes accessed | tf_op | source)
XLA Modules:
  0.0 25.2 jit_solution(9847586782677230684)
XLA Ops:
  0.6 1.5 %shard_map.186 = (bf16[128,128]{1,0:T(8,128)(2,1)S(1)}, bf16[1,784,128]{2,1,0:T(8,128)(2,1)S(1)}, f32[1,8,128]{2,1,0:T(8,128)S(1)}, bf16[1,128,512]{2,1,0:T(8,12...) custom-call(f32[1,8,128]{2,1,0:T(8,128)} %refs_0_.1, ...), custom_call_target="tpu_custom_call" | custom-call | tf_op jit(solution)/shard_map/pallas_call | solution.py:494
  2.2 3.0 %collective-permute-start.2 = (bf16[784,128]{1,0:T(8,128)(2,1)S(1)}, bf16[784,128]{1,0:T(8,128)(2,1)S(1)}, u32[]{:S(2)}, u32[]{:S(2)}) collective-permute-start(bf16[784,128]{1,0:T(8,128)(2,1)S(1)} %bitcast.8), channel_id=1, source_target_pairs={{0,16},{4,20},{8,24},{12,28},{16,0},{20,4},{24,8},{28,12},{1,17},{... | collective-permute-start | bytes 602120 | tf_op jit(solution)/shard_map/ppermute | solution.py:467
  5.2 1.5 %collective-permute-start.1 = (bf16[128,128]{1,0:T(8,128)(2,1)S(1)}, bf16[128,128]{1,0:T(8,128)(2,1)S(1)}, u32[]{:S(2)}, u32[]{:S(2)}) collective-permute-start(bf16[128,128]{1,0:T(8,128)(2,1)S(1)} %get-tuple-element.64.refs_13_), channel_id=1, source_target_pairs={{0,20},{4,16},{8,28},{12,24},{16,4},{20,0},{24,12},{28,8},{1,21},{... | collective-permute-start | bytes 98312 | tf_op jit(solution)/shard_map/ppermute | solution.py:467
  6.7 0.1 collective-permute-start
  6.8 0.0 copy-start
  6.8 0.0 copy-start.1
  6.8 0.0 copy-start.2
  6.8 0.6 %copy-done = f32[8]{0:T(128)S(1)} copy-done((f32[8]{0:T(128)S(1)}, f32[8]{0:T(128)}, u32[]{:S(2)}) %copy-start) | copy-done | bytes 56
  7.4 0.0 copy-done.1
  7.5 0.0 copy-done.2
  7.5 1.4 %shard_map.187 = (f32[128,512]{1,0:T(8,128)S(1)}, f32[128,512]{1,0:T(8,128)S(1)}, f32[128,512]{1,0:T(8,128)S(1)}, f32[128,512]{1,0:T(8,128)S(1)}, f32[128,512]{1...) custom-call(bf16[1,128,512]{2,1,0:T(8,128)(2,1)S(1)} %get-tuple-elem, ...), custom_call_target="tpu_custom_call" | custom-call | tf_op jit(solution)/shard_map/pallas_call | solution.py:450
  8.9 1.5 %collective-permute-done.1.refs_12_ = bf16[128,128]{1,0:T(8,128)(2,1)S(1)} collective-permute-done((bf16[128,128]{1,0:T(8,128)(2,1)S(1)}, bf16[128,128]{1,0:T(8,128)(2,1)S(1)}, u32[]{:S(2)}, u32[]{:S(2)}) %collective-permute-start.1) | collective-permute-done | bytes 32800 | tf_op jit(solution)/shard_map/ppermute | solution.py:467
  10.4 0.3 %collective-permute-done.refs_3_ = bf16[128,128]{1,0:T(8,128)(2,1)S(1)} collective-permute-done((bf16[128,128]{1,0:T(8,128)(2,1)S(1)}, bf16[128,128]{1,0:T(8,128)(2,1)S(1)}, u32[]{:S(2)}, u32[]{:S(2)}) %collective-permute-start) | collective-permute-done | bytes 32800 | tf_op jit(solution)/shard_map/ppermute | solution.py:467
  10.6 0.3 %collective-permute-done.2.refs_14_ = bf16[784,128]{1,0:T(8,128)(2,1)S(1)} collective-permute-done((bf16[784,128]{1,0:T(8,128)(2,1)S(1)}, bf16[784,128]{1,0:T(8,128)(2,1)S(1)}, u32[]{:S(2)}, u32[]{:S(2)}) %collective-permute-start.2) | collective-permute-done | bytes 200736 | tf_op jit(solution)/shard_map/ppermute | solution.py:467
  10.9 1.6 %shard_map.188 = (bf16[2,128,128]{2,1,0:T(8,128)(2,1)S(1)}, bf16[512,128]{1,0:T(8,128)(2,1)S(1)}, bf16[512,256]{1,0:T(8,128)(2,1)S(1)}, bf16[128,256]{1,0:T(8,12...) custom-call(bf16[1,128,512]{2,1,0:T(8,128)(2,1)S(1)} %get-tuple-element.63.refs_0_, ...), custom_call_target="tpu_custom_call" | custom-call | tf_op jit(solution)/shard_map/pallas_call | solution.py:450
  12.5 1.9 %collective-permute-start.3 = (bf16[512,128]{1,0:T(8,128)(2,1)S(1)}, bf16[512,128]{1,0:T(8,128)(2,1)S(1)}, u32[]{:S(2)}, u32[]{:S(2)}) collective-permute-start(bf16[512,128]{1,0:T(8,128)(2,1)S(1)} %get-tuple-element.78), channel_id=1, source_target_pairs={{0,4},{4,0},{8,12},{12,8},{16,20},{20,16},{24,28},{28,24},{1,5},{5... | collective-permute-start | bytes 393224 | tf_op jit(solution)/shard_map/ppermute | solution.py:467
  14.3 1.2 %shard_map.189 = (f32[1,8,128]{2,1,0:T(8,128)}, f32[8,128]{1,0:T(8,128)S(1)}) custom-call(bf16[400,512]{1,0:T(8,128)(2,1)S(1)} %get-tuple-element.79.products, bf16[128,512]{1,0:T(8,128)(2,1)S(1)} %get-tuple-element.74.scaled.refs_1_, bf16[1024,128]{1,0:T(8,128)(2,1)S(1)} %get-tuple-element.71.refs_10_.halves, f32[1024,128]{1,0:T(8,128)S(1)} %get-tuple-element.80.back, ...), custom_call_target="tpu_custom_call" | custom-call | tf_op jit(solution)/shard_map/pallas_call | solution.py:450
  15.6 0.0 collective-permute-start.6
  15.6 1.5 %collective-permute-start.5 = (f32[8,128]{1,0:T(8,128)S(1)}, f32[8,128]{1,0:T(8,128)S(1)}, u32[]{:S(2)}, u32[]{:S(2)}) collective-permute-start(f32[8,128]{1,0:T(8,128)S(1)} %get-tuple-element.90), channel_id=1, source_target_pairs={{0,2},{1,3},{2,0},{3,1},{4,6},{5,7},{6,4},{7,5},{8,10},{9,11},{10,... | collective-permute-start | bytes 12296 | tf_op jit(solution)/shard_map/ppermute | solution.py:569
  17.1 0.3 %collective-permute-start.4 = (f32[8,128]{1,0:T(8,128)S(1)}, f32[8,128]{1,0:T(8,128)S(1)}, u32[]{:S(2)}, u32[]{:S(2)}) collective-permute-start(f32[8,128]{1,0:T(8,128)S(1)} %get-tuple-element.90), channel_id=1, source_target_pairs={{0,1},{1,0},{2,3},{3,2},{4,5},{5,4},{6,7},{7,6},{8,9},{9,8},{10,11... | collective-permute-start | bytes 12296 | tf_op jit(solution)/shard_map/ppermute | solution.py:569
  17.4 0.1 collective-permute-done.3.refs_2_
  17.5 2.9 %collective-permute-start.7 = (bf16[256,128]{1,0:T(8,128)(2,1)S(1)}, bf16[256,128]{1,0:T(8,128)(2,1)S(1)}, u32[]{:S(2)}, u32[]{:S(2)}) collective-permute-start(bf16[256,128]{1,0:T(8,128)(2,1)S(1)} %add_convert_fusion.mine), channel_id=1, source_target_pairs={{0,8},{4,12},{8,0},{12,4},{16,24},{20,28},{24,16},{28,20},{1,9},{5... | collective-permute-start | bytes 196616 | tf_op jit(solution)/shard_map/ppermute | solution.py:467
  20.4 0.0 collective-permute-done.6
  20.4 0.0 collective-permute-done.5
  20.4 0.0 collective-permute-done.4
  20.5 1.6 %collective-permute-start.8 = (bf16[144,128]{1,0:T(8,128)(2,1)S(1)}, bf16[144,128]{1,0:T(8,128)(2,1)S(1)}, u32[]{:S(2)}, u32[]{:S(2)}) collective-permute-start(bf16[144,128]{1,0:T(8,128)(2,1)S(1)} %pad_maximum_fusion), channel_id=1, source_target_pairs={{0,16},{4,20},{8,24},{12,28},{16,0},{20,4},{24,8},{28,12},{1,17},{... | collective-permute-start | bytes 110600 | tf_op jit(solution)/shard_map/ppermute | solution.py:467
  22.1 1.0 %shard_map.190 = (f32[1,128,512]{2,1,0:T(8,128)}, f32[1,128,512]{2,1,0:T(8,128)}) custom-call(bf16[128,1024]{1,0:T(8,128)(2,1)S(1)} %get-tuple-element.62.refs_0_, bf16[128,512]{1,0:T(8,128)(2,1)S(1)} %get-tuple-element.74.scaled.refs_1_, f32[128,512]{1,0:T(8,128)S(1)} %get-tuple-element.75.refs_2_, f32[128,512]{1,0:T(8,128)S(1)} %get-tuple-element.76.refs_3_, ...), custom_call_target="tpu_custom_call" | custom-call | tf_op jit(solution)/shard_map/pallas_call | solution.py:450
  23.1 0.1 collective-permute-done.7.other
  23.2 0.7 %shard_map.191 = (f32[1,128,128]{2,1,0:T(8,128)}, f32[1,128,128]{2,1,0:T(8,128)}) custom-call(bf16[256,128]{1,0:T(8,128)(2,1)S(1)} %add_convert_fusion.mine, bf16[256,128]{1,0:T(8,128)(2,1)S(1)} %collective-permute-done.7.other), custom_call_target="tpu_custom_call" | custom-call | tf_op jit(solution)/shard_map/pallas_call | solution.py:450
  23.8 0.7 %collective-permute-done.8.refs_0_ = bf16[144,128]{1,0:T(8,128)(2,1)S(1)} collective-permute-done((bf16[144,128]{1,0:T(8,128)(2,1)S(1)}, bf16[144,128]{1,0:T(8,128)(2,1)S(1)}, u32[]{:S(2)}, u32[]{:S(2)}) %collective-permute-start.8) | collective-permute-done | bytes 36896 | tf_op jit(solution)/shard_map/ppermute | solution.py:467
  24.5 0.6 %shard_map.192 = (f32[1,64,128]{2,1,0:T(8,128)}, f32[1,64,128]{2,1,0:T(8,128)}, f32[8]{0:T(128)}, f32[8]{0:T(128)}, f32[8]{0:T(128)}) custom-call(bf16[144,128]{1,0:T(8,128)(2,1)S(1)} %collective-permute-done.8.refs_0_, bf16[2,128,128]{2,1,0:T(8,128)(2,1)S(1)} %get-tuple-element.89.refs_1_, bf16[512,128]{1,0:T(8,128)(2,1)S(1)} %collective-permute-done.3.refs_2_, ...), custom_call_target="tpu_custom_call" | custom-call | tf_op jit(solution)/shard_map/pallas_call | solution.py:450
  (6 shorter events, 0.1 us)
Async XLA Ops:
  2.2 8.7 %collective-permute-start.2 = (bf16[784,128]{1,0:T(8,128)(2,1)S(1)}, bf16[784,128]{1,0:T(8,128)(2,1)S(1)}, u32[]{:S(2)}, u32[]{:S(2)}) collective-permute-start(bf16[784,128]{1,0:T(8,128)(2,1)S(1)} %bitcast.8), channel_id=1, source_target_pairs={{0,16},{4,20},{8,24},{12,28},{16,0},{20,4},{24,8},{28,12},{1,17},{... | collective-permute-start | bytes 602120 | tf_op jit(solution)/shard_map/ppermute | solution.py:467
  5.2 5.2 %collective-permute-start.1 = (bf16[128,128]{1,0:T(8,128)(2,1)S(1)}, bf16[128,128]{1,0:T(8,128)(2,1)S(1)}, u32[]{:S(2)}, u32[]{:S(2)}) collective-permute-start(bf16[128,128]{1,0:T(8,128)(2,1)S(1)} %get-tuple-element.64.refs_13_), channel_id=1, source_target_pairs={{0,20},{4,16},{8,28},{12,24},{16,4},{20,0},{24,12},{28,8},{1,21},{... | collective-permute-start | bytes 98312 | tf_op jit(solution)/shard_map/ppermute | solution.py:467
  6.7 3.9 %collective-permute-start = (bf16[128,128]{1,0:T(8,128)(2,1)S(1)}, bf16[128,128]{1,0:T(8,128)(2,1)S(1)}, u32[]{:S(2)}, u32[]{:S(2)}) collective-permute-start(bf16[128,128]{1,0:T(8,128)(2,1)S(1)} %get-tuple-element.64.refs_13_), channel_id=1, source_target_pairs={{0,4},{4,0},{8,12},{12,8},{16,20},{20,16},{24,28},{28,24},{1,5},{5... | collective-permute-start | bytes 98312 | tf_op jit(solution)/shard_map/ppermute | solution.py:467
  6.8 0.7 %copy-start = (f32[8]{0:T(128)S(1)}, f32[8]{0:T(128)}, u32[]{:S(2)}) copy-start(f32[8]{0:T(128)} %alog.1) | copy-start | bytes 100
  6.8 0.7 %copy-start.1 = (f32[8]{0:T(128)S(1)}, f32[8]{0:T(128)}, u32[]{:S(2)}) copy-start(f32[8]{0:T(128)} %bias.1) | copy-start | bytes 100
  6.8 0.7 %copy-start.2 = (f32[8]{0:T(128)S(1)}, f32[8]{0:T(128)}, u32[]{:S(2)}) copy-start(f32[8]{0:T(128)} %skip.1) | copy-start | bytes 100
  12.5 5.0 %collective-permute-start.3 = (bf16[512,128]{1,0:T(8,128)(2,1)S(1)}, bf16[512,128]{1,0:T(8,128)(2,1)S(1)}, u32[]{:S(2)}, u32[]{:S(2)}) collective-permute-start(bf16[512,128]{1,0:T(8,128)(2,1)S(1)} %get-tuple-element.78), channel_id=1, source_target_pairs={{0,4},{4,0},{8,12},{12,8},{16,20},{20,16},{24,28},{28,24},{1,5},{5... | collective-permute-start | bytes 393224 | tf_op jit(solution)/shard_map/ppermute | solution.py:467
  15.6 4.8 %collective-permute-start.6 = (f32[8,128]{1,0:T(8,128)S(1)}, f32[8,128]{1,0:T(8,128)S(1)}, u32[]{:S(2)}, u32[]{:S(2)}) collective-permute-start(f32[8,128]{1,0:T(8,128)S(1)} %get-tuple-element.90), channel_id=1, source_target_pairs={{0,3},{1,2},{2,1},{3,0},{4,7},{5,6},{6,5},{7,4},{8,11},{9,10},{10,... | collective-permute-start | bytes 12296 | tf_op jit(solution)/shard_map/ppermute | solution.py:569
  15.6 4.8 %collective-permute-start.5 = (f32[8,128]{1,0:T(8,128)S(1)}, f32[8,128]{1,0:T(8,128)S(1)}, u32[]{:S(2)}, u32[]{:S(2)}) collective-permute-start(f32[8,128]{1,0:T(8,128)S(1)} %get-tuple-element.90), channel_id=1, source_target_pairs={{0,2},{1,3},{2,0},{3,1},{4,6},{5,7},{6,4},{7,5},{8,10},{9,11},{10,... | collective-permute-start | bytes 12296 | tf_op jit(solution)/shard_map/ppermute | solution.py:569
  17.1 3.3 %collective-permute-start.4 = (f32[8,128]{1,0:T(8,128)S(1)}, f32[8,128]{1,0:T(8,128)S(1)}, u32[]{:S(2)}, u32[]{:S(2)}) collective-permute-start(f32[8,128]{1,0:T(8,128)S(1)} %get-tuple-element.90), channel_id=1, source_target_pairs={{0,1},{1,0},{2,3},{3,2},{4,5},{5,4},{6,7},{7,6},{8,9},{9,8},{10,11... | collective-permute-start | bytes 12296 | tf_op jit(solution)/shard_map/ppermute | solution.py:569
  17.5 5.6 %collective-permute-start.7 = (bf16[256,128]{1,0:T(8,128)(2,1)S(1)}, bf16[256,128]{1,0:T(8,128)(2,1)S(1)}, u32[]{:S(2)}, u32[]{:S(2)}) collective-permute-start(bf16[256,128]{1,0:T(8,128)(2,1)S(1)} %add_convert_fusion.mine), channel_id=1, source_target_pairs={{0,8},{4,12},{8,0},{12,4},{16,24},{20,28},{24,16},{28,20},{1,9},{5... | collective-permute-start | bytes 196616 | tf_op jit(solution)/shard_map/ppermute | solution.py:467
  20.5 4.0 %collective-permute-start.8 = (bf16[144,128]{1,0:T(8,128)(2,1)S(1)}, bf16[144,128]{1,0:T(8,128)(2,1)S(1)}, u32[]{:S(2)}, u32[]{:S(2)}) collective-permute-start(bf16[144,128]{1,0:T(8,128)(2,1)S(1)} %pad_maximum_fusion), channel_id=1, source_target_pairs={{0,16},{4,20},{8,24},{12,28},{16,0},{20,4},{24,8},{28,12},{1,17},{... | collective-permute-start | bytes 110600 | tf_op jit(solution)/shard_map/ppermute | solution.py:467

commit v9 on v8

--- a/solution.py
+++ b/solution.py
@@ -77,9 +77,7 @@
 
 def rates(raw, bias, alog, upto, count=PARTS):
     shifted = raw + bias
-    small = jnp.exp(-jnp.abs(shifted))
-    log_one = jnp.log1p(small) if count == PARTS else jnp.log(1.0 + small)
-    step = jnp.maximum(shifted, 0.0) + log_one
+    step = jnp.maximum(shifted, 0.0) + jnp.log1p(jnp.exp(-jnp.abs(shifted)))
     rate = step * jnp.exp(alog)
     return step, rate, dot_flags([rate], upto, count)
 
@@ -140,7 +138,7 @@
         pltpu.make_async_copy(source, here, arrived.at[i])
         for i, (source, here) in enumerate(zip(sources, held))
     ]
-    for place in (0, 6, 7, 1, 2, 3, 4, 8, 9, 5):
+    for place in (1, 2, 0, 6, 7, 3, 4, 8, 9, 5):
         copies[place].start()
     here = lax.axis_index("seq")
     heads, rows = raw.shape[1:]

time: 25.4 us -> 25.5 us (level)
  no operation moved by 1% of the time
where the time goes in v9:
time: 25.5 us; the launch traced here: 25.3 us
  starting transfers between devices  12.8 us (50%)
  Pallas kernels  8.16 us (32%)
  waiting for transfers between devices  2.88 us (11%)
  between operations  0.72 us (3%)
  local copies, waits for them, and re-layouts  0.68 us (3%)
    ppermute x6, starting transfers between devices, swap(): return lax.ppermute(array, ('seq', 'tp'), pairs)  10.9 us
    pallas_call x6, Pallas kernels, call(): pl.pallas_call(kernel, out_shape=outs, in_specs=[(specs or {}).get(i, VME...  6.51 us
    ppermute x6, waiting for transfers between devices, swap(): return lax.ppermute(array, ('seq', 'tp'), pairs)  2.87 us
    ppermute x3, starting transfers between devices, body(): lax.ppermute(params, 'dp', flip('dp', k * reach))  1.86 us
    pallas_call x1, Pallas kernels, body(): pl.pallas_call(share_kernel, out_shape=(shape((head_dim, rows), BF16), sh...  1.64 us
    unnamed x6, local copies, waits for them, and re-layouts  0.68 us
  transfers between devices with their start and end apart: 9, of which 6 were waited for; matrix products, arithmetic and copies ran while one was open for 0% of the time, Pallas kernels for 17%

profile of v9, /device:TPU:0, one launch (start us, length us, event | category | flops | bytes accessed | tf_op | source)
XLA Modules:
  0.0 25.3 jit_solution(12768524775836149413)
XLA Ops:
  0.6 1.6 %shard_map.186 = (bf16[128,128]{1,0:T(8,128)(2,1)S(1)}, bf16[1,784,128]{2,1,0:T(8,128)(2,1)S(1)}, f32[1,8,128]{2,1,0:T(8,128)S(1)}, bf16[1,128,512]{2,1,0:T(8,12...) custom-call(f32[1,8,128]{2,1,0:T(8,128)} %refs_0_.1, ...), custom_call_target="tpu_custom_call" | custom-call | tf_op jit(solution)/shard_map/pallas_call | solution.py:492
  2.3 3.0 %collective-permute-start.2 = (bf16[784,128]{1,0:T(8,128)(2,1)S(1)}, bf16[784,128]{1,0:T(8,128)(2,1)S(1)}, u32[]{:S(2)}, u32[]{:S(2)}) collective-permute-start(bf16[784,128]{1,0:T(8,128)(2,1)S(1)} %bitcast.8), channel_id=1, source_target_pairs={{0,16},{4,20},{8,24},{12,28},{16,0},{20,4},{24,8},{28,12},{1,17},{... | collective-permute-start | bytes 602120 | tf_op jit(solution)/shard_map/ppermute | solution.py:465
  5.3 1.5 %collective-permute-start.1 = (bf16[128,128]{1,0:T(8,128)(2,1)S(1)}, bf16[128,128]{1,0:T(8,128)(2,1)S(1)}, u32[]{:S(2)}, u32[]{:S(2)}) collective-permute-start(bf16[128,128]{1,0:T(8,128)(2,1)S(1)} %get-tuple-element.64.refs_13_), channel_id=1, source_target_pairs={{0,20},{4,16},{8,28},{12,24},{16,4},{20,0},{24,12},{28,8},{1,21},{... | collective-permute-start | bytes 98312 | tf_op jit(solution)/shard_map/ppermute | solution.py:465
  6.9 0.1 collective-permute-start
  6.9 0.0 copy-start
  6.9 0.0 copy-start.1
  6.9 0.0 copy-start.2
  6.9 0.6 %copy-done = f32[8]{0:T(128)S(1)} copy-done((f32[8]{0:T(128)S(1)}, f32[8]{0:T(128)}, u32[]{:S(2)}) %copy-start) | copy-done | bytes 56
  7.6 0.0 copy-done.1
  7.6 0.0 copy-done.2
  7.6 1.4 %shard_map.187 = (f32[128,512]{1,0:T(8,128)S(1)}, f32[128,512]{1,0:T(8,128)S(1)}, f32[128,512]{1,0:T(8,128)S(1)}, f32[128,512]{1,0:T(8,128)S(1)}, f32[128,512]{1...) custom-call(bf16[1,128,512]{2,1,0:T(8,128)(2,1)S(1)} %get-tuple-elem, ...), custom_call_target="tpu_custom_call" | custom-call | tf_op jit(solution)/shard_map/pallas_call | solution.py:448
  9.0 1.5 %collective-permute-done.1.refs_12_ = bf16[128,128]{1,0:T(8,128)(2,1)S(1)} collective-permute-done((bf16[128,128]{1,0:T(8,128)(2,1)S(1)}, bf16[128,128]{1,0:T(8,128)(2,1)S(1)}, u32[]{:S(2)}, u32[]{:S(2)}) %collective-permute-start.1) | collective-permute-done | bytes 32800 | tf_op jit(solution)/shard_map/ppermute | solution.py:465
  10.5 0.3 %collective-permute-done.refs_3_ = bf16[128,128]{1,0:T(8,128)(2,1)S(1)} collective-permute-done((bf16[128,128]{1,0:T(8,128)(2,1)S(1)}, bf16[128,128]{1,0:T(8,128)(2,1)S(1)}, u32[]{:S(2)}, u32[]{:S(2)}) %collective-permute-start) | collective-permute-done | bytes 32800 | tf_op jit(solution)/shard_map/ppermute | solution.py:465
  10.8 0.3 %collective-permute-done.2.refs_14_ = bf16[784,128]{1,0:T(8,128)(2,1)S(1)} collective-permute-done((bf16[784,128]{1,0:T(8,128)(2,1)S(1)}, bf16[784,128]{1,0:T(8,128)(2,1)S(1)}, u32[]{:S(2)}, u32[]{:S(2)}) %collective-permute-start.2) | collective-permute-done | bytes 200736 | tf_op jit(solution)/shard_map/ppermute | solution.py:465
  11.0 1.6 %shard_map.188 = (bf16[2,128,128]{2,1,0:T(8,128)(2,1)S(1)}, bf16[512,128]{1,0:T(8,128)(2,1)S(1)}, bf16[512,256]{1,0:T(8,128)(2,1)S(1)}, bf16[128,256]{1,0:T(8,12...) custom-call(bf16[1,128,512]{2,1,0:T(8,128)(2,1)S(1)} %get-tuple-element.63.refs_0_, ...), custom_call_target="tpu_custom_call" | custom-call | tf_op jit(solution)/shard_map/pallas_call | solution.py:448
  12.6 1.9 %collective-permute-start.3 = (bf16[512,128]{1,0:T(8,128)(2,1)S(1)}, bf16[512,128]{1,0:T(8,128)(2,1)S(1)}, u32[]{:S(2)}, u32[]{:S(2)}) collective-permute-start(bf16[512,128]{1,0:T(8,128)(2,1)S(1)} %get-tuple-element.78), channel_id=1, source_target_pairs={{0,4},{4,0},{8,12},{12,8},{16,20},{20,16},{24,28},{28,24},{1,5},{5... | collective-permute-start | bytes 393224 | tf_op jit(solution)/shard_map/ppermute | solution.py:465
  14.5 1.2 %shard_map.189 = (f32[1,8,128]{2,1,0:T(8,128)}, f32[8,128]{1,0:T(8,128)S(1)}) custom-call(bf16[400,512]{1,0:T(8,128)(2,1)S(1)} %get-tuple-element.79.products, bf16[128,512]{1,0:T(8,128)(2,1)S(1)} %get-tuple-element.74.scaled.refs_1_, bf16[1024,128]{1,0:T(8,128)(2,1)S(1)} %get-tuple-element.71.refs_10_.halves, f32[1024,128]{1,0:T(8,128)S(1)} %get-tuple-element.80.back, ...), custom_call_target="tpu_custom_call" | custom-call | tf_op jit(solution)/shard_map/pallas_call | solution.py:448
  15.7 0.0 collective-permute-start.6
  15.7 1.5 %collective-permute-start.5 = (f32[8,128]{1,0:T(8,128)S(1)}, f32[8,128]{1,0:T(8,128)S(1)}, u32[]{:S(2)}, u32[]{:S(2)}) collective-permute-start(f32[8,128]{1,0:T(8,128)S(1)} %get-tuple-element.90), channel_id=1, source_target_pairs={{0,2},{1,3},{2,0},{3,1},{4,6},{5,7},{6,4},{7,5},{8,10},{9,11},{10,... | collective-permute-start | bytes 12296 | tf_op jit(solution)/shard_map/ppermute | solution.py:567
  17.2 0.3 %collective-permute-start.4 = (f32[8,128]{1,0:T(8,128)S(1)}, f32[8,128]{1,0:T(8,128)S(1)}, u32[]{:S(2)}, u32[]{:S(2)}) collective-permute-start(f32[8,128]{1,0:T(8,128)S(1)} %get-tuple-element.90), channel_id=1, source_target_pairs={{0,1},{1,0},{2,3},{3,2},{4,5},{5,4},{6,7},{7,6},{8,9},{9,8},{10,11... | collective-permute-start | bytes 12296 | tf_op jit(solution)/shard_map/ppermute | solution.py:567
  17.6 0.1 collective-permute-done.3.refs_2_
  17.7 2.9 %collective-permute-start.7 = (bf16[256,128]{1,0:T(8,128)(2,1)S(1)}, bf16[256,128]{1,0:T(8,128)(2,1)S(1)}, u32[]{:S(2)}, u32[]{:S(2)}) collective-permute-start(bf16[256,128]{1,0:T(8,128)(2,1)S(1)} %add_convert_fusion.mine), channel_id=1, source_target_pairs={{0,8},{4,12},{8,0},{12,4},{16,24},{20,28},{24,16},{28,20},{1,9},{5... | collective-permute-start | bytes 196616 | tf_op jit(solution)/shard_map/ppermute | solution.py:465
  20.5 0.0 collective-permute-done.6
  20.5 0.0 collective-permute-done.5
  20.6 0.0 collective-permute-done.4
  20.6 1.6 %collective-permute-start.8 = (bf16[144,128]{1,0:T(8,128)(2,1)S(1)}, bf16[144,128]{1,0:T(8,128)(2,1)S(1)}, u32[]{:S(2)}, u32[]{:S(2)}) collective-permute-start(bf16[144,128]{1,0:T(8,128)(2,1)S(1)} %pad_maximum_fusion), channel_id=1, source_target_pairs={{0,16},{4,20},{8,24},{12,28},{16,0},{20,4},{24,8},{28,12},{1,17},{... | collective-permute-start | bytes 110600 | tf_op jit(solution)/shard_map/ppermute | solution.py:465
  22.2 1.0 %shard_map.190 = (f32[1,128,512]{2,1,0:T(8,128)}, f32[1,128,512]{2,1,0:T(8,128)}) custom-call(bf16[128,1024]{1,0:T(8,128)(2,1)S(1)} %get-tuple-element.62.refs_0_, bf16[128,512]{1,0:T(8,128)(2,1)S(1)} %get-tuple-element.74.scaled.refs_1_, f32[128,512]{1,0:T(8,128)S(1)} %get-tuple-element.75.refs_2_, f32[128,512]{1,0:T(8,128)S(1)} %get-tuple-element.76.refs_3_, ...), custom_call_target="tpu_custom_call" | custom-call | tf_op jit(solution)/shard_map/pallas_call | solution.py:448
  23.2 0.1 collective-permute-done.7.other
  23.3 0.7 %shard_map.191 = (f32[1,128,128]{2,1,0:T(8,128)}, f32[1,128,128]{2,1,0:T(8,128)}) custom-call(bf16[256,128]{1,0:T(8,128)(2,1)S(1)} %add_convert_fusion.mine, bf16[256,128]{1,0:T(8,128)(2,1)S(1)} %collective-permute-done.7.other), custom_call_target="tpu_custom_call" | custom-call | tf_op jit(solution)/shard_map/pallas_call | solution.py:448
  24.0 0.7 %collective-permute-done.8.refs_0_ = bf16[144,128]{1,0:T(8,128)(2,1)S(1)} collective-permute-done((bf16[144,128]{1,0:T(8,128)(2,1)S(1)}, bf16[144,128]{1,0:T(8,128)(2,1)S(1)}, u32[]{:S(2)}, u32[]{:S(2)}) %collective-permute-start.8) | collective-permute-done | bytes 36896 | tf_op jit(solution)/shard_map/ppermute | solution.py:465
  24.6 0.6 %shard_map.192 = (f32[1,64,128]{2,1,0:T(8,128)}, f32[1,64,128]{2,1,0:T(8,128)}, f32[8]{0:T(128)}, f32[8]{0:T(128)}, f32[8]{0:T(128)}) custom-call(bf16[144,128]{1,0:T(8,128)(2,1)S(1)} %collective-permute-done.8.refs_0_, bf16[2,128,128]{2,1,0:T(8,128)(2,1)S(1)} %get-tuple-element.89.refs_1_, bf16[512,128]{1,0:T(8,128)(2,1)S(1)} %collective-permute-done.3.refs_2_, ...), custom_call_target="tpu_custom_call" | custom-call | tf_op jit(solution)/shard_map/pallas_call | solution.py:448
  (6 shorter events, 0.1 us)
Async XLA Ops:
  2.3 8.7 %collective-permute-start.2 = (bf16[784,128]{1,0:T(8,128)(2,1)S(1)}, bf16[784,128]{1,0:T(8,128)(2,1)S(1)}, u32[]{:S(2)}, u32[]{:S(2)}) collective-permute-start(bf16[784,128]{1,0:T(8,128)(2,1)S(1)} %bitcast.8), channel_id=1, source_target_pairs={{0,16},{4,20},{8,24},{12,28},{16,0},{20,4},{24,8},{28,12},{1,17},{... | collective-permute-start | bytes 602120 | tf_op jit(solution)/shard_map/ppermute | solution.py:465
  5.3 5.2 %collective-permute-start.1 = (bf16[128,128]{1,0:T(8,128)(2,1)S(1)}, bf16[128,128]{1,0:T(8,128)(2,1)S(1)}, u32[]{:S(2)}, u32[]{:S(2)}) collective-permute-start(bf16[128,128]{1,0:T(8,128)(2,1)S(1)} %get-tuple-element.64.refs_13_), channel_id=1, source_target_pairs={{0,20},{4,16},{8,28},{12,24},{16,4},{20,0},{24,12},{28,8},{1,21},{... | collective-permute-start | bytes 98312 | tf_op jit(solution)/shard_map/ppermute | solution.py:465
  6.9 3.9 %collective-permute-start = (bf16[128,128]{1,0:T(8,128)(2,1)S(1)}, bf16[128,128]{1,0:T(8,128)(2,1)S(1)}, u32[]{:S(2)}, u32[]{:S(2)}) collective-permute-start(bf16[128,128]{1,0:T(8,128)(2,1)S(1)} %get-tuple-element.64.refs_13_), channel_id=1, source_target_pairs={{0,4},{4,0},{8,12},{12,8},{16,20},{20,16},{24,28},{28,24},{1,5},{5... | collective-permute-start | bytes 98312 | tf_op jit(solution)/shard_map/ppermute | solution.py:465
  6.9 0.7 %copy-start = (f32[8]{0:T(128)S(1)}, f32[8]{0:T(128)}, u32[]{:S(2)}) copy-start(f32[8]{0:T(128)} %alog.1) | copy-start | bytes 100
  6.9 0.7 %copy-start.1 = (f32[8]{0:T(128)S(1)}, f32[8]{0:T(128)}, u32[]{:S(2)}) copy-start(f32[8]{0:T(128)} %bias.1) | copy-start | bytes 100
  6.9 0.7 %copy-start.2 = (f32[8]{0:T(128)S(1)}, f32[8]{0:T(128)}, u32[]{:S(2)}) copy-start(f32[8]{0:T(128)} %skip.1) | copy-start | bytes 100
  12.6 5.0 %collective-permute-start.3 = (bf16[512,128]{1,0:T(8,128)(2,1)S(1)}, bf16[512,128]{1,0:T(8,128)(2,1)S(1)}, u32[]{:S(2)}, u32[]{:S(2)}) collective-permute-start(bf16[512,128]{1,0:T(8,128)(2,1)S(1)} %get-tuple-element.78), channel_id=1, source_target_pairs={{0,4},{4,0},{8,12},{12,8},{16,20},{20,16},{24,28},{28,24},{1,5},{5... | collective-permute-start | bytes 393224 | tf_op jit(solution)/shard_map/ppermute | solution.py:465
  15.7 4.8 %collective-permute-start.6 = (f32[8,128]{1,0:T(8,128)S(1)}, f32[8,128]{1,0:T(8,128)S(1)}, u32[]{:S(2)}, u32[]{:S(2)}) collective-permute-start(f32[8,128]{1,0:T(8,128)S(1)} %get-tuple-element.90), channel_id=1, source_target_pairs={{0,3},{1,2},{2,1},{3,0},{4,7},{5,6},{6,5},{7,4},{8,11},{9,10},{10,... | collective-permute-start | bytes 12296 | tf_op jit(solution)/shard_map/ppermute | solution.py:567
  15.7 4.8 %collective-permute-start.5 = (f32[8,128]{1,0:T(8,128)S(1)}, f32[8,128]{1,0:T(8,128)S(1)}, u32[]{:S(2)}, u32[]{:S(2)}) collective-permute-start(f32[8,128]{1,0:T(8,128)S(1)} %get-tuple-element.90), channel_id=1, source_target_pairs={{0,2},{1,3},{2,0},{3,1},{4,6},{5,7},{6,4},{7,5},{8,10},{9,11},{10,... | collective-permute-start | bytes 12296 | tf_op jit(solution)/shard_map/ppermute | solution.py:567
  17.2 3.3 %collective-permute-start.4 = (f32[8,128]{1,0:T(8,128)S(1)}, f32[8,128]{1,0:T(8,128)S(1)}, u32[]{:S(2)}, u32[]{:S(2)}) collective-permute-start(f32[8,128]{1,0:T(8,128)S(1)} %get-tuple-element.90), channel_id=1, source_target_pairs={{0,1},{1,0},{2,3},{3,2},{4,5},{5,4},{6,7},{7,6},{8,9},{9,8},{10,11... | collective-permute-start | bytes 12296 | tf_op jit(solution)/shard_map/ppermute | solution.py:567
  17.7 5.6 %collective-permute-start.7 = (bf16[256,128]{1,0:T(8,128)(2,1)S(1)}, bf16[256,128]{1,0:T(8,128)(2,1)S(1)}, u32[]{:S(2)}, u32[]{:S(2)}) collective-permute-start(bf16[256,128]{1,0:T(8,128)(2,1)S(1)} %add_convert_fusion.mine), channel_id=1, source_target_pairs={{0,8},{4,12},{8,0},{12,4},{16,24},{20,28},{24,16},{28,20},{1,9},{5... | collective-permute-start | bytes 196616 | tf_op jit(solution)/shard_map/ppermute | solution.py:465
  20.6 4.0 %collective-permute-start.8 = (bf16[144,128]{1,0:T(8,128)(2,1)S(1)}, bf16[144,128]{1,0:T(8,128)(2,1)S(1)}, u32[]{:S(2)}, u32[]{:S(2)}) collective-permute-start(bf16[144,128]{1,0:T(8,128)(2,1)S(1)} %pad_maximum_fusion), channel_id=1, source_target_pairs={{0,16},{4,20},{8,24},{12,28},{16,0},{20,4},{24,8},{28,12},{1,17},{... | collective-permute-start | bytes 110600 | tf_op jit(solution)/shard_map/ppermute | solution.py:465
